TPU v7x, 128 devices: a whole 4x4x4 slice. The times are simulated.
128 devices in a mesh: seq: 32 (over z, y_lo, x), tp: 4 (over y_hi, core).
Axes of the slice: x: 4, y: 4 (y_hi: 2, y_lo: 2; y = y_hi * 2 + y_lo), z: 4, core: 2. Of those that a mesh axis runs over, the one named last changes fastest.
Arguments:
- hidden: bfloat16 [8192, 4096], P('seq', 'tp'), may hold values from -6 to 6
- ctx_weight: bfloat16 [4096, 1024], P('tp'), may hold values from -0.09375 to 0.09375
- codes: int32 [8192, 8], P(('seq', 'tp')), may hold values from 0 to 2047, as said below
- table: bfloat16 [2048, 1024], replicated, may hold values from -6 to 6
- qkv_weight: bfloat16 [1024, 3072], replicated, may hold values from -0.1875 to 0.1875
- out_weight: bfloat16 [1024, 1024], replicated, may hold values from -0.1875 to 0.1875
- cotangent: bfloat16 [8192, 8, 1024], P(('seq', 'tp')), may hold values from -6 to 6
Outputs:
- d_hidden: bfloat16 [8192, 4096], P('seq', 'tp')
- grad_ctx: float32 [4096, 1024], P('tp')
- grad_table: float32 [2048, 1024], P(('seq', 'tp'))
- grad_qkv: float32 [1024, 3072], P(('seq', 'tp'))
- grad_out: float32 [1024, 1024], P(('seq', 'tp'))
Inputs may be any that keep to these rules, and one draw needn't show every extreme that they name: `codes`: split the ids into groups of 16 consecutive values starting at multiples of 16. Among the ids of one device (its 64 frames in order, 8 ids each), no group occurs more than 8 times, and one group occurs exactly 8 times among the ids of every device.
All inputs are finite; a program needn't handle non-finite values.
Results may differ from a plain program's by a relative error of at most 0.04.
Values may be sent and summed in bfloat16 or wider, within the bound.
No kernel may reach another device: no remote copies, remote signals or barrier semaphores. Data moves between devices by JAX's collectives and lax.ppermute only.
A program may use at most 128 MiB of HBM per device.

v0:
```python
import jax
import jax.numpy as jnp
from jax import lax
from jax.sharding import PartitionSpec as P

HEADS = 16


def embed(codes, table):
    vocab = table.shape[0]
    onehot = (codes.reshape(-1)[:, None] == jnp.arange(vocab, dtype=jnp.int32)[None, :]).astype(
        jnp.bfloat16
    )
    return (onehot, jnp.dot(onehot, table, preferred_element_type=jnp.float32))


def depth_rest(context, embedded, qkv_weight, out_weight):
    frames = context.shape[0]
    width = context.shape[1]
    books = embedded.shape[0] // frames
    size = width // HEADS
    stream = (
        embedded.reshape(frames, books, width) + context.astype(jnp.float32)[:, None, :]
    ).astype(jnp.bfloat16)
    flat = stream.reshape(frames * books, width)
    projected = jnp.dot(
        flat, qkv_weight.astype(jnp.bfloat16), preferred_element_type=jnp.float32
    ).astype(jnp.bfloat16)
    projected = projected.reshape(frames, books, 3, HEADS, size).astype(jnp.float32)
    query, keys, values = (projected[:, :, 0], projected[:, :, 1], projected[:, :, 2])
    scores = jnp.einsum("fqhd,fkhd->fhqk", query, keys) / jnp.sqrt(jnp.float32(size))
    causal = jnp.arange(books)[:, None] >= jnp.arange(books)[None, :]
    weights = jnp.where(causal[None, None], jnp.exp(scores), jnp.float32(0.0))
    probs = (weights / jnp.sum(weights, axis=-1, keepdims=True)).astype(jnp.bfloat16)
    mixed = jnp.einsum("fhqk,fkhd->fqhd", probs.astype(jnp.float32), values).astype(jnp.bfloat16)
    result = jnp.dot(
        mixed.reshape(frames * books, width),
        out_weight.astype(jnp.bfloat16),
        preferred_element_type=jnp.float32,
    )
    return stream.astype(jnp.float32) + result.reshape(frames, books, width)


def dense_table(onehot, d_embedded):
    return lax.dot_general(
        onehot.astype(jnp.float32),
        d_embedded,
        (((0,), (0,)), ((), ())),
        precision=lax.Precision.HIGHEST,
        preferred_element_type=jnp.float32,
    )


def on_device(hidden, ctx_weight, codes, table, qkv_weight, out_weight, cotangent):
    partial_ctx = jnp.dot(hidden, ctx_weight, preferred_element_type=jnp.float32)
    summed = lax.psum_scatter(
        partial_ctx.astype(jnp.bfloat16), "tp", scatter_dimension=0, tiled=True
    )
    onehot, embedded = embed(codes, table)
    unused, pull = jax.vjp(
        depth_rest, summed, embedded, qkv_weight.astype(jnp.float32), out_weight.astype(jnp.float32)
    )
    d_context, d_embedded, d_qkv, d_out = pull(cotangent.astype(jnp.float32))
    d_table = dense_table(onehot, d_embedded)
    grad_table, grad_qkv, grad_out = (
        lax.psum_scatter(d_table, ("seq", "tp"), scatter_dimension=0, tiled=True),
        lax.psum_scatter(d_qkv, ("seq", "tp"), scatter_dimension=0, tiled=True),
        lax.psum_scatter(d_out, ("seq", "tp"), scatter_dimension=0, tiled=True),
    )
    d_gathered = lax.all_gather(d_context, "tp", axis=0, tiled=True)
    d_hidden = lax.dot_general(
        d_gathered, ctx_weight, (((1,), (1,)), ((), ())), preferred_element_type=jnp.float32
    ).astype(jnp.bfloat16)
    ctx_part = lax.dot_general(
        hidden, d_gathered, (((0,), (0,)), ((), ())), preferred_element_type=jnp.float32
    )
    grad_ctx = lax.psum(ctx_part.astype(jnp.bfloat16), "seq").astype(jnp.float32)
    return (d_hidden, grad_ctx, grad_table, grad_qkv, grad_out)


def solution(mesh):
    in_specs = (
        P("seq", "tp"),
        P("tp", None),
        P(("seq", "tp"), None),
        P(),
        P(),
        P(),
        P(("seq", "tp"), None, None),
    )
    out_specs = (
        P("seq", "tp"),
        P("tp", None),
        P(("seq", "tp"), None),
        P(("seq", "tp"), None),
        P(("seq", "tp"), None),
    )
    return jax.shard_map(
        on_device, mesh=mesh, in_specs=in_specs, out_specs=out_specs, check_vma=False
    )
```

profile of v0, /device:TPU:1, one launch (start us, length us, event | category | flops | bytes accessed | tf_op | source)
XLA Modules:
  0.0 2389.4 jit_solution(4323155703431974841)
XLA Ops:
  7.2 0.0 copy-start
  7.2 0.0 reduce-scatter.5.cloned.1.call-start
  7.2 3.4 convolution_convert_fusion.4
  10.6 0.0 reduce-scatter.5.cloned.1.call-update
  10.6 0.0 all-reduce.5.cloned.1.call-start
  10.7 0.8 copy.20
  11.5 0.1 eq.15
  11.6 0.0 copy-done
  11.6 2.5 convolution_convert_fusion.1
  14.1 1.3 reshape.63
  15.4 27.6 %reduce-scatter.5.cloned.1.call-done = bf16[64,1024]{1,0:T(8,128)(2,1)} async-done(((bf16[256,1024]{1,0:T(8,128)(2,1)}), bf16[64,1024]{1,0:T(8,128)(2,1)}) %reduce-scatter.5.cloned.1.call-update) | async-done | bytes 131088 | tf_op jit(solution)/shard_map/reduce_scatter | solution.py:56
  43.0 1.1 convert_element_type.77
  44.1 0.0 slice-start.1
  44.1 4.8 fusion.10
  48.9 0.0 copy-start.10
  48.9 1.1 copy-done.10
  50.0 0.0 slice-done
  50.0 0.0 slice-done.1
  50.0 4.8 convolution_convert_fusion
  54.8 8.5 reshape.64
  63.3 4.3 fusion.29
  67.6 0.0 copy-start.4
  67.6 2.2 fusion.9
  69.8 0.0 copy-start.6
  69.8 0.0 copy-start.9
  69.8 0.1 multiply_divide_fusion
  69.9 0.0 copy-done.4
  69.9 2.8 fusion.5
  72.7 1.9 convolution_bitcast_fusion
  74.7 3.4 convolution_bitcast_fusion.1
  78.0 0.0 copy-done.6
  78.0 0.0 copy-done.9
  78.0 3.4 convolution_bitcast_fusion.2
  81.4 7.6 add_convert_fusion
  89.0 7.3 copy.25
  96.3 8.8 reshape.65
  105.1 0.0 copy-done.5
  105.1 8.6 fusion.30
  113.8 0.0 copy-start.7
  113.8 8.9 all_gather.3
  122.7 0.0 copy-done.8
  122.7 2.1 convert_bitcast_fusion.1
  124.8 0.0 all-reduce.5.cloned.1.call-update
  124.8 0.0 reduce-scatter.11.cloned.1.call-start
  124.9 3.8 convert_bitcast_fusion
  128.7 0.6 copy.27
  129.3 1.5 reshape.68
  130.8 4.6 convert_convert_fusion.1
  135.4 0.0 reduce-scatter.11.cloned.1.call-update
  135.4 0.3 reduce-scatter.7.cloned.1.call-start
  135.7 0.0 copy-done.12
  135.7 5.7 fusion.6
  141.3 0.0 reduce-scatter.7.cloned.1.call-update
  141.3 0.0 reduce-scatter.9.cloned.1.call-start
  141.4 1.2 copy-done.11
  142.6 8.3 convert_convert_fusion
  150.8 0.0 reduce-scatter.9.cloned.1.call-update
  150.8 1.0 copy-done.3
  151.9 3.3 convolution_convert_fusion.3
  155.1 258.9 %all-reduce.5.cloned.1.call-done = bf16[1024,1024]{0,1:T(8,128)(2,1)} async-done(((bf16[1024,1024]{0,1:T(8,128)(2,1)}), bf16[1024,1024]{0,1:T(8,128)(2,1)}) %all-reduce.5.cloned.1.call-update) | async-done | bytes 2097168 | tf_op jit(solution)/shard_map/psum | solution.py:77
  414.1 4.1 copy.28
  418.2 658.8 %reduce-scatter.11.cloned.1.call-done = f32[8,1024]{1,0:T(8,128)} async-done(((f32[1024,1024]{1,0:T(8,128)}), f32[8,1024]{1,0:T(8,128)}) %reduce-scatter.11.cloned.1.call-update) | async-done | bytes 32784 | tf_op jit(solution)/shard_map/reduce_scatter | solution.py:68
  1077.0 649.2 %reduce-scatter.7.cloned.1.call-done = f32[16,1024]{1,0:T(8,128)} async-done(((f32[2048,1024]{1,0:T(8,128)}), f32[16,1024]{1,0:T(8,128)}) %reduce-scatter.7.cloned.1.call-update) | async-done | bytes 65552 | tf_op jit(solution)/shard_map/reduce_scatter | solution.py:66
  1726.2 656.7 %reduce-scatter.9.cloned.1.call-done = f32[8,3072]{1,0:T(8,128)} async-done(((f32[1024,3072]{1,0:T(8,128)}), f32[8,3072]{1,0:T(8,128)}) %reduce-scatter.9.cloned.1.call-update) | async-done | bytes 98320 | tf_op jit(solution)/shard_map/reduce_scatter | solution.py:67
  (14 shorter events, 0.1 us)
Async XLA Ops:
  7.2 4.4 copy-start
  7.2 35.8 %reduce-scatter.5.cloned.1.call-start = ((), (), s32[]{:S(2)}) async-start(), calls=%async_computation.4 | async-start | bytes 655360 | tf_op jit(solution)/shard_map/reduce_scatter | solution.py:56
  10.6 403.4 %all-reduce.5.cloned.1.call-start = ((), (), s32[]{:S(2)}) async-start(), calls=%async_computation.5 | async-start | bytes 4194304 | tf_op jit(solution)/shard_map/psum | solution.py:77
  43.0 7.0 slice-start
  44.1 5.9 slice-start.1
  48.9 1.1 copy-start.10
  67.6 2.3 copy-start.4
  69.8 8.2 copy-start.6
  69.8 8.2 copy-start.9
  96.3 8.8 copy-start.5
  105.1 17.6 copy-start.8
  113.8 11.1 copy-start.7
  122.7 2.1 copy-start.2
  124.8 952.2 %reduce-scatter.11.cloned.1.call-start = ((), (), s32[]{:S(2)}) async-start(), calls=%async_computation.8 | async-start | bytes 4227072 | tf_op jit(solution)/shard_map/reduce_scatter | solution.py:68
  130.8 4.9 copy-start.12
  135.4 1590.8 %reduce-scatter.7.cloned.1.call-start = ((), (), s32[]{:S(2)}) async-start(), calls=%async_computation.6 | async-start | bytes 8454144 | tf_op jit(solution)/shard_map/reduce_scatter | solution.py:66
  141.3 1.2 copy-start.11
  141.3 2241.5 %reduce-scatter.9.cloned.1.call-start = ((), (), s32[]{:S(2)}) async-start(), calls=%async_computation.7 | async-start | bytes 12681216 | tf_op jit(solution)/shard_map/reduce_scatter | solution.py:67
  150.8 1.0 copy-start.3
  151.9 2231.0 %copy-start.1 = (bf16[1024,1024]{1,0:T(8,128)(2,1)S(1)}, bf16[1024,1024]{1,0:T(8,128)(2,1)}, u32[]{:S(2)}) copy-start(bf16[1024,1024]{1,0:T(8,128)(2,1)} %param.12) | copy-start | bytes 6291460
Sparse Core Ops, SparseCore 0:
  11.2 31.7 reduce-scatter.4
  124.9 289.0 all-reduce.4
  417.0 659.9 reduce-scatter.10
  1079.9 646.2 reduce-scatter.6
  1729.0 653.8 reduce-scatter.8
where the time goes:
time: 2400 us; the launch traced here: 2390 us
  waiting for transfers between devices  2250 us (94%)
  matrix products  65.4 us (3%)
  local copies, waits for them, and re-layouts  40.7 us (2%)
    reduce_scatter x1, waiting for transfers between devices, on_device(): lax.psum_scatter(d_out, ('seq', 'tp'), scatter_dimension=0, tiled=True)  659 us
    reduce_scatter x1, waiting for transfers between devices, on_device(): lax.psum_scatter(d_qkv, ('seq', 'tp'), scatter_dimension=0, tiled=True)  657 us
    reduce_scatter x1, waiting for transfers between devices, on_device(): lax.psum_scatter(d_table, ('seq', 'tp'), scatter_dimension=0, tiled=True)  649 us
    psum x1, waiting for transfers between devices, on_device(): lax.psum(ctx_part.astype(jnp.bfloat16), 'seq').astype(jnp.float32)  259 us
  transfers between devices with their start and end apart: 5, of which 5 were waited for; matrix products, arithmetic and copies ran while one was open for 2% of the time, Pallas kernels for 0%

commit v1 on v0

v1 whole, which is shorter than its diff:
```python
import functools

import jax
import jax.numpy as jnp
from jax import lax
from jax.experimental import pallas as pl
from jax.experimental.pallas import tpu as pltpu
from jax.sharding import Mesh, PartitionSpec as P

HEADS = 16
BOOKS = 8
SIZE = 64
LANES = 128
BLOCK = 128

ALL = ("z", "yl", "x", "yh", "c")
CHIPS = ("z", "yl", "x", "yh")
SEQ = ("z", "yl", "x")
SWAP = [(0, 1), (1, 0)]
F32 = jnp.float32
BF16 = jnp.bfloat16


def dot(a, b, ca, cb):
    return lax.dot_general(a, b, (((ca,), (cb,)), ((), ())), preferred_element_type=F32)


def attention_kernel(proj_ref, d_mixed_ref, mixed_ref, d_proj_ref):
    half = d_mixed_ref.shape[1]
    row = lax.broadcasted_iota(jnp.int32, (2 * BLOCK, BLOCK), 0) % BLOCK
    col = lax.broadcasted_iota(jnp.int32, (2 * BLOCK, BLOCK), 1)
    visible = (row // BOOKS == col // BOOKS) & (col <= row)
    low = lax.broadcasted_iota(jnp.int32, (BLOCK, LANES), 1) < SIZE

    def stack(a):
        zero = jnp.zeros_like(a)
        return jnp.concatenate([jnp.where(low, a, zero), jnp.where(low, zero, a)], axis=0)

    def pick(a):
        return jnp.where(low, a[:BLOCK], a[BLOCK:])

    for pair in range(half // LANES):
        cols = slice(pair * LANES, (pair + 1) * LANES)
        kcols = slice(half + pair * LANES, half + (pair + 1) * LANES)
        vcols = slice(2 * half + pair * LANES, 2 * half + (pair + 1) * LANES)
        query = stack(proj_ref[:, cols])
        keys = proj_ref[:, kcols]
        values = proj_ref[:, vcols]
        d_mixed = stack(d_mixed_ref[:, cols])
        scores = dot(query, keys, 1, 1) * F32(0.125)
        weights = jnp.where(visible, jnp.exp(scores), F32(0.0))
        scale = F32(1.0) / jnp.sum(weights, axis=1, keepdims=True)
        exact = weights * scale
        probs = exact.astype(BF16)
        mixed_ref[:, cols] = pick(dot(probs, values, 1, 0)).astype(BF16)
        d_probs = dot(d_mixed, values, 1, 1).astype(BF16).astype(F32)
        inner = jnp.sum(d_probs * exact, axis=1, keepdims=True)
        d_scores = (exact * (d_probs - inner) * F32(0.125)).astype(BF16)
        d_proj_ref[:, cols] = pick(dot(d_scores, keys, 1, 0)).astype(BF16)
        d_proj_ref[:, kcols] = dot(d_scores, query, 0, 0).astype(BF16)
        d_proj_ref[:, vcols] = dot(probs, d_mixed, 0, 0).astype(BF16)


def attention(proj, d_mixed):
    tokens, wide = proj.shape
    half = d_mixed.shape[1]
    return pl.pallas_call(
        attention_kernel,
        grid=(tokens // BLOCK,),
        in_specs=[
            pl.BlockSpec((BLOCK, wide), lambda i: (i, 0)),
            pl.BlockSpec((BLOCK, half), lambda i: (i, 0)),
        ],
        out_specs=[
            pl.BlockSpec((BLOCK, half), lambda i: (i, 0)),
            pl.BlockSpec((BLOCK, wide), lambda i: (i, 0)),
        ],
        out_shape=[
            jax.ShapeDtypeStruct((tokens, half), BF16),
            jax.ShapeDtypeStruct((tokens, wide), BF16),
        ],
        compiler_params=pltpu.CompilerParams(vmem_limit_bytes=24 * 1024 * 1024),
        cost_estimate=pl.CostEstimate(
            flops=12 * tokens * BLOCK * 2 * half,
            bytes_accessed=2 * tokens * (wide + half) * 2,
            transcendentals=tokens * BLOCK * half // SIZE,
        ),
    )(proj, d_mixed)


def merge_kernel(cot_ref, mine_ref, other_ref, d_stream_ref, d_ctx_ref):
    d_flat = (mine_ref[...].astype(F32) + other_ref[...].astype(F32)).astype(BF16)
    d_stream = (cot_ref[...].astype(F32) + d_flat.astype(F32)).astype(BF16)
    d_stream_ref[...] = d_stream
    rows, width = d_stream.shape
    d_ctx = jnp.sum(d_stream.astype(F32).reshape(rows // BOOKS, BOOKS, width), axis=1)
    d_ctx_ref[...] = d_ctx.astype(BF16)


def merge(cot, mine, other):
    tokens, width = cot.shape
    steps = 4
    rows = tokens // steps
    spec = pl.BlockSpec((rows, width), lambda i: (i, 0))
    return pl.pallas_call(
        merge_kernel,
        grid=(steps,),
        in_specs=[spec, spec, pl.BlockSpec((rows, width), lambda i: ((i + steps // 2) % steps, 0))],
        out_specs=[spec, pl.BlockSpec((rows // BOOKS, width), lambda i: (i, 0))],
        out_shape=[
            jax.ShapeDtypeStruct((tokens, width), BF16),
            jax.ShapeDtypeStruct((tokens // BOOKS, width), BF16),
        ],
        compiler_params=pltpu.CompilerParams(vmem_limit_bytes=24 * 1024 * 1024),
        cost_estimate=pl.CostEstimate(
            flops=4 * tokens * width, bytes_accessed=8 * tokens * width, transcendentals=0
        ),
    )(cot, mine, other)


def scatter_sum(parts, axes):
    got = lax.all_to_all(parts, axes, 0, 0, tiled=False)
    return jnp.sum(got.astype(F32), axis=0)


def on_device(hidden, ctx_weight, codes, table, qkv_weight, out_weight, cotangent):
    core = lax.axis_index("c")
    yh = lax.axis_index("yh")
    width = ctx_weight.shape[1]
    half = width // 2
    frames = codes.shape[0]
    tokens = 2 * frames * BOOKS
    vocab = table.shape[0]

    swap = functools.partial(lax.ppermute, axis_name="c", perm=SWAP)
    ids = jnp.concatenate([codes, swap(codes)], axis=0).reshape(tokens)
    cot = cotangent.reshape(frames * BOOKS, width)
    cot = jnp.concatenate([cot, swap(cot)], axis=0)

    partial_ctx = dot(hidden, ctx_weight, 1, 0).astype(BF16).reshape(2, 2 * frames, width)
    away = lax.dynamic_index_in_dim(partial_ctx, 1 - yh, 0, keepdims=False)
    near = lax.dynamic_index_in_dim(partial_ctx, yh, 0, keepdims=False)
    chip_ctx = (near.astype(F32) + lax.ppermute(away, "yh", SWAP).astype(F32)).astype(BF16)
    context = (chip_ctx.astype(F32) + swap(chip_ctx).astype(F32)).astype(BF16)
    context = jnp.where(core == 0, context, jnp.roll(context, frames, axis=0))

    onehot = (ids[:, None] == jnp.arange(vocab, dtype=jnp.int32)[None, :]).astype(BF16)
    embedded = dot(onehot, table, 1, 0).astype(BF16)
    weight = lax.dynamic_index_in_dim(
        qkv_weight.reshape(width, 3, 2, half), core, 2, keepdims=False
    ).reshape(width, 3 * half)
    out_half = lax.dynamic_slice_in_dim(out_weight, core * half, half, 0)
    d_mixed = dot(cot, out_half, 1, 1).astype(BF16)

    stream = (
        embedded.astype(F32).reshape(2 * frames, BOOKS, width) + context.astype(F32)[:, None, :]
    ).astype(BF16).reshape(tokens, width)
    proj = dot(stream, weight, 1, 0).astype(BF16)
    mixed, d_proj = attention(proj, d_mixed)

    d_out = dot(mixed, cot, 0, 0).astype(BF16)
    d_flat = dot(d_proj, weight, 1, 1).astype(BF16)
    d_qkv = dot(stream, d_proj, 0, 0).astype(BF16)

    d_stream, d_ctx = merge(cot, d_flat, swap(d_flat))
    d_ctx = jnp.where(core == 0, d_ctx, jnp.roll(d_ctx, frames, axis=0))
    d_ctx_far = lax.ppermute(d_ctx, "yh", SWAP)
    d_ctx = jnp.where(
        yh == 0,
        jnp.concatenate([d_ctx, d_ctx_far], axis=0),
        jnp.concatenate([d_ctx_far, d_ctx], axis=0),
    )

    chips = 64
    d_out = d_out.reshape(2, 16, 2, 8, width).transpose(2, 0, 1, 3, 4).reshape(chips, 8, width)
    sum_out = scatter_sum(d_out, CHIPS)
    grad_out = lax.ppermute(
        sum_out, ("z", "c"), [(2 * z + c, 2 * (2 * c + z % 2) + z // 2) for z in range(4) for c in range(2)]
    )

    sum_qkv = scatter_sum(d_qkv.reshape(chips, 16, 3 * half), CHIPS)
    keep = lax.dynamic_slice_in_dim(sum_qkv, core * 8, 8, 0)
    give = lax.dynamic_slice_in_dim(sum_qkv, 8 - core * 8, 8, 0)
    take = swap(give)
    keep, take = keep.reshape(8, 3, 1, half), take.reshape(8, 3, 1, half)
    grad_qkv = jnp.where(
        core == 0, jnp.concatenate([keep, take], axis=2), jnp.concatenate([take, keep], axis=2)
    ).reshape(8, 6 * half)

    place = jnp.arange(vocab // 2, dtype=jnp.int32)
    rows = place // 16 * 32 + core * 16 + place % 16
    d_table = dot((rows[:, None] == ids[None, :]).astype(BF16), d_stream, 1, 0).astype(BF16)
    grad_table = scatter_sum(d_table.reshape(chips, 16, width), CHIPS)

    d_hidden = dot(d_ctx, ctx_weight, 1, 1).astype(BF16)
    ctx_part = dot(hidden, d_ctx, 0, 0).astype(BF16)
    ctx_sum = scatter_sum(ctx_part.reshape(32, 32, width), SEQ).astype(BF16)
    grad_ctx = lax.all_to_all(
        jnp.broadcast_to(ctx_sum[None], (32, 32, width)), SEQ, 0, 0, tiled=False
    ).reshape(32 * 32, width).astype(F32)
    return (d_hidden, grad_ctx, grad_table, grad_qkv, grad_out)


def solution(mesh):
    fine = Mesh(mesh.devices.reshape(4, 2, 4, 2, 2), ALL)
    in_specs = (
        P(SEQ, ("yh", "c")),
        P(("yh", "c"), None),
        P(ALL, None),
        P(),
        P(),
        P(),
        P(ALL, None, None),
    )
    out_specs = (
        P(SEQ, ("yh", "c")),
        P(("yh", "c"), None),
        P(ALL, None),
        P(ALL, None),
        P(ALL, None),
    )
    return jax.shard_map(
        on_device, mesh=fine, in_specs=in_specs, out_specs=out_specs, check_vma=False
    )
```

time: 2400 us -> 257 us (0.11)
  waiting for transfers between devices: 2250 us -> 106 us
  starting transfers between devices: 0.43 us -> 55.1 us
  matrix products: 65.4 us -> 40.5 us
    reduce_scatter x4 -> x0, waiting for transfers between devices: 1990 us -> none  [the longest x1 659 us: on_device(): lax.psum_scatter(d_out, ('seq', 'tp'), scatter_dimension=0, tiled=True)]
    psum x1 -> x0, waiting for transfers between devices: 259 us -> none  [on_device(): lax.psum(ctx_part.astype(jnp.bfloat16), 'seq').astype(jnp.float32)]
    all_to_all x0 -> x5, waiting for transfers between devices: none -> 55.9 us  [the longest x4 55.9 us: scatter_sum(): got = lax.all_to_all(parts, axes, 0, 0, tiled=False)]
    ppermute x0 -> x8, waiting for transfers between devices: none -> 49.7 us  [the longest x1 32.8 us: on_device(): d_ctx_far = lax.ppermute(d_ctx, 'yh', SWAP)]
    all_to_all x0 -> x5, starting transfers between devices: none -> 40.5 us  [the longest x4 35.7 us: scatter_sum(): got = lax.all_to_all(parts, axes, 0, 0, tiled=False)]
    dot_general x16 -> x10, matrix products: 65.4 us -> 40.5 us  [dot(): lax.dot_general(a, b, (((ca,), (cb,)), ((), ())), preferred_element_type=...]
  transfers between devices with their start and end apart: 5 -> 13, of which waited for: 5 -> 5; matrix products, arithmetic and copies ran while one was open for 2% -> 22% of each run, Pallas kernels for 0% -> 2%
where the time goes in v1:
time: 257 us; the launch traced here: 254 us
  waiting for transfers between devices  106 us (41%)
  starting transfers between devices  55.1 us (21%)
  matrix products  40.5 us (16%)
  Pallas kernels  19.5 us (8%)
  local copies, waits for them, and re-layouts  18 us (7%)
  other arithmetic  14.2 us (6%)
    all_to_all x4, waiting for transfers between devices, scatter_sum(): got = lax.all_to_all(parts, axes, 0, 0, tiled=False)  55.9 us
    dot_general x10, matrix products, dot(): lax.dot_general(a, b, (((ca,), (cb,)), ((), ())), preferred_element_type=...  40.5 us
    all_to_all x4, starting transfers between devices, scatter_sum(): got = lax.all_to_all(parts, axes, 0, 0, tiled=False)  35.7 us
    ppermute x1, waiting for transfers between devices, on_device(): d_ctx_far = lax.ppermute(d_ctx, 'yh', SWAP)  32.8 us
    ppermute x1, waiting for transfers between devices, on_device(): lax.ppermute(sum_out, ('z', 'c'), [(2 * z + c, 2 * (2 * c + z % 2) + z //...  16.9 us
    pallas_call x1, Pallas kernels, attention(): pl.pallas_call(attention_kernel, grid=(tokens // BLOCK,), in_specs=[pl.Bl...  15.5 us
    unnamed x32, local copies, waits for them, and re-layouts  10.9 us
    ppermute x1, starting transfers between devices, on_device(): lax.ppermute(sum_out, ('z', 'c'), [(2 * z + c, 2 * (2 * c + z % 2) + z //...  6.29 us
  transfers between devices with their start and end apart: 13, of which 5 were waited for; matrix products, arithmetic and copies ran while one was open for 22% of the time, Pallas kernels for 2%

profile of v1, /device:TPU:1, one launch (start us, length us, event | category | flops | bytes accessed | tf_op | source)
XLA Modules:
  0.0 253.8 jit_solution(17497581157803763703)
XLA Ops:
  0.6 0.0 copy-start
  0.7 0.0 copy-start.9
  0.7 2.6 %convolution_convert_fusion.7 = bf16[256,1024]{1,0:T(8,128)(2,1)S(1)} fusion(bf16[256,1024]{1,0:T(8,128)(2,1)} %param.7, bf16[1024,1024]{1,0:T(8,128)(2,1)} %param.8), kind=kOutput, calls=%fused_computation.22 | convolution fusion | flops 537133056 | bytes 3145728 | tf_op jit(solution)/shard_map/dot_general | solution.py:25
  3.3 0.0 copy-start.10
  3.3 3.8 %collective-permute-start.2 = (bf16[128,1024]{1,0:T(8,128)(2,1)S(1)}, bf16[128,1024]{1,0:T(8,128)(2,1)}, u32[]{:S(2)}, u32[]{:S(2)}) collective-permute-start(bf16[128,1024]{1,0:T(8,128)(2,1)S(1)} %dynamic-slice_bitcast_fusion), channel_id=1, source_target_pairs={{0,2},{2,0},{1,3},{3,1},{4,6},{6,4},{5,7},{7,5},{8,10},{10,8},{9,1... | collective-permute-start | bytes 786440 | tf_op jit(solution)/shard_map/ppermute | solution.py:143
  7.2 1.0 collective-permute-start.1
  8.1 0.1 collective-permute-start
  8.2 8.6 %copy.15 = bf16[1024,3072]{0,1:T(8,128)(2,1)} copy(bf16[1024,3072]{1,0:T(8,128)(2,1)} %param.11) | data formatting | bytes 12582912 | tf_op args[4]
  16.9 0.0 collective-permute-done.2
  16.9 1.1 fusion.11
  18.0 0.5 collective-permute-start.3
  18.5 3.9 %constant_dynamic-slice_fusion.2 = bf16[1024,3,1,512]{0,3,2,1:T(8,128)(2,1)} fusion(bf16[1024,3,2,512]{0,3,2,1:T(8,128)(2,1)} %bitcast.41, s32[]{:T(128)S(6)} %select_n.77), kind=kLoop, calls=%fused_computation.51 | loop fusion | bytes 6291460 | tf_op jit(solution)/shard_map/jit(dynamic_index_in_dim)/dynamic_slice | solution.py:149
  22.3 0.0 collective-permute-done.1
  22.3 0.1 pad_add_fusion
  22.4 0.1 copy.14
  22.5 0.1 eq.40
  22.6 0.0 collective-permute-done.3
  22.6 1.0 add_convert_fusion
  23.7 0.1 fusion.12
  23.7 0.0 copy-start.8
  23.7 7.2 %fusion.1 = bf16[1024,1024]{1,0:T(8,128)(2,1)S(1)} fusion(f32[128,1024]{1,0:T(8,128)S(1)} %fusion.12, bf16[2048,1024]{1,0:T(8,128)(2,1)} %param.10, s32[1024]{0:T(1024)S(1)} %eq.40), kind=kOutput, calls=%fused_computation.4 | convolution fusion | flops 4301258752 | bytes 6819840 | tf_op jit(solution)/shard_map/dot_general | solution.py:25
  31.0 3.7 %convolution_convert_fusion.1.proj_ref = bf16[1024,1536]{1,0:T(8,128)(2,1)S(1)} fusion(bf16[1024,1024]{1,0:T(8,128)(2,1)S(1)} %fusion.1, bf16[1024,1536]{0,1:T(8,128)(2,1)S(1)} %bitcast.43), kind=kOutput, calls=%fused_computation.10 | convolution fusion | flops 3222798336 | bytes 8388608 | tf_op jit(solution)/shard_map/dot_general | solution.py:25
  34.8 0.0 collective-permute-done
  34.8 2.5 convolution_convert_fusion.5.d_mixed_ref
  37.3 15.5 %shard_map.110 = (bf16[1024,512]{1,0:T(8,128)(2,1)S(1)}, bf16[1024,1536]{1,0:T(8,128)(2,1)S(1)}) custom-call(bf16[1024,1536]{1,0:T(8,128)(2,1)S(1)} %convolution_convert_fusion.1.proj_ref, bf16[1024,512]{1,0:T(8,128)(2,1)S(1)} %convolution_convert_fusion.5.d_mixed_ref), custom_call_target="tpu_custom_call" | custom-call | flops 1610612736 | bytes 8388608 | tf_op jit(solution)/shard_map/pallas_call | solution.py:67
  52.8 3.3 %convolution_convert_fusion.4 = bf16[512,1024]{1,0:T(8,128)(2,1)S(1)} fusion(bf16[1024,512]{1,0:T(8,128)(2,1)S(1)} %get-tuple-element.12, bf16[512,1024]{1,0:T(8,128)(2,1)} %collective-permute-done, bf16[512,1024]{1,0:T(8,128)(2,1)S(1)} %bitcast.51), kind=kOutput, calls=%fused_computation.19 | convolution fusion | flops 1078460416 | bytes 4194304 | tf_op jit(solution)/shard_map/dot_general | solution.py:25
  56.1 1.2 copy.16
  57.3 9.2 %all-to-all-start.4 = ((bf16[64,8,1024]{2,1,0:T(8,128)(2,1)}), bf16[64,8,1024]{2,1,0:T(8,128)(2,1)S(1)}, u32[]{:S(2)}, u32[]{:S(2)}) async-start(bf16[64,8,1024]{2,1,0:T(8,128)(2,1)} %bitcast.17), calls=%async_computation.4 | async-start | bytes 2097152 | tf_op jit(solution)/shard_map/all_to_all | solution.py:122
  66.5 6.4 %convolution_convert_fusion.3.mine_ref = bf16[1024,1024]{1,0:T(8,128)(2,1)S(1)} fusion(bf16[1024,1536]{1,0:T(8,128)(2,1)} %copy-done.4, bf16[1024,1536]{0,1:T(8,128)(2,1)} %bitcast.42), kind=kOutput, calls=%fused_computation.18 | convolution fusion | flops 3222274048 | bytes 8388608 | tf_op jit(solution)/shard_map/dot_general | solution.py:25
  72.9 0.4 collective-permute-start.4
  73.4 4.9 %convolution_convert_fusion = bf16[1024,1536]{1,0:T(8,128)(2,1)} fusion(bf16[1024,1024]{1,0:T(8,128)(2,1)S(1)} %copy-done.14, bf16[1024,1536]{1,0:T(8,128)(2,1)S(1)} %copy-done.5), kind=kOutput, calls=%fused_computation.9 | convolution fusion | flops 3222798336 | bytes 8388608 | tf_op jit(solution)/shard_map/dot_general | solution.py:25
  78.3 6.1 %all-to-all-done.4 = bf16[64,8,1024]{2,1,0:T(8,128)(2,1)S(1)} async-done(((bf16[64,8,1024]{2,1,0:T(8,128)(2,1)}), bf16[64,8,1024]{2,1,0:T(8,128)(2,1)S(1)}, u32[]{:S(2)}, u32[]{:S(2)}) %all-to-all-start.4) | async-done | bytes 1048608 | tf_op jit(solution)/shard_map/all_to_all | solution.py:122
  84.4 5.6 %all-to-all-start.3 = ((bf16[64,16,1536]{2,1,0:T(8,128)(2,1)}), bf16[64,16,1536]{2,1,0:T(8,128)(2,1)}, u32[]{:S(2)}, u32[]{:S(2)}) async-start(bf16[64,16,1536]{2,1,0:T(8,128)(2,1)} %bitcast.44), calls=%async_computation.3 | async-start | bytes 6291456 | tf_op jit(solution)/shard_map/all_to_all | solution.py:122
  90.0 1.7 pad_maximum_fusion.cot_ref
  91.7 0.0 collective-permute-done.4.other_ref
  91.7 4.0 %shard_map.111 = (bf16[1024,1024]{1,0:T(8,128)(2,1)S(1)}, bf16[128,1024]{1,0:T(8,128)(2,1)S(1)}) custom-call(bf16[1024,1024]{1,0:T(8,128)(2,1)S(1)} %pad_maximum_fusion.cot_ref, bf16[1024,1024]{1,0:T(8,128)(2,1)S(1)} %convolution_convert_fusion.3.mine_ref, bf16[1024,1024]{1,0:T(8,128)(2,1)} %collective-permute-done.4.other_ref), custom_call_target="tpu_custom_call" | custom-call | flops 4194304 | bytes 8388608 | tf_op jit(solution)/shard_map/pallas_call | solution.py:105
  95.7 1.4 copy-done.2
  97.1 0.1 maximum_select_fusion.2
  97.2 2.4 collective-permute-start.5
  99.6 32.8 %collective-permute-done.5 = bf16[128,1024]{1,0:T(8,128)(2,1)} collective-permute-done((bf16[128,1024]{1,0:T(8,128)(2,1)S(1)}, bf16[128,1024]{1,0:T(8,128)(2,1)}, u32[]{:S(2)}, u32[]{:S(2)}) %collective-permute-start.5) | collective-permute-done | bytes 262176 | tf_op jit(solution)/shard_map/ppermute | solution.py:167
  132.4 3.4 %convolution_convert_fusion.2 = bf16[1024,1024]{0,1:T(8,128)(2,1)} fusion(bf16[256,1024]{1,0:T(8,128)(2,1)} %param.7, bf16[128,1024]{1,0:T(8,128)(2,1)} %collective-permute-done.5, bf16[128,1024]{1,0:T(8,128)(2,1)S(1)} %maximum_select_fusion.2, pred[]{:T(512)S(6)} %eq.38), kind=kOutput, calls=%fused_computation.17 | convolution fusion | flops 540278784 | bytes 3145729 | tf_op jit(solution)/shard_map/dot_general | solution.py:25
  135.8 0.0 all-to-all-done.3
  135.8 8.1 %all-to-all-start = ((bf16[32,32,1024]{2,1,0:T(8,128)(2,1)}), bf16[32,32,1024]{2,1,0:T(8,128)(2,1)}, u32[]{:S(2)}, u32[]{:S(2)}) async-start(bf16[32,32,1024]{2,1,0:T(8,128)(2,1)} %bitcast.45), calls=%async_computation | async-start | bytes 4194304 | tf_op jit(solution)/shard_map/all_to_all | solution.py:122
  143.9 3.7 %fusion.7 = bf16[1024,1024]{1,0:T(8,128)(2,1)} fusion(bf16[1024,1024]{1,0:T(8,128)(2,1)S(1)} %copy-done.3, s32[1024]{0:T(1024)S(1)} %eq.40, s32[1024]{0:T(1024)S(1)} %fusion.21), kind=kOutput, calls=%fused_computation.16 | convolution fusion | flops 2149580800 | bytes 4202496 | tf_op jit(solution)/shard_map/dot_general | solution.py:25
  147.6 22.5 %all-to-all-done = bf16[32,32,1024]{2,1,0:T(8,128)(2,1)} async-done(((bf16[32,32,1024]{2,1,0:T(8,128)(2,1)}), bf16[32,32,1024]{2,1,0:T(8,128)(2,1)}, u32[]{:S(2)}, u32[]{:S(2)}) %all-to-all-start) | async-done | bytes 2097184 | tf_op jit(solution)/shard_map/all_to_all | solution.py:122
  170.1 12.8 %all-to-all-start.2 = ((bf16[64,16,1024]{2,1,0:T(8,128)(2,1)}), bf16[64,16,1024]{2,1,0:T(8,128)(2,1)S(1)}, u32[]{:S(2)}, u32[]{:S(2)}) async-start(bf16[64,16,1024]{2,1,0:T(8,128)(2,1)} %bitcast.46), calls=%async_computation.2 | async-start | bytes 4194304 | tf_op jit(solution)/shard_map/all_to_all | solution.py:122
  182.9 2.0 reduce_sum.39
  184.9 27.3 %all-to-all-done.2 = bf16[64,16,1024]{2,1,0:T(8,128)(2,1)S(1)} async-done(((bf16[64,16,1024]{2,1,0:T(8,128)(2,1)}), bf16[64,16,1024]{2,1,0:T(8,128)(2,1)S(1)}, u32[]{:S(2)}, u32[]{:S(2)}) %all-to-all-start.2) | async-done | bytes 2097184 | tf_op jit(solution)/shard_map/all_to_all | solution.py:122
  212.2 1.8 broadcast_in_dim.2
  214.0 0.2 copy-done.6
  214.2 4.8 %all-to-all-start.1 = ((bf16[32,32,1024]{2,1,0:T(8,128)(2,1)}), bf16[32,32,1024]{2,1,0:T(8,128)(2,1)}, u32[]{:S(2)}, u32[]{:S(2)}) async-start(bf16[32,32,1024]{2,1,0:T(8,128)(2,1)} %broadcast_in_dim.2), calls=%async_computation.1 | async-start | bytes 4194304 | tf_op jit(solution)/shard_map/all_to_all | solution.py:198
  218.9 0.2 convert_reduce_fusion.2
  219.1 6.3 %collective-permute-start.7 = (f32[8,1024]{1,0:T(8,128)S(1)}, f32[8,1024]{1,0:T(8,128)S(1)}, u32[]{:S(2)}, u32[]{:S(2)}) collective-permute-start(f32[8,1024]{1,0:T(8,128)S(1)} %convert_reduce_fusion.2), channel_id=1, source_target_pairs={{0,0},{1,64},{32,32},{33,96},{64,1},{65,65},{96,33},{97,97},{2,2},... | collective-permute-start | bytes 98312 | tf_op jit(solution)/shard_map/ppermute | solution.py:177
  225.4 0.0 copy-start.12
  225.4 16.9 %collective-permute-done.7 = f32[8,1024]{1,0:T(8,128)S(1)} collective-permute-done((f32[8,1024]{1,0:T(8,128)S(1)}, f32[8,1024]{1,0:T(8,128)S(1)}, u32[]{:S(2)}, u32[]{:S(2)}) %collective-permute-start.7) | collective-permute-done | bytes 32800 | tf_op jit(solution)/shard_map/ppermute | solution.py:177
  242.3 2.3 convert_reduce_fusion
  244.7 0.1 collective-permute-start.6
  244.8 2.7 %convolution_convert_fusion.6 = bf16[256,1024]{1,0:T(8,128)(2,1)} fusion(bf16[1024,1024]{1,0:T(8,128)(2,1)S(1)} %copy-done.12, bf16[128,1024]{1,0:T(8,128)(2,1)} %collective-permute-done.5, bf16[128,1024]{1,0:T(8,128)(2,1)S(1)} %maximum_select_fusion.2, pred[]{:T(512)S(6)} %eq.38), kind=kOutput, calls=%fused_computation.21 | convolution fusion | flops 539492352 | bytes 3145729 | tf_op jit(solution)/shard_map/dot_general | solution.py:25
  247.5 0.0 collective-permute-done.6
  247.5 0.6 maximum_select_fusion.3
  248.2 1.0 convert_reduce_fusion.1
  249.2 0.0 all-to-all-done.1
  249.2 4.1 %bitcast_convert_fusion = f32[1024,1024]{1,0:T(8,128)} fusion(bf16[32,32,1024]{2,1,0:T(8,128)(2,1)} %all-to-all-done.1), kind=kLoop, calls=%fused_computation.12 | loop fusion | flops 1048576 | bytes 6291456 | tf_op jit(solution)/shard_map/convert_element_type | solution.py:200
  253.2 0.6 copy.18
  (28 shorter events, 0.1 us)
Async XLA Ops:
  0.6 34.1 %copy-start = (bf16[1024,1024]{1,0:T(8,128)(2,1)S(1)}, bf16[1024,1024]{1,0:T(8,128)(2,1)}, u32[]{:S(2)}) copy-start(bf16[1024,1024]{1,0:T(8,128)(2,1)} %param.12) | copy-start | bytes 6291460
  0.6 6.5 %copy-start.11 = (s32[64,8]{0,1:T(8,128)S(1)}, s32[64,8]{0,1:T(8,128)}, u32[]{:S(2)}) copy-start(s32[64,8]{0,1:T(8,128)} %param.9) | copy-start | bytes 6148
  0.7 7.5 %copy-start.9 = (bf16[64,8,1024]{2,1,0:T(8,128)(2,1)S(1)}, bf16[64,8,1024]{2,1,0:T(8,128)(2,1)}, u32[]{:S(2)}) copy-start(bf16[64,8,1024]{2,1,0:T(8,128)(2,1)} %param.13) | copy-start | bytes 3145732
  3.3 4.8 %copy-start.10 = (bf16[256,1024]{1,0:T(8,128)(2,1)}, bf16[256,1024]{1,0:T(8,128)(2,1)S(1)}, u32[]{:S(2)}) copy-start(bf16[256,1024]{1,0:T(8,128)(2,1)S(1)} %convolution_convert_fusion.7) | copy-start | bytes 1572868
  3.3 13.5 %collective-permute-start.2 = (bf16[128,1024]{1,0:T(8,128)(2,1)S(1)}, bf16[128,1024]{1,0:T(8,128)(2,1)}, u32[]{:S(2)}, u32[]{:S(2)}) collective-permute-start(bf16[128,1024]{1,0:T(8,128)(2,1)S(1)} %dynamic-slice_bitcast_fusion), channel_id=1, source_target_pairs={{0,2},{2,0},{1,3},{3,1},{4,6},{6,4},{5,7},{7,5},{8,10},{10,8},{9,1... | collective-permute-start | bytes 786440 | tf_op jit(solution)/shard_map/ppermute | solution.py:143
  7.2 15.2 %collective-permute-start.1 = (s32[64,8]{0,1:T(8,128)S(1)}, s32[64,8]{0,1:T(8,128)S(1)}, u32[]{:S(2)}, u32[]{:S(2)}) collective-permute-start(s32[64,8]{0,1:T(8,128)S(1)} %copy-done.11), channel_id=1, source_target_pairs={{0,1},{1,0},{2,3},{3,2},{4,5},{5,4},{6,7},{7,6},{8,9},{9,8},{10,11... | collective-permute-start | bytes 6152 | tf_op jit(solution)/shard_map/ppermute | solution.py:136
  8.1 26.6 %collective-permute-start = (bf16[512,1024]{1,0:T(8,128)(2,1)S(1)}, bf16[512,1024]{1,0:T(8,128)(2,1)}, u32[]{:S(2)}, u32[]{:S(2)}) collective-permute-start(bf16[512,1024]{1,0:T(8,128)(2,1)S(1)} %bitcast.49), channel_id=1, source_target_pairs={{0,1},{1,0},{2,3},{3,2},{4,5},{5,4},{6,7},{7,6},{8,9},{9,8},{10,11... | collective-permute-start | bytes 3145736 | tf_op jit(solution)/shard_map/ppermute | solution.py:138
  18.0 4.6 %collective-permute-start.3 = (bf16[128,1024]{1,0:T(8,128)(2,1)S(1)}, bf16[128,1024]{1,0:T(8,128)(2,1)}, u32[]{:S(2)}, u32[]{:S(2)}) collective-permute-start(bf16[128,1024]{1,0:T(8,128)(2,1)S(1)} %fusion.11), channel_id=1, source_target_pairs={{0,1},{1,0},{2,3},{3,2},{4,5},{5,4},{6,7},{7,6},{8,9},{9,8},{10,11... | collective-permute-start | bytes 786440 | tf_op jit(solution)/shard_map/ppermute | solution.py:144
  23.7 7.3 %copy-start.8 = (bf16[1024,3,1,512]{0,3,2,1:T(8,128)(2,1)S(1)}, bf16[1024,3,1,512]{0,3,2,1:T(8,128)(2,1)}, u32[]{:S(2)}) copy-start(bf16[1024,3,1,512]{0,3,2,1:T(8,128)(2,1)} %constant_dynamic-slice_fusion.2) | copy-start | bytes 9437188
  31.0 3.8 %copy-start.13 = (bf16[1024,1024]{1,0:T(8,128)(2,1)}, bf16[1024,1024]{1,0:T(8,128)(2,1)S(1)}, u32[]{:S(2)}) copy-start(bf16[1024,1024]{1,0:T(8,128)(2,1)S(1)} %fusion.1) | copy-start | bytes 6291460
  52.8 4.5 %copy-start.4 = (bf16[1024,1536]{1,0:T(8,128)(2,1)}, bf16[1024,1536]{1,0:T(8,128)(2,1)S(1)}, u32[]{:S(2)}) copy-start(bf16[1024,1536]{1,0:T(8,128)(2,1)S(1)} %get-tuple-element.9) | copy-start | bytes 9437188
  57.3 27.1 %all-to-all-start.4 = ((bf16[64,8,1024]{2,1,0:T(8,128)(2,1)}), bf16[64,8,1024]{2,1,0:T(8,128)(2,1)S(1)}, u32[]{:S(2)}, u32[]{:S(2)}) async-start(bf16[64,8,1024]{2,1,0:T(8,128)(2,1)} %bitcast.17), calls=%async_computation.4 | async-start | bytes 2097152 | tf_op jit(solution)/shard_map/all_to_all | solution.py:122
  66.5 6.9 %copy-start.5 = (bf16[1024,1536]{1,0:T(8,128)(2,1)S(1)}, bf16[1024,1536]{1,0:T(8,128)(2,1)}, u32[]{:S(2)}) copy-start(bf16[1024,1536]{1,0:T(8,128)(2,1)} %copy-done.4) | copy-start | bytes 9437188
  66.5 6.9 %copy-start.14 = (bf16[1024,1024]{1,0:T(8,128)(2,1)S(1)}, bf16[1024,1024]{1,0:T(8,128)(2,1)}, u32[]{:S(2)}) copy-start(bf16[1024,1024]{1,0:T(8,128)(2,1)} %copy-done.13) | copy-start | bytes 6291460
  72.9 18.8 %collective-permute-start.4 = (bf16[1024,1024]{1,0:T(8,128)(2,1)S(1)}, bf16[1024,1024]{1,0:T(8,128)(2,1)}, u32[]{:S(2)}, u32[]{:S(2)}) collective-permute-start(bf16[1024,1024]{1,0:T(8,128)(2,1)S(1)} %convolution_convert_fusion.3.mine_ref), channel_id=1, source_target_pairs={{0,1},{1,0},{2,3},{3,2},{4,5},{5,4},{6,7},{7,6},{8,9},{9,8},{10,11... | collective-permute-start | bytes 6291464 | tf_op jit(solution)/shard_map/ppermute | solution.py:165
  84.4 51.4 %all-to-all-start.3 = ((bf16[64,16,1536]{2,1,0:T(8,128)(2,1)}), bf16[64,16,1536]{2,1,0:T(8,128)(2,1)}, u32[]{:S(2)}, u32[]{:S(2)}) async-start(bf16[64,16,1536]{2,1,0:T(8,128)(2,1)} %bitcast.44), calls=%async_computation.3 | async-start | bytes 6291456 | tf_op jit(solution)/shard_map/all_to_all | solution.py:122
  95.7 1.4 copy-start.2
  97.2 35.2 %collective-permute-start.5 = (bf16[128,1024]{1,0:T(8,128)(2,1)S(1)}, bf16[128,1024]{1,0:T(8,128)(2,1)}, u32[]{:S(2)}, u32[]{:S(2)}) collective-permute-start(bf16[128,1024]{1,0:T(8,128)(2,1)S(1)} %maximum_select_fusion.2), channel_id=1, source_target_pairs={{0,2},{2,0},{1,3},{3,1},{4,6},{6,4},{5,7},{7,5},{8,10},{10,8},{9,1... | collective-permute-start | bytes 786440 | tf_op jit(solution)/shard_map/ppermute | solution.py:167
  99.6 44.3 %copy-start.3 = (bf16[1024,1024]{1,0:T(8,128)(2,1)S(1)}, bf16[1024,1024]{1,0:T(8,128)(2,1)}, u32[]{:S(2)}) copy-start(bf16[1024,1024]{1,0:T(8,128)(2,1)} %copy-done.2) | copy-start | bytes 6291460
  135.8 34.3 %all-to-all-start = ((bf16[32,32,1024]{2,1,0:T(8,128)(2,1)}), bf16[32,32,1024]{2,1,0:T(8,128)(2,1)}, u32[]{:S(2)}, u32[]{:S(2)}) async-start(bf16[32,32,1024]{2,1,0:T(8,128)(2,1)} %bitcast.45), calls=%async_computation | async-start | bytes 4194304 | tf_op jit(solution)/shard_map/all_to_all | solution.py:122
  170.1 42.1 %all-to-all-start.2 = ((bf16[64,16,1024]{2,1,0:T(8,128)(2,1)}), bf16[64,16,1024]{2,1,0:T(8,128)(2,1)S(1)}, u32[]{:S(2)}, u32[]{:S(2)}) async-start(bf16[64,16,1024]{2,1,0:T(8,128)(2,1)} %bitcast.46), calls=%async_computation.2 | async-start | bytes 4194304 | tf_op jit(solution)/shard_map/all_to_all | solution.py:122
  212.2 2.0 copy-start.6
  214.2 35.0 %all-to-all-start.1 = ((bf16[32,32,1024]{2,1,0:T(8,128)(2,1)}), bf16[32,32,1024]{2,1,0:T(8,128)(2,1)}, u32[]{:S(2)}, u32[]{:S(2)}) async-start(bf16[32,32,1024]{2,1,0:T(8,128)(2,1)} %broadcast_in_dim.2), calls=%async_computation.1 | async-start | bytes 4194304 | tf_op jit(solution)/shard_map/all_to_all | solution.py:198
  219.1 23.2 %collective-permute-start.7 = (f32[8,1024]{1,0:T(8,128)S(1)}, f32[8,1024]{1,0:T(8,128)S(1)}, u32[]{:S(2)}, u32[]{:S(2)}) collective-permute-start(f32[8,1024]{1,0:T(8,128)S(1)} %convert_reduce_fusion.2), channel_id=1, source_target_pairs={{0,0},{1,64},{32,32},{33,96},{64,1},{65,65},{96,33},{97,97},{2,2},... | collective-permute-start | bytes 98312 | tf_op jit(solution)/shard_map/ppermute | solution.py:177
  225.4 19.4 %copy-start.12 = (bf16[1024,1024]{1,0:T(8,128)(2,1)S(1)}, bf16[1024,1024]{1,0:T(8,128)(2,1)}, u32[]{:S(2)}) copy-start(bf16[1024,1024]{1,0:T(8,128)(2,1)} %param.8) | copy-start | bytes 6291460
  244.7 3.5 %copy-start.7 = (bf16[64,16,1024]{2,1,0:T(8,128)(2,1)S(1)}, bf16[64,16,1024]{2,1,0:T(8,128)(2,1)}, u32[]{:S(2)}) copy-start(bf16[64,16,1024]{2,1,0:T(8,128)(2,1)} %copy-done.6) | copy-start | bytes 6291460
  244.7 2.8 %collective-permute-start.6 = (f32[8,1536]{1,0:T(8,128)S(1)}, f32[8,1536]{1,0:T(8,128)S(1)}, u32[]{:S(2)}, u32[]{:S(2)}) collective-permute-start(f32[8,1536]{1,0:T(8,128)S(1)} %get-tuple-element.18), channel_id=1, source_target_pairs={{0,1},{1,0},{2,3},{3,2},{4,5},{5,4},{6,7},{7,6},{8,9},{9,8},{10,11... | collective-permute-start | bytes 147464 | tf_op jit(solution)/shard_map/ppermute | solution.py:184
  248.2 5.7 %copy-start.1 = (bf16[1024,1024]{1,0:T(8,128)(2,1)S(1)}, bf16[1024,1024]{1,0:T(8,128)(2,1)}, u32[]{:S(2)}) copy-start(bf16[1024,1024]{1,0:T(8,128)(2,1)} %param.12) | copy-start | bytes 6291460

commit v2 on v1

v2 whole, which is shorter than its diff:
```python
import functools

import jax
import jax.numpy as jnp
from jax import lax
from jax.experimental import pallas as pl
from jax.experimental.pallas import tpu as pltpu
from jax.sharding import Mesh, PartitionSpec as P

HEADS = 16
BOOKS = 8
SIZE = 64
LANES = 128
BLOCK = 128

ALL = ("z", "yl", "x", "yh", "c")
CHIPS = ("z", "yl", "x", "yh")
SEQ = ("z", "yl", "x")
SWAP = [(0, 1), (1, 0)]
F32 = jnp.float32
BF16 = jnp.bfloat16


def dot(a, b, ca, cb):
    return lax.dot_general(a, b, (((ca,), (cb,)), ((), ())), preferred_element_type=F32)


def attend(query, keys, values, d_mixed):
    row = lax.broadcasted_iota(jnp.int32, (2 * BLOCK, BLOCK), 0) % BLOCK
    col = lax.broadcasted_iota(jnp.int32, (2 * BLOCK, BLOCK), 1)
    visible = (row // BOOKS == col // BOOKS) & (col <= row)
    low = lax.broadcasted_iota(jnp.int32, (BLOCK, LANES), 1) < SIZE

    def stack(a):
        zero = jnp.zeros_like(a)
        return jnp.concatenate([jnp.where(low, a, zero), jnp.where(low, zero, a)], axis=0)

    def pick(a):
        return jnp.where(low, a[:BLOCK], a[BLOCK:]).astype(BF16)

    query, d_mixed = stack(query), stack(d_mixed)
    scores = dot(query, keys, 1, 1) * F32(0.125)
    weights = jnp.where(visible, jnp.exp(scores), F32(0.0))
    exact = weights * (F32(1.0) / jnp.sum(weights, axis=1, keepdims=True))
    probs = exact.astype(BF16)
    mixed = pick(dot(probs, values, 1, 0))
    d_probs = dot(d_mixed, values, 1, 1).astype(BF16).astype(F32)
    inner = jnp.sum(d_probs * exact, axis=1, keepdims=True)
    d_scores = (exact * (d_probs - inner) * F32(0.125)).astype(BF16)
    d_query = pick(dot(d_scores, keys, 1, 0))
    d_keys = dot(d_scores, query, 0, 0).astype(BF16)
    d_values = dot(probs, d_mixed, 0, 0).astype(BF16)
    return mixed, d_query, d_keys, d_values


def block_kernel(
    core_ref, emb_ref, ctx_ref, cot_ref, wq_ref, wk_ref, wv_ref, wo_ref, d_flat_ref, grad_ref,
    proj, d_proj, d_mixed, mixed, acc_qkv, acc_out,
):
    step = pl.program_id(0)
    rows, width = emb_ref.shape
    half = wq_ref.shape[1]
    stream = (
        emb_ref[...].astype(F32).reshape(rows // BOOKS, BOOKS, width)
        + ctx_ref[...].astype(F32)[:, None, :]
    ).reshape(rows, width).astype(BF16)
    cot = cot_ref[...]
    for part, w_ref in enumerate((wq_ref, wk_ref, wv_ref)):
        proj[:, part * half : (part + 1) * half] = dot(stream, w_ref[...], 1, 0).astype(BF16)
    d_mixed[...] = dot(cot, wo_ref[...], 1, 1).astype(BF16)
    for block in range(rows // BLOCK):
        at = slice(block * BLOCK, (block + 1) * BLOCK)
        for pair in range(half // LANES):
            q = slice(pair * LANES, (pair + 1) * LANES)
            k = slice(half + pair * LANES, half + (pair + 1) * LANES)
            v = slice(2 * half + pair * LANES, 2 * half + (pair + 1) * LANES)
            mixed[at, q], d_proj[at, q], d_proj[at, k], d_proj[at, v] = attend(
                proj[at, q], proj[at, k], proj[at, v], d_mixed[at, q]
            )
    d_flat = dot(d_proj[:, :half], wq_ref[...], 1, 1)
    d_flat += dot(d_proj[:, half : 2 * half], wk_ref[...], 1, 1)
    d_flat += dot(d_proj[:, 2 * half :], wv_ref[...], 1, 1)
    d_flat_ref[...] = d_flat.astype(BF16)

    @pl.when(step == 0)
    def _():
        acc_qkv[...] = dot(stream, d_proj[...], 0, 0)
        acc_out[...] = dot(mixed[...], cot, 0, 0)

    @pl.when(step > 0)
    def _():
        acc_qkv[...] += dot(stream, d_proj[...], 0, 0)
        acc_out[...] += dot(mixed[...], cot, 0, 0)

    @pl.when(step == pl.num_programs(0) - 1)
    def _():
        grad_ref[:, : 3 * half] = acc_qkv[...].astype(BF16)
        for chip in range(width // 16):
            source = (chip % 32) * 2 + chip // 32
            own = acc_out[source * 8 : (source + 1) * 8, :]
            grad_ref[chip * 16 : (chip + 1) * 16, 3 * half :] = jnp.concatenate(
                [own[:, :half], own[:, half:]], axis=0
            ).astype(BF16)


def block(core, embedded, context, cot, qkv_weight, out_weight):
    tokens, width = cot.shape
    half = width // 2
    steps = 4
    rows = tokens // steps
    tall = pl.BlockSpec((rows, width), lambda i, c: (i, 0))

    def third(part):
        return pl.BlockSpec((width, half), lambda i, c: (0, 2 * part + c[0]))

    return pl.pallas_call(
        block_kernel,
        grid_spec=pltpu.PrefetchScalarGridSpec(
            num_scalar_prefetch=1,
            grid=(steps,),
            in_specs=[
                tall,
                pl.BlockSpec((rows // BOOKS, width), lambda i, c: (i, 0)),
                tall,
                third(0),
                third(1),
                third(2),
                pl.BlockSpec((half, width), lambda i, c: (c[0], 0)),
            ],
            out_specs=[tall, pl.BlockSpec((width, 2 * width), lambda i, c: (0, 0))],
            scratch_shapes=[
                pltpu.VMEM((rows, 3 * half), BF16),
                pltpu.VMEM((rows, 3 * half), BF16),
                pltpu.VMEM((rows, half), BF16),
                pltpu.VMEM((rows, half), BF16),
                pltpu.VMEM((width, 3 * half), F32),
                pltpu.VMEM((half, width), F32),
            ],
        ),
        out_shape=[
            jax.ShapeDtypeStruct((tokens, width), BF16),
            jax.ShapeDtypeStruct((width, 2 * width), BF16),
        ],
        compiler_params=pltpu.CompilerParams(vmem_limit_bytes=48 * 1024 * 1024),
        cost_estimate=pl.CostEstimate(
            flops=22 * tokens * width * width // 2,
            bytes_accessed=20 * 1024 * 1024,
            transcendentals=tokens * BLOCK * half // SIZE,
        ),
    )(core, embedded, context, cot, qkv_weight, qkv_weight, qkv_weight, out_weight)


def merge_kernel(core_ref, ids_ref, cot_ref, mine_ref, other_ref, d_table_ref, d_ctx_ref, acc):
    step = pl.program_id(0)
    d_flat = (mine_ref[...].astype(F32) + other_ref[...].astype(F32)).astype(BF16)
    d_stream = (cot_ref[...].astype(F32) + d_flat.astype(F32)).astype(BF16)
    rows, width = d_stream.shape
    d_ctx = jnp.sum(d_stream.astype(F32).reshape(rows // BOOKS, BOOKS, width), axis=1)
    d_ctx_ref[...] = d_ctx.astype(BF16)
    place = lax.broadcasted_iota(jnp.int32, (acc.shape[0], rows), 0)
    row = place // 16 * 32 + core_ref[0] * 16 + place % 16
    onehot = jnp.where(row == ids_ref[...], F32(1.0), F32(0.0)).astype(BF16)
    part = dot(onehot, d_stream, 1, 0)

    @pl.when(step == 0)
    def _():
        acc[...] = part

    @pl.when(step > 0)
    def _():
        acc[...] += part

    @pl.when(step == pl.num_programs(0) - 1)
    def _():
        d_table_ref[...] = acc[...].astype(BF16)


def merge(core, ids, cot, mine, other, vocab):
    tokens, width = cot.shape
    steps = 4
    rows = tokens // steps
    spec = pl.BlockSpec((rows, width), lambda i, c: (i, 0))
    return pl.pallas_call(
        merge_kernel,
        grid_spec=pltpu.PrefetchScalarGridSpec(
            num_scalar_prefetch=1,
            grid=(steps,),
            in_specs=[
                pl.BlockSpec((1, rows), lambda i, c: (0, i)),
                spec,
                spec,
                pl.BlockSpec((rows, width), lambda i, c: ((i + steps // 2) % steps, 0)),
            ],
            out_specs=[
                pl.BlockSpec((vocab // 2, width), lambda i, c: (0, 0)),
                pl.BlockSpec((rows // BOOKS, width), lambda i, c: (i, 0)),
            ],
            scratch_shapes=[pltpu.VMEM((vocab // 2, width), F32)],
        ),
        out_shape=[
            jax.ShapeDtypeStruct((vocab // 2, width), BF16),
            jax.ShapeDtypeStruct((tokens // BOOKS, width), BF16),
        ],
        compiler_params=pltpu.CompilerParams(vmem_limit_bytes=32 * 1024 * 1024),
        cost_estimate=pl.CostEstimate(
            flops=tokens * width * vocab, bytes_accessed=9 * tokens * width, transcendentals=0
        ),
    )(core, ids, cot, mine, other)


def scatter_sum(parts, axes):
    got = lax.all_to_all(parts, axes, 0, 0, tiled=False)
    return jnp.sum(got.astype(F32), axis=0)


def on_device(hidden, ctx_weight, codes, table, qkv_weight, out_weight, cotangent):
    core = lax.axis_index("c")
    yh = lax.axis_index("yh")
    width = ctx_weight.shape[1]
    half = width // 2
    frames = codes.shape[0]
    tokens = 2 * frames * BOOKS
    vocab = table.shape[0]

    swap = functools.partial(lax.ppermute, axis_name="c", perm=SWAP)
    ids = jnp.concatenate([codes, swap(codes)], axis=0).reshape(tokens)
    cot = cotangent.reshape(frames * BOOKS, width)
    cot = jnp.concatenate([cot, swap(cot)], axis=0)

    partial_ctx = dot(hidden, ctx_weight, 1, 0).astype(BF16).reshape(2, 2 * frames, width)
    away = lax.dynamic_index_in_dim(partial_ctx, 1 - yh, 0, keepdims=False)
    near = lax.dynamic_index_in_dim(partial_ctx, yh, 0, keepdims=False)
    chip_ctx = (near.astype(F32) + lax.ppermute(away, "yh", SWAP).astype(F32)).astype(BF16)
    context = (chip_ctx.astype(F32) + swap(chip_ctx).astype(F32)).astype(BF16)
    context = jnp.where(core == 0, context, jnp.roll(context, frames, axis=0))

    onehot = (ids[:, None] == jnp.arange(vocab, dtype=jnp.int32)[None, :]).astype(BF16)
    embedded = dot(onehot, table, 1, 0).astype(BF16)
    which = core.astype(jnp.int32).reshape(1)
    d_flat, grads = block(which, embedded, context, cot, qkv_weight, out_weight)
    d_table, d_ctx = merge(which, ids.reshape(1, tokens), cot, d_flat, swap(d_flat), vocab)
    d_ctx = jnp.where(core == 0, d_ctx, jnp.roll(d_ctx, frames, axis=0))
    d_ctx_far = lax.ppermute(d_ctx, "yh", SWAP)
    d_ctx = jnp.where(
        yh == 0,
        jnp.concatenate([d_ctx, d_ctx_far], axis=0),
        jnp.concatenate([d_ctx_far, d_ctx], axis=0),
    )

    chips = 64
    sums = scatter_sum(grads.reshape(chips, 16, 2 * width), CHIPS)
    sum_out = jnp.concatenate([sums[:8, 3 * half :], sums[8:, 3 * half :]], axis=1)
    grad_out = lax.ppermute(
        sum_out, ("z", "c"), [(2 * z + c, 2 * (2 * c + z % 2) + z // 2) for z in range(4) for c in range(2)]
    )
    sum_qkv = sums[:, : 3 * half]
    keep = lax.dynamic_slice_in_dim(sum_qkv, core * 8, 8, 0)
    give = lax.dynamic_slice_in_dim(sum_qkv, 8 - core * 8, 8, 0)
    take = swap(give)
    keep, take = keep.reshape(8, 3, 1, half), take.reshape(8, 3, 1, half)
    grad_qkv = jnp.where(
        core == 0, jnp.concatenate([keep, take], axis=2), jnp.concatenate([take, keep], axis=2)
    ).reshape(8, 6 * half)

    grad_table = scatter_sum(d_table.reshape(chips, 16, width), CHIPS)

    d_hidden = dot(d_ctx, ctx_weight, 1, 1).astype(BF16)
    ctx_part = dot(hidden, d_ctx, 0, 0).astype(BF16)
    ctx_sum = scatter_sum(ctx_part.reshape(32, 32, width), SEQ).astype(BF16)
    grad_ctx = lax.all_to_all(
        jnp.broadcast_to(ctx_sum[None], (32, 32, width)), SEQ, 0, 0, tiled=False
    ).reshape(32 * 32, width).astype(F32)
    return (d_hidden, grad_ctx, grad_table, grad_qkv, grad_out)


def solution(mesh):
    fine = Mesh(mesh.devices.reshape(4, 2, 4, 2, 2), ALL)
    in_specs = (
        P(SEQ, ("yh", "c")),
        P(("yh", "c"), None),
        P(ALL, None),
        P(),
        P(),
        P(),
        P(ALL, None, None),
    )
    out_specs = (
        P(SEQ, ("yh", "c")),
        P(("yh", "c"), None),
        P(ALL, None),
        P(ALL, None),
        P(ALL, None),
    )
    return jax.shard_map(
        on_device, mesh=fine, in_specs=in_specs, out_specs=out_specs, check_vma=False
    )
```

time: 257 us -> 243 us (0.946)
  blocking collectives: 0 us -> 35.2 us
  matrix products: 40.5 us -> 12.5 us
  waiting for transfers between devices: 106 us -> 82.6 us
  Pallas kernels: 19.5 us -> 39.6 us
  starting transfers between devices: 55.1 us -> 43.7 us
  local copies, waits for them, and re-layouts: 18 us -> 10.7 us
    all_to_all x0 -> x1, blocking collectives: none -> 35.2 us  [scatter_sum(): got = lax.all_to_all(parts, axes, 0, 0, tiled=False)]
    all_to_all x4 -> x2, waiting for transfers between devices: 55.9 us -> 26.5 us  [scatter_sum(): got = lax.all_to_all(parts, axes, 0, 0, tiled=False)]
    dot_general x10 -> x4, matrix products: 40.5 us -> 12.5 us  [dot(): lax.dot_general(a, b, (((ca,), (cb,)), ((), ())), preferred_element_type=...]
    pallas_call x2, Pallas kernels: 19.5 us -> 39.6 us  [the longest x1 31.5 us: block(): pl.pallas_call(block_kernel, grid_spec=pltpu.PrefetchScalarGridSpec(num_s...]
    all_to_all x4 -> x2, starting transfers between devices: 35.7 us -> 22.3 us  [scatter_sum(): got = lax.all_to_all(parts, axes, 0, 0, tiled=False)]
    ppermute x1, waiting for transfers between devices: 16.9 us -> 8.64 us  [on_device(): lax.ppermute(sum_out, ('z', 'c'), [(2 * z + c, 2 * (2 * c + z % 2) + z //...]
    ppermute x1, waiting for transfers between devices: 0.01 us -> 4.09 us  [on_device(): swap(d_flat)]
    dynamic_slice x1 -> x0, local copies, waits for them, and re-layouts: 3.86 us -> none  [on_device(): lax.dynamic_index_in_dim(qkv_weight.reshape(width, 3, 2, half), core, 2,...]
  transfers between devices with their start and end apart: 13 -> 11, of which waited for: 5 -> 7; matrix products, arithmetic and copies ran while one was open for 22% -> 9% of each run, Pallas kernels for 2% -> 3%
where the time goes in v2:
time: 243 us; the launch traced here: 241 us
  waiting for transfers between devices  82.6 us (34%)
  starting transfers between devices  43.7 us (18%)
  Pallas kernels  39.6 us (16%)
  blocking collectives  35.2 us (14%)
  other arithmetic  15.6 us (6%)
  matrix products  12.5 us (5%)
  local copies, waits for them, and re-layouts  10.7 us (4%)
    ppermute x1, waiting for transfers between devices, on_device(): d_ctx_far = lax.ppermute(d_ctx, 'yh', SWAP)  36.3 us
    all_to_all x1, blocking collectives, scatter_sum(): got = lax.all_to_all(parts, axes, 0, 0, tiled=False)  35.2 us
    pallas_call x1, Pallas kernels, block(): pl.pallas_call(block_kernel, grid_spec=pltpu.PrefetchScalarGridSpec(num_s...  31.5 us
    all_to_all x2, waiting for transfers between devices, scatter_sum(): got = lax.all_to_all(parts, axes, 0, 0, tiled=False)  26.5 us
    all_to_all x2, starting transfers between devices, scatter_sum(): got = lax.all_to_all(parts, axes, 0, 0, tiled=False)  22.3 us
    dot_general x4, matrix products, dot(): lax.dot_general(a, b, (((ca,), (cb,)), ((), ())), preferred_element_type=...  12.5 us
    ppermute x1, waiting for transfers between devices, on_device(): lax.ppermute(sum_out, ('z', 'c'), [(2 * z + c, 2 * (2 * c + z % 2) + z //...  8.64 us
    pallas_call x1, Pallas kernels, merge(): pl.pallas_call(merge_kernel, grid_spec=pltpu.PrefetchScalarGridSpec(num_s...  8.11 us
  transfers between devices with their start and end apart: 11, of which 7 were waited for; matrix products, arithmetic and copies ran while one was open for 9% of the time, Pallas kernels for 3%

profile of v2, /device:TPU:1, one launch (start us, length us, event | category | flops | bytes accessed | tf_op | source)
XLA Modules:
  0.0 240.8 jit_solution(1130062018073266368)
XLA Ops:
  0.6 0.0 copy-start
  0.6 0.0 copy-start.7
  0.7 0.0 copy-start.5
  0.7 1.6 copy-done
  2.2 1.7 convolution_convert_fusion.2
  4.0 0.0 copy-start.6
  4.0 3.8 %collective-permute-start.2 = (bf16[128,1024]{1,0:T(8,128)(2,1)S(1)}, bf16[128,1024]{1,0:T(8,128)(2,1)}, u32[]{:S(2)}, u32[]{:S(2)}) collective-permute-start(bf16[128,1024]{1,0:T(8,128)(2,1)S(1)} %dynamic-slice_bitcast_fusion), channel_id=1, source_target_pairs={{0,2},{2,0},{1,3},{3,1},{4,6},{6,4},{5,7},{7,5},{8,10},{10,8},{9,1... | collective-permute-start | bytes 786440 | tf_op jit(solution)/shard_map/ppermute | solution.py:233
  7.9 0.0 copy-done.7
  7.9 1.0 collective-permute-start
  8.8 0.0 copy-done.6
  8.8 0.0 copy-done.5
  8.8 0.1 collective-permute-start.1
  8.9 0.7 collective-permute-done
  9.6 0.1 pad_add_fusion
  9.7 0.1 copy.14
  9.8 0.1 eq.25
  9.9 3.8 %collective-permute-done.2 = bf16[128,1024]{1,0:T(8,128)(2,1)} collective-permute-done((bf16[128,1024]{1,0:T(8,128)(2,1)S(1)}, bf16[128,1024]{1,0:T(8,128)(2,1)}, u32[]{:S(2)}, u32[]{:S(2)}) %collective-permute-start.2) | collective-permute-done | bytes 262176 | tf_op jit(solution)/shard_map/ppermute | solution.py:233
  13.7 1.1 fusion.3
  14.8 1.6 collective-permute-start.3
  16.4 7.1 %fusion.2.emb_ref = bf16[1024,1024]{1,0:T(8,128)(2,1)S(1)} fusion(bf16[2048,1024]{1,0:T(8,128)(2,1)} %param.10, s32[1024]{0:T(1024)S(1)} %eq.25), kind=kOutput, calls=%fused_computation.7 | convolution fusion | flops 4298113024 | bytes 6295552 | tf_op jit(solution)/shard_map/dot_general | solution.py:25
  23.5 0.0 collective-permute-done.3
  23.5 0.1 add_convert_fusion
  23.6 0.1 maximum_select_fusion.1.ctx_ref
  23.7 0.0 collective-permute-done.1
  23.7 2.8 %pad_maximum_fusion.cot_ref = bf16[1024,1024]{1,0:T(8,128)(2,1)} fusion(bf16[512,1024]{1,0:T(8,128)(2,1)} %collective-permute-done.1, bf16[512,1024]{1,0:T(8,128)(2,1)S(1)} %bitcast.28), kind=kLoop, calls=%fused_computation.5 | loop fusion | flops 4194304 | bytes 4194304 | tf_op jit(solution)/shard_map/concatenate | solution.py:228
  26.4 31.5 %shard_map.110 = (bf16[1024,1024]{1,0:T(8,128)(2,1)S(1)}, bf16[1024,2048]{1,0:T(8,128)(2,1)}) custom-call(s32[1]{0:T(128)} %bitcast.core_ref, bf16[1024,1024]{1,0:T(8,128)(2,1)S(1)} %fusion.2.emb_ref, bf16[128,1024]{1,0:T(8,128)(2,1)S(1)} %maximum_select_fusion.1.ctx_ref, bf16[1024,1024]{1,0:T(8,128)(2,1)} %pad_maximum_fusion.cot_ref, ...), custom_call_target="tpu_custom_call" | custom-call | flops 11811160064 | bytes 20971520 | tf_op jit(solution)/shard_map/pallas_call | solution.py:116
  57.9 0.0 copy-start.3
  57.9 1.4 copy-done.3
  59.3 11.4 %all-to-all-start.3 = ((bf16[64,16,2048]{2,1,0:T(8,128)(2,1)}), bf16[64,16,2048]{2,1,0:T(8,128)(2,1)}, u32[]{:S(2)}, u32[]{:S(2)}) async-start(bf16[64,16,2048]{2,1,0:T(8,128)(2,1)} %bitcast.25), calls=%async_computation.3 | async-start | bytes 8388608 | tf_op jit(solution)/shard_map/all_to_all | solution.py:212
  70.7 0.4 collective-permute-start.4
  71.1 0.1 reshape_reshape.3.ids_ref
  71.2 4.1 %collective-permute-done.4.other_ref = bf16[1024,1024]{1,0:T(8,128)(2,1)} collective-permute-done((bf16[1024,1024]{1,0:T(8,128)(2,1)}, bf16[1024,1024]{1,0:T(8,128)(2,1)}, u32[]{:S(2)}, u32[]{:S(2)}) %collective-permute-start.4) | collective-permute-done | bytes 2097184 | tf_op jit(solution)/shard_map/ppermute | solution.py:241
  75.3 0.0 copy-start.2
  75.3 1.6 copy-done.2
  76.9 0.0 copy-start.4
  76.9 1.6 copy-done.4
  78.5 0.0 copy-start.8
  78.5 8.1 %shard_map.111 = (bf16[1024,1024]{1,0:T(8,128)(2,1)S(1)}, bf16[128,1024]{1,0:T(8,128)(2,1)S(1)}) custom-call(s32[1]{0:T(128)} %bitcast.core_ref, s32[1,1024]{1,0:T(1,128)S(1)} %reshape_reshape.3.ids_ref, bf16[1024,1024]{1,0:T(8,128)(2,1)S(1)} %copy-done.2, bf16[1024,1024]{1,0:T(8,128)(2,1)S(1)} %copy-done.4, bf16[1024,1024]{1,0:T(8,128)(2,1)} %collective-permute-done.4.other_ref), custom_call_target="tpu_custom_call" | custom-call | flops 2147483648 | bytes 9437184 | tf_op jit(solution)/shard_map/pallas_call | solution.py:183
  86.6 0.0 copy-start.1
  86.6 1.3 copy-done.1
  88.0 0.1 maximum_select_fusion.2
  88.1 2.7 %collective-permute-start.5 = (bf16[128,1024]{1,0:T(8,128)(2,1)S(1)}, bf16[128,1024]{1,0:T(8,128)(2,1)S(1)}, u32[]{:S(2)}, u32[]{:S(2)}) collective-permute-start(bf16[128,1024]{1,0:T(8,128)(2,1)S(1)} %maximum_select_fusion.2), channel_id=1, source_target_pairs={{0,2},{2,0},{1,3},{3,1},{4,6},{6,4},{5,7},{7,5},{8,10},{10,8},{9,1... | collective-permute-start | bytes 786440 | tf_op jit(solution)/shard_map/ppermute | solution.py:243
  90.8 36.3 %collective-permute-done.5 = bf16[128,1024]{1,0:T(8,128)(2,1)S(1)} collective-permute-done((bf16[128,1024]{1,0:T(8,128)(2,1)S(1)}, bf16[128,1024]{1,0:T(8,128)(2,1)S(1)}, u32[]{:S(2)}, u32[]{:S(2)}) %collective-permute-start.5) | collective-permute-done | bytes 262176 | tf_op jit(solution)/shard_map/ppermute | solution.py:243
  127.1 0.0 copy-done.8
  127.1 2.1 convolution_convert_fusion
  129.2 0.0 all-to-all-done.3
  129.2 35.2 %all_to_all.20 = bf16[32,32,1024]{2,1,0:T(8,128)(2,1)} all-to-all(bf16[32,32,1024]{2,1,0:T(8,128)(2,1)} %bitcast.26), channel_id=1, replica_groups=mesh['z'=4,'yl'=2,'x'=4,'yh'=2,'c'=2] {'z','yl','x'}, dimensions={0} | all-to-all | bytes 4194304 | tf_op jit(solution)/shard_map/all_to_all | solution.py:212
  164.4 10.9 %all-to-all-start.2 = ((bf16[64,16,1024]{2,1,0:T(8,128)(2,1)}), bf16[64,16,1024]{2,1,0:T(8,128)(2,1)}, u32[]{:S(2)}, u32[]{:S(2)}) async-start(bf16[64,16,1024]{2,1,0:T(8,128)(2,1)} %bitcast.24), calls=%async_computation.2 | async-start | bytes 4194304 | tf_op jit(solution)/shard_map/all_to_all | solution.py:212
  175.3 2.0 reduce_sum.30
  177.3 26.5 %all-to-all-done.2 = bf16[64,16,1024]{2,1,0:T(8,128)(2,1)} async-done(((bf16[64,16,1024]{2,1,0:T(8,128)(2,1)}), bf16[64,16,1024]{2,1,0:T(8,128)(2,1)}, u32[]{:S(2)}, u32[]{:S(2)}) %all-to-all-start.2) | async-done | bytes 2097184 | tf_op jit(solution)/shard_map/all_to_all | solution.py:212
  203.7 1.6 broadcast_in_dim.2
  205.3 4.8 %all-to-all-start.1 = ((bf16[32,32,1024]{2,1,0:T(8,128)(2,1)}), bf16[32,32,1024]{2,1,0:T(8,128)(2,1)}, u32[]{:S(2)}, u32[]{:S(2)}) async-start(bf16[32,32,1024]{2,1,0:T(8,128)(2,1)} %broadcast_in_dim.2), calls=%async_computation.1 | async-start | bytes 4194304 | tf_op jit(solution)/shard_map/all_to_all | solution.py:270
  210.1 1.6 convolution_convert_fusion.1
  211.6 2.9 %convert_reduce_fusion = f32[16,2048]{1,0:T(8,128)S(1)} fusion(bf16[64,16,2048]{2,1,0:T(8,128)(2,1)} %all-to-all-done.3), kind=kLoop, calls=%fused_computation | loop fusion | flops 4161536 | bytes 4325376 | tf_op jit(solution)/shard_map/reduce_sum | solution.py:213
  214.6 7.0 %collective-permute-start.7 = (f32[8,1024]{1,0:T(8,128)S(1)}, f32[8,1024]{1,0:T(8,128)S(1)}, u32[]{:S(2)}, u32[]{:S(2)}) collective-permute-start(f32[8,1024]{1,0:T(8,128)S(1)} %pad_maximum_fusion.1), channel_id=1, source_target_pairs={{0,0},{1,64},{32,32},{33,96},{64,1},{65,65},{96,33},{97,97},{2,2},... | collective-permute-start | bytes 98312 | tf_op jit(solution)/shard_map/ppermute | solution.py:253
  221.6 0.1 collective-permute-start.6
  221.6 2.6 %convert_reduce_fusion.1 = f32[16,1024]{1,0:T(8,128)} fusion(bf16[64,16,1024]{2,1,0:T(8,128)(2,1)} %all-to-all-done.2), kind=kLoop, calls=%fused_computation.3 | loop fusion | flops 2080768 | bytes 2162688 | tf_op jit(solution)/shard_map/reduce_sum | solution.py:213
  224.2 8.6 %collective-permute-done.7 = f32[8,1024]{1,0:T(8,128)S(1)} collective-permute-done((f32[8,1024]{1,0:T(8,128)S(1)}, f32[8,1024]{1,0:T(8,128)S(1)}, u32[]{:S(2)}, u32[]{:S(2)}) %collective-permute-start.7) | collective-permute-done | bytes 32800 | tf_op jit(solution)/shard_map/ppermute | solution.py:253
  232.9 0.0 collective-permute-done.6
  232.9 0.6 copy.16
  233.5 2.6 %all-to-all-done.1 = bf16[32,32,1024]{2,1,0:T(8,128)(2,1)} async-done(((bf16[32,32,1024]{2,1,0:T(8,128)(2,1)}), bf16[32,32,1024]{2,1,0:T(8,128)(2,1)}, u32[]{:S(2)}, u32[]{:S(2)}) %all-to-all-start.1) | async-done | bytes 2097184 | tf_op jit(solution)/shard_map/all_to_all | solution.py:270
  236.1 4.1 %bitcast_convert_fusion = f32[1024,1024]{1,0:T(8,128)} fusion(bf16[32,32,1024]{2,1,0:T(8,128)(2,1)} %all-to-all-done.1), kind=kLoop, calls=%fused_computation.6 | loop fusion | flops 1048576 | bytes 6291456 | tf_op jit(solution)/shard_map/convert_element_type | solution.py:272
  240.2 0.6 copy.18
  (8 shorter events, 0.1 us)
Async XLA Ops:
  0.6 1.6 copy-start
  0.6 7.2 %copy-start.7 = (s32[64,8]{0,1:T(8,128)S(1)}, s32[64,8]{0,1:T(8,128)}, u32[]{:S(2)}) copy-start(s32[64,8]{0,1:T(8,128)} %param.9) | copy-start | bytes 6148
  0.7 8.2 %copy-start.5 = (bf16[64,8,1024]{2,1,0:T(8,128)(2,1)S(1)}, bf16[64,8,1024]{2,1,0:T(8,128)(2,1)}, u32[]{:S(2)}) copy-start(bf16[64,8,1024]{2,1,0:T(8,128)(2,1)} %param.13) | copy-start | bytes 3145732
  4.0 4.8 %copy-start.6 = (bf16[256,1024]{1,0:T(8,128)(2,1)}, bf16[256,1024]{1,0:T(8,128)(2,1)S(1)}, u32[]{:S(2)}) copy-start(bf16[256,1024]{1,0:T(8,128)(2,1)S(1)} %convolution_convert_fusion.2) | copy-start | bytes 1572868
  4.0 9.7 %collective-permute-start.2 = (bf16[128,1024]{1,0:T(8,128)(2,1)S(1)}, bf16[128,1024]{1,0:T(8,128)(2,1)}, u32[]{:S(2)}, u32[]{:S(2)}) collective-permute-start(bf16[128,1024]{1,0:T(8,128)(2,1)S(1)} %dynamic-slice_bitcast_fusion), channel_id=1, source_target_pairs={{0,2},{2,0},{1,3},{3,1},{4,6},{6,4},{5,7},{7,5},{8,10},{10,8},{9,1... | collective-permute-start | bytes 786440 | tf_op jit(solution)/shard_map/ppermute | solution.py:233
  7.9 1.8 collective-permute-start
  8.8 14.9 %collective-permute-start.1 = (bf16[512,1024]{1,0:T(8,128)(2,1)S(1)}, bf16[512,1024]{1,0:T(8,128)(2,1)}, u32[]{:S(2)}, u32[]{:S(2)}) collective-permute-start(bf16[512,1024]{1,0:T(8,128)(2,1)S(1)} %bitcast.27), channel_id=1, source_target_pairs={{0,1},{1,0},{2,3},{3,2},{4,5},{5,4},{6,7},{7,6},{8,9},{9,8},{10,11... | collective-permute-start | bytes 3145736 | tf_op jit(solution)/shard_map/ppermute | solution.py:228
  14.8 8.7 %collective-permute-start.3 = (bf16[128,1024]{1,0:T(8,128)(2,1)S(1)}, bf16[128,1024]{1,0:T(8,128)(2,1)S(1)}, u32[]{:S(2)}, u32[]{:S(2)}) collective-permute-start(bf16[128,1024]{1,0:T(8,128)(2,1)S(1)} %fusion.3), channel_id=1, source_target_pairs={{0,1},{1,0},{2,3},{3,2},{4,5},{5,4},{6,7},{7,6},{8,9},{9,8},{10,11... | collective-permute-start | bytes 786440 | tf_op jit(solution)/shard_map/ppermute | solution.py:234
  57.9 1.4 copy-start.3
  59.3 70.0 %all-to-all-start.3 = ((bf16[64,16,2048]{2,1,0:T(8,128)(2,1)}), bf16[64,16,2048]{2,1,0:T(8,128)(2,1)}, u32[]{:S(2)}, u32[]{:S(2)}) async-start(bf16[64,16,2048]{2,1,0:T(8,128)(2,1)} %bitcast.25), calls=%async_computation.3 | async-start | bytes 8388608 | tf_op jit(solution)/shard_map/all_to_all | solution.py:212
  70.7 4.6 %collective-permute-start.4 = (bf16[1024,1024]{1,0:T(8,128)(2,1)}, bf16[1024,1024]{1,0:T(8,128)(2,1)}, u32[]{:S(2)}, u32[]{:S(2)}) collective-permute-start(bf16[1024,1024]{1,0:T(8,128)(2,1)} %copy-done.3), channel_id=1, source_target_pairs={{0,1},{1,0},{2,3},{3,2},{4,5},{5,4},{6,7},{7,6},{8,9},{9,8},{10,11... | collective-permute-start | bytes 6291464 | tf_op jit(solution)/shard_map/ppermute | solution.py:241
  75.3 1.6 copy-start.2
  76.9 1.6 copy-start.4
  78.5 48.6 %copy-start.8 = (bf16[256,1024]{1,0:T(8,128)(2,1)S(1)}, bf16[256,1024]{1,0:T(8,128)(2,1)}, u32[]{:S(2)}) copy-start(bf16[256,1024]{1,0:T(8,128)(2,1)} %param.7) | copy-start | bytes 1572868
  86.6 1.4 copy-start.1
  88.1 39.0 %collective-permute-start.5 = (bf16[128,1024]{1,0:T(8,128)(2,1)S(1)}, bf16[128,1024]{1,0:T(8,128)(2,1)S(1)}, u32[]{:S(2)}, u32[]{:S(2)}) collective-permute-start(bf16[128,1024]{1,0:T(8,128)(2,1)S(1)} %maximum_select_fusion.2), channel_id=1, source_target_pairs={{0,2},{2,0},{1,3},{3,1},{4,6},{6,4},{5,7},{7,5},{8,10},{10,8},{9,1... | collective-permute-start | bytes 786440 | tf_op jit(solution)/shard_map/ppermute | solution.py:243
  164.4 39.3 %all-to-all-start.2 = ((bf16[64,16,1024]{2,1,0:T(8,128)(2,1)}), bf16[64,16,1024]{2,1,0:T(8,128)(2,1)}, u32[]{:S(2)}, u32[]{:S(2)}) async-start(bf16[64,16,1024]{2,1,0:T(8,128)(2,1)} %bitcast.24), calls=%async_computation.2 | async-start | bytes 4194304 | tf_op jit(solution)/shard_map/all_to_all | solution.py:212
  205.3 30.8 %all-to-all-start.1 = ((bf16[32,32,1024]{2,1,0:T(8,128)(2,1)}), bf16[32,32,1024]{2,1,0:T(8,128)(2,1)}, u32[]{:S(2)}, u32[]{:S(2)}) async-start(bf16[32,32,1024]{2,1,0:T(8,128)(2,1)} %broadcast_in_dim.2), calls=%async_computation.1 | async-start | bytes 4194304 | tf_op jit(solution)/shard_map/all_to_all | solution.py:270
  214.6 18.3 %collective-permute-start.7 = (f32[8,1024]{1,0:T(8,128)S(1)}, f32[8,1024]{1,0:T(8,128)S(1)}, u32[]{:S(2)}, u32[]{:S(2)}) collective-permute-start(f32[8,1024]{1,0:T(8,128)S(1)} %pad_maximum_fusion.1), channel_id=1, source_target_pairs={{0,0},{1,64},{32,32},{33,96},{64,1},{65,65},{96,33},{97,97},{2,2},... | collective-permute-start | bytes 98312 | tf_op jit(solution)/shard_map/ppermute | solution.py:253
  221.6 11.3 %collective-permute-start.6 = (f32[8,1536]{1,0:T(8,128)S(1)}, f32[8,1536]{1,0:T(8,128)S(1)}, u32[]{:S(2)}, u32[]{:S(2)}) collective-permute-start(f32[8,1536]{1,0:T(8,128)S(1)} %get-tuple-element.20), channel_id=1, source_target_pairs={{0,1},{1,0},{2,3},{3,2},{4,5},{5,4},{6,7},{7,6},{8,9},{9,8},{10,11... | collective-permute-start | bytes 147464 | tf_op jit(solution)/shard_map/ppermute | solution.py:259

commit v3 on v2

v3 whole, which is shorter than its diff:
```python
import functools

import jax
import jax.numpy as jnp
from jax import lax
from jax.experimental import pallas as pl
from jax.experimental.pallas import tpu as pltpu
from jax.sharding import Mesh, PartitionSpec as P

HEADS = 16
BOOKS = 8
SIZE = 64
LANES = 128
BLOCK = 128

ALL = ("z", "yl", "x", "yh", "c")
SEQ = ("z", "yl", "x")
SWAP = [(0, 1), (1, 0)]

CHIPS = (("z", 4), ("yl", 2), ("x", 4), ("yh", 2))
RINGS = {"x": ("x",), "y": ("yl", "yh"), "z": ("z",)}
RING_ORDER = ("x", "y", "z")
F32 = jnp.float32
BF16 = jnp.bfloat16


def dot(a, b, ca, cb):
    return lax.dot_general(a, b, (((ca,), (cb,)), ((), ())), preferred_element_type=F32)


def attend(query, keys, values, d_mixed):
    row = lax.broadcasted_iota(jnp.int32, (2 * BLOCK, BLOCK), 0) % BLOCK
    col = lax.broadcasted_iota(jnp.int32, (2 * BLOCK, BLOCK), 1)
    visible = (row // BOOKS == col // BOOKS) & (col <= row)
    low = lax.broadcasted_iota(jnp.int32, (BLOCK, LANES), 1) < SIZE

    def stack(a):
        zero = jnp.zeros_like(a)
        return jnp.concatenate([jnp.where(low, a, zero), jnp.where(low, zero, a)], axis=0)

    def pick(a):
        return jnp.where(low, a[:BLOCK], a[BLOCK:]).astype(BF16)

    query, d_mixed = stack(query), stack(d_mixed)
    scores = dot(query, keys, 1, 1) * F32(0.125)
    weights = jnp.where(visible, jnp.exp(scores), F32(0.0))
    exact = weights * (F32(1.0) / jnp.sum(weights, axis=1, keepdims=True))
    probs = exact.astype(BF16)
    mixed = pick(dot(probs, values, 1, 0))
    d_probs = dot(d_mixed, values, 1, 1).astype(BF16).astype(F32)
    inner = jnp.sum(d_probs * exact, axis=1, keepdims=True)
    d_scores = (exact * (d_probs - inner) * F32(0.125)).astype(BF16)
    d_query = pick(dot(d_scores, keys, 1, 0))
    d_keys = dot(d_scores, query, 0, 0).astype(BF16)
    d_values = dot(probs, d_mixed, 0, 0).astype(BF16)
    return mixed, d_query, d_keys, d_values


def ring_place(axis):
    if axis == "y":
        return 2 * lax.axis_index("yh") + lax.axis_index("yl")
    return lax.axis_index(axis)


def ring_parts(axis):
    core, place = lax.axis_index("c"), ring_place(axis)
    first = jnp.where(core == 0, place ^ 1, 3 - place)
    second = jnp.where(core == 0, 3 - place, place ^ 1)
    return (first, place ^ 2, place, second)


def ring_pairs(axis, step):
    def index(place, core):
        if axis == "y":
            place = place % 2 * 2 + place // 2
        return 2 * place + core

    return [
        (index(p, c), index(p ^ 1 if c == step else 3 - p, c)) for p in range(4) for c in range(2)
    ]


def ring_shift(axis, shift):
    def index(place):
        return place % 2 * 2 + place // 2 if axis == "y" else place

    return [(index(p), index((p + shift) % 4)) for p in range(4)]


def ring_base(axis, place):
    if axis == "x":
        return place * 2
    if axis == "y":
        return place % 2 * 8 + place // 2
    return place * 16


def ring_rest(axis):
    if axis == "x":
        return [16 * z + 8 * yl + yh for z in range(4) for yl in range(2) for yh in range(2)]
    if axis == "y":
        return [16 * z + 2 * x for z in range(4) for x in range(4)]
    return list(range(16))


def positions():
    out = [lax.axis_index("c")]
    for axis in RING_ORDER:
        out += [ring_base(axis, place) for place in ring_parts(axis)]
    return jnp.stack(out).astype(jnp.int32)


def write_parts(at_ref, axis, give, keep, read):
    for part in range(4):
        out = give if part < 2 else keep
        for rest, offset in enumerate(ring_rest(axis)):
            chip = at_ref[1 + 4 * RING_ORDER.index(axis) + part] + offset
            row = (part % 2 * 16 + rest) * 16
            out[row : row + 16, :] = read(chip).astype(BF16)


class Stream:
    def __init__(self, give, keep, order):
        self.order = order
        self.sizes = [1 if name in RINGS[order[0].lower()] else size for name, size in CHIPS]
        self.give, self.keep, self.got = give, keep, None
        self.step, self.total = 0, None

    def send(self):
        axis = self.order[0]
        if axis.islower():
            self.got = [lax.ppermute(self.give, RINGS[axis] + ("c",), ring_pairs(axis, self.step))]
        else:
            axis = axis.lower()
            self.got = [
                lax.ppermute(give, RINGS[axis], ring_shift(axis, shift))
                for give, shift in zip(self.give, (2, 1, 3))
            ]

    def add(self):
        got, keep = [g.astype(F32) for g in self.got], self.keep.astype(F32)
        if self.order[0].islower() and self.step == 0:
            half = keep.shape[0] // 2
            self.keep = (keep[:half] + got[0][:half]).astype(BF16)
            self.give = (keep[half:] + got[0][half:]).astype(BF16)
            self.step = 1
            return
        total = sum(got, keep)
        self.step, self.order = 0, self.order[1:]
        if not self.order:
            self.total = total
        else:
            self.begin(total.astype(BF16))

    def begin(self, data):
        self.data = data
        axis = self.order[0].lower()
        width = data.shape[1]
        data = data.reshape(*self.sizes, 16, width)

        def part(place):
            out = data
            for dim, (name, _) in enumerate(CHIPS):
                if name in RINGS[axis]:
                    at = {"yl": place % 2, "yh": place // 2}.get(name, place)
                    out = lax.dynamic_slice_in_dim(out, at, 1, dim)
            return out.reshape(-1, width)

        if self.order[0].islower():
            first, third, mine, second = ring_parts(axis)
            self.give = jnp.concatenate([part(first), part(third)], axis=0)
            self.keep = jnp.concatenate([part(mine), part(second)], axis=0)
        else:
            place = ring_place(axis)
            self.give = [part(place ^ 2), part((place + 1) % 4), part((place + 3) % 4)]
            self.keep = part(place)
        self.sizes = [
            1 if name in RINGS[axis] else size for size, (name, _) in zip(self.sizes, CHIPS)
        ]


def join(a, b):
    out = Stream(None, None, a.order)
    out.sizes = [size if name in RINGS[a.order.lower()] else 1 for name, size in CHIPS]
    out.begin(jnp.concatenate([a.data, b.data], axis=1))
    return out


def together(streams, *values):
    out = lax.optimization_barrier(([s.got for s in streams], values))
    for s, got in zip(streams, out[0]):
        s.got = got
    return out[1]


def block_kernel(
    at_ref, emb_ref, ctx_ref, own_ref, oth_ref, wq_ref, wk_ref, wv_ref, wo_ref,
    d_flat_ref, d_ctx_ref, give_x, keep_x, give_z, keep_z,
    proj, d_proj, d_mixed, mixed, acc_qkv, acc_out,
):
    step = pl.program_id(0)
    rows, width = emb_ref.shape
    half = wq_ref.shape[1]
    stream = (
        emb_ref[...].astype(F32).reshape(rows // BOOKS, BOOKS, width)
        + ctx_ref[...].astype(F32)[:, None, :]
    ).reshape(rows, width).astype(BF16)
    cot = jnp.where(step < pl.num_programs(0) // 2, own_ref[...], oth_ref[...])
    for part, w_ref in enumerate((wq_ref, wk_ref, wv_ref)):
        proj[:, part * half : (part + 1) * half] = dot(stream, w_ref[...], 1, 0).astype(BF16)
    d_mixed[...] = dot(cot, wo_ref[...], 1, 1).astype(BF16)
    for block in range(rows // BLOCK):
        at = slice(block * BLOCK, (block + 1) * BLOCK)
        for pair in range(half // LANES):
            q = slice(pair * LANES, (pair + 1) * LANES)
            k = slice(half + pair * LANES, half + (pair + 1) * LANES)
            v = slice(2 * half + pair * LANES, 2 * half + (pair + 1) * LANES)
            mixed[at, q], d_proj[at, q], d_proj[at, k], d_proj[at, v] = attend(
                proj[at, q], proj[at, k], proj[at, v], d_mixed[at, q]
            )
    d_flat = dot(d_proj[:, :half], wq_ref[...], 1, 1)
    d_flat += dot(d_proj[:, half : 2 * half], wk_ref[...], 1, 1)
    d_flat += dot(d_proj[:, 2 * half :], wv_ref[...], 1, 1)
    d_flat_ref[...] = d_flat.astype(BF16)
    own = jnp.where(step < pl.num_programs(0) // 2, F32(1.0), F32(0.0))
    d_flat += cot.astype(F32) * own
    d_ctx_ref[...] = jnp.sum(d_flat.reshape(rows // BOOKS, BOOKS, width), axis=1).astype(BF16)

    @pl.when(step == 0)
    def _():
        acc_qkv[...] = dot(stream, d_proj[...], 0, 0)
        acc_out[...] = dot(mixed[...], cot, 0, 0)

    @pl.when(step > 0)
    def _():
        acc_qkv[...] += dot(stream, d_proj[...], 0, 0)
        acc_out[...] += dot(mixed[...], cot, 0, 0)

    @pl.when(step == pl.num_programs(0) - 1)
    def _():
        def qkv(chip, cols):
            return acc_qkv[pl.ds(pl.multiple_of(chip * 16, 16), 16), cols]

        def qk(chip):
            return qkv(chip, slice(0, 2 * half))

        def v_and_out(chip):
            start = pl.multiple_of((chip % 32 * 2 + chip // 32) * 8, 8)
            own = acc_out[pl.ds(start, 8), :]
            own = jnp.concatenate([own[:, :half], own[:, half:]], axis=0)
            return jnp.concatenate([qkv(chip, slice(2 * half, 3 * half)), own], axis=1)

        write_parts(at_ref, "x", give_x, keep_x, qk)
        write_parts(at_ref, "z", give_z, keep_z, v_and_out)


def halves(rows, width):
    last = 1
    return [
        pl.BlockSpec((rows, width), lambda i, *_: (jnp.minimum(i, last), 0)),
        pl.BlockSpec((rows, width), lambda i, *_: (jnp.maximum(i - last - 1, 0), 0)),
    ]


STEPS = 4


def block(at, embedded, context, own, oth, qkv_weight, out_weight):
    tokens, width = embedded.shape
    half = width // 2
    rows = tokens // STEPS
    tall = pl.BlockSpec((rows, width), lambda i, a: (i, 0))

    def third(part):
        return pl.BlockSpec((width, half), lambda i, a: (0, 2 * part + a[0]))

    out = (width // 2, width)
    return pl.pallas_call(
        block_kernel,
        grid_spec=pltpu.PrefetchScalarGridSpec(
            num_scalar_prefetch=1,
            grid=(STEPS,),
            in_specs=[
                tall,
                pl.BlockSpec((rows // BOOKS, width), lambda i, a: (i, 0)),
                *halves(rows, width),
                third(0),
                third(1),
                third(2),
                pl.BlockSpec((half, width), lambda i, a: (a[0], 0)),
            ],
            out_specs=[
                tall,
                pl.BlockSpec(
                    (rows // BOOKS, width), lambda i, a: ((i + STEPS // 2 * a[0]) % STEPS, 0)
                ),
            ]
            + [pl.BlockSpec(out, lambda i, a: (0, 0))] * 4,
            scratch_shapes=[
                pltpu.VMEM((rows, 3 * half), BF16),
                pltpu.VMEM((rows, 3 * half), BF16),
                pltpu.VMEM((rows, half), BF16),
                pltpu.VMEM((rows, half), BF16),
                pltpu.VMEM((width, 3 * half), F32),
                pltpu.VMEM((half, width), F32),
            ],
        ),
        out_shape=[
            jax.ShapeDtypeStruct((tokens, width), BF16),
            jax.ShapeDtypeStruct((tokens // BOOKS, width), BF16),
        ]
        + [jax.ShapeDtypeStruct(out, BF16)] * 4,
        compiler_params=pltpu.CompilerParams(vmem_limit_bytes=48 * 1024 * 1024),
        cost_estimate=pl.CostEstimate(
            flops=22 * tokens * width * width // 2,
            bytes_accessed=20 * 1024 * 1024,
            transcendentals=tokens * BLOCK * half // SIZE,
        ),
    )(at, embedded, context, own, oth, qkv_weight, qkv_weight, qkv_weight, out_weight)


def table_kernel(at_ref, ids_ref, own_ref, oth_ref, mine_ref, other_ref, d_table_ref, acc):
    step = pl.program_id(0)
    cot = jnp.where(step < pl.num_programs(0) // 2, own_ref[...], oth_ref[...])
    d_flat = (mine_ref[...].astype(F32) + other_ref[...].astype(F32)).astype(BF16)
    d_stream = (cot.astype(F32) + d_flat.astype(F32)).astype(BF16)
    place = lax.broadcasted_iota(jnp.int32, (acc.shape[0], d_stream.shape[0]), 0)
    row = place // 16 * 32 + at_ref[0] * 16 + place % 16
    onehot = jnp.where(row == ids_ref[...], F32(1.0), F32(0.0)).astype(BF16)
    part = dot(onehot, d_stream, 1, 0)

    @pl.when(step == 0)
    def _():
        acc[...] = part

    @pl.when(step > 0)
    def _():
        acc[...] += part

    @pl.when(step == pl.num_programs(0) - 1)
    def _():
        d_table_ref[...] = acc[...].astype(BF16)


def table_grad(at, ids, own, oth, mine, other, vocab):
    tokens, width = mine.shape
    rows = tokens // STEPS
    out = (vocab // 2, width)
    return pl.pallas_call(
        table_kernel,
        grid_spec=pltpu.PrefetchScalarGridSpec(
            num_scalar_prefetch=1,
            grid=(STEPS,),
            in_specs=[
                pl.BlockSpec((1, rows), lambda i, a: (0, i)),
                *halves(rows, width),
                pl.BlockSpec((rows, width), lambda i, a: (i, 0)),
                pl.BlockSpec((rows, width), lambda i, a: ((i + STEPS // 2) % STEPS, 0)),
            ],
            out_specs=pl.BlockSpec(out, lambda i, a: (0, 0)),
            scratch_shapes=[pltpu.VMEM(out, F32)],
        ),
        out_shape=jax.ShapeDtypeStruct(out, BF16),
        compiler_params=pltpu.CompilerParams(vmem_limit_bytes=32 * 1024 * 1024),
        cost_estimate=pl.CostEstimate(
            flops=tokens * width * vocab, bytes_accessed=9 * tokens * width, transcendentals=0
        ),
    )(at, ids, own, oth, mine, other)


def on_device(hidden, ctx_weight, codes, table, qkv_weight, out_weight, cotangent):
    core = lax.axis_index("c")
    yh = lax.axis_index("yh")
    width = ctx_weight.shape[1]
    half = width // 2
    frames = codes.shape[0]
    tokens = 2 * frames * BOOKS
    vocab = table.shape[0]
    at = positions()

    partial_ctx = dot(hidden, ctx_weight, 1, 0).astype(BF16).reshape(2, 2 * frames, width)
    away = lax.dynamic_index_in_dim(partial_ctx, 1 - yh, 0, keepdims=False)
    near = lax.dynamic_index_in_dim(partial_ctx, yh, 0, keepdims=False)
    far = lax.ppermute(away, "yh", SWAP)

    swap = functools.partial(lax.ppermute, axis_name="c", perm=SWAP)
    ids = jnp.concatenate([codes, swap(codes)], axis=0).reshape(tokens)
    own = cotangent.reshape(frames * BOOKS, width)
    oth = swap(own)
    onehot = (ids[:, None] == jnp.arange(vocab, dtype=jnp.int32)[None, :]).astype(BF16)
    embedded = dot(onehot, table, 1, 0).astype(BF16)

    far, embedded, oth = lax.optimization_barrier((far, embedded, oth))
    chip_ctx = (near.astype(F32) + far.astype(F32)).astype(BF16)
    context = (chip_ctx.astype(F32) + swap(chip_ctx).astype(F32)).astype(BF16)
    context = jnp.where(core == 0, context, jnp.roll(context, frames, axis=0))

    d_flat, d_ctx, give_x, keep_x, give_z, keep_z = block(
        at, embedded, context, own, oth, qkv_weight, out_weight
    )
    d_ctx = (d_ctx.astype(F32) + swap(d_ctx).astype(F32)).astype(BF16)
    d_ctx_far = lax.ppermute(d_ctx, "yh", SWAP)
    qk, vo = Stream(give_x, keep_x, "xzY"), Stream(give_z, keep_z, "zxY")
    for s in (qk, vo):
        s.send()
    other = swap(d_flat)
    d_ctx, d_ctx_far, other = together([qk, vo], d_ctx, d_ctx_far, other)

    d_ctx = jnp.where(
        yh == 0,
        jnp.concatenate([d_ctx, d_ctx_far], axis=0),
        jnp.concatenate([d_ctx_far, d_ctx], axis=0),
    )
    ctx_part = dot(hidden, d_ctx, 0, 0).astype(BF16)
    arrived = lax.all_to_all(ctx_part.reshape(32, 32, width), SEQ, 0, 0, tiled=False)
    for s in (qk, vo):
        s.add()
        s.send()
    d_table = table_grad(at, ids.reshape(1, tokens), own, oth, d_flat, other, vocab)
    arrived, d_table = together([qk, vo], arrived, d_table)

    got_table = lax.all_to_all(d_table.reshape(64, 16, width), ALL[:4], 0, 0, tiled=False)
    ctx_sum = jnp.sum(arrived.astype(F32), axis=0).astype(BF16)
    spread = jnp.broadcast_to(ctx_sum[None], (32, 32, width))
    for s in (qk, vo):
        s.add()
        s.send()
    got_table, spread = together([qk, vo], got_table, spread)

    grad_ctx = lax.all_to_all(spread, SEQ, 0, 0, tiled=False).reshape(32 * 32, width).astype(F32)
    grad_table = jnp.sum(got_table.astype(F32), axis=0)
    for s in (qk, vo):
        s.add()
        s.send()
    for s in (qk, vo):
        s.add()
    both = join(qk, vo)
    both.send()
    both.add()
    d_hidden = dot(d_ctx, ctx_weight, 1, 1).astype(BF16)

    sum_qkv, sum_out = both.total[:, : 3 * half], both.total[:, 3 * half :]
    sum_out = jnp.concatenate([sum_out[:8], sum_out[8:]], axis=1)
    grad_out = lax.ppermute(
        sum_out, ("z", "c"), [(2 * z + c, 2 * (2 * c + z % 2) + z // 2) for z in range(4) for c in range(2)]
    )
    keep = lax.dynamic_slice_in_dim(sum_qkv, core * 8, 8, 0)
    give = lax.dynamic_slice_in_dim(sum_qkv, 8 - core * 8, 8, 0)
    take = swap(give)
    keep, take = keep.reshape(8, 3, 1, half), take.reshape(8, 3, 1, half)
    grad_qkv = jnp.where(
        core == 0, jnp.concatenate([keep, take], axis=2), jnp.concatenate([take, keep], axis=2)
    ).reshape(8, 6 * half)
    return (d_hidden, grad_ctx, grad_table, grad_qkv, grad_out)


def solution(mesh):
    fine = Mesh(mesh.devices.reshape(4, 2, 4, 2, 2), ALL)
    in_specs = (
        P(SEQ, ("yh", "c")),
        P(("yh", "c"), None),
        P(ALL, None),
        P(),
        P(),
        P(),
        P(ALL, None, None),
    )
    out_specs = (
        P(SEQ, ("yh", "c")),
        P(("yh", "c"), None),
        P(ALL, None),
        P(ALL, None),
        P(ALL, None),
    )
    return jax.shard_map(
        on_device, mesh=fine, in_specs=in_specs, out_specs=out_specs, check_vma=False
    )
```

time: 243 us -> 208 us (0.86)
  blocking collectives: 35.2 us -> 0 us
  waiting for transfers between devices: 82.6 us -> 57.7 us
  other arithmetic: 15.6 us -> 26.1 us
  starting transfers between devices: 43.7 us -> 53.4 us
  matrix products: 12.5 us -> 15.7 us
    ppermute x3 -> x15, waiting for transfers between devices: 7.9 us -> 47.8 us  [the longest x8 30.6 us: send(): lax.ppermute(self.give, RINGS[axis] + ('c',), ring_pairs(axis, self.step))]
    all_to_all x1 -> x0, blocking collectives: 35.2 us -> none  [scatter_sum(): got = lax.all_to_all(parts, axes, 0, 0, tiled=False)]
    all_to_all x3, waiting for transfers between devices: 29.1 us -> 0.01 us  [the longest x1 0.01 us: on_device(): lax.all_to_all(ctx_part.reshape(32, 32, width), SEQ, 0, 0, tiled=False)]
    ppermute x1, waiting for transfers between devices: 36.3 us -> 8.55 us  [on_device(): d_ctx_far = lax.ppermute(d_ctx, 'yh', SWAP)]
    ppermute x3 -> x15, starting transfers between devices: 4.31 us -> 23.4 us  [the longest x8 13.8 us: send(): lax.ppermute(self.give, RINGS[axis] + ('c',), ring_pairs(axis, self.step))]
    convert_element_type x2 -> x18, other arithmetic: 5.16 us -> 19.9 us  [the longest x8 7.48 us: add(): got, keep = ([g.astype(F32) for g in self.got], self.keep.astype(F32))]
    ppermute x1, waiting for transfers between devices: 8.64 us -> 0.01 us  [on_device(): lax.ppermute(sum_out, ('z', 'c'), [(2 * z + c, 2 * (2 * c + z % 2) + z //...]
    all_to_all x3, starting transfers between devices: 27.1 us -> 19.8 us  [the longest x1 8.69 us: on_device(): lax.all_to_all(d_table.reshape(64, 16, width), ALL[:4], 0, 0, tiled=False)]
  transfers between devices with their start and end apart: 11 -> 23, of which waited for: 7 -> 10; matrix products, arithmetic and copies ran while one was open for 9% -> 16% of each run, Pallas kernels for 3% -> 3%
where the time goes in v3:
time: 208 us; the launch traced here: 205 us
  waiting for transfers between devices  57.7 us (28%)
  starting transfers between devices  53.4 us (26%)
  Pallas kernels  39.8 us (19%)
  other arithmetic  26.1 us (13%)
  matrix products  15.7 us (8%)
  local copies, waits for them, and re-layouts  11.1 us (5%)
    pallas_call x1, Pallas kernels, block(): pl.pallas_call(block_kernel, grid_spec=pltpu.PrefetchScalarGridSpec(num_s...  32.8 us
    ppermute x8, waiting for transfers between devices, send(): lax.ppermute(self.give, RINGS[axis] + ('c',), ring_pairs(axis, self.step))  30.6 us
    dot_general x4, matrix products, dot(): lax.dot_general(a, b, (((ca,), (cb,)), ((), ())), preferred_element_type=...  15.7 us
    ppermute x3, waiting for transfers between devices, send(): lax.ppermute(give, RINGS[axis], ring_shift(axis, shift))  15.7 us
    ppermute x8, starting transfers between devices, send(): lax.ppermute(self.give, RINGS[axis] + ('c',), ring_pairs(axis, self.step))  13.8 us
    all_to_all x1, starting transfers between devices, on_device(): lax.all_to_all(d_table.reshape(64, 16, width), ALL[:4], 0, 0, tiled=False)  8.69 us
    ppermute x1, waiting for transfers between devices, on_device(): d_ctx_far = lax.ppermute(d_ctx, 'yh', SWAP)  8.55 us
    unnamed x37, local copies, waits for them, and re-layouts  8.27 us
  transfers between devices with their start and end apart: 23, of which 10 were waited for; matrix products, arithmetic and copies ran while one was open for 16% of the time, Pallas kernels for 3%

profile of v3, /device:TPU:1, one launch (start us, length us, event | category | flops | bytes accessed | tf_op | source)
XLA Modules:
  0.0 205.0 jit_solution(9883421412578759171)
XLA Ops:
  0.7 1.5 collective-permute-start.1
  2.2 0.4 copy-done
  2.5 1.7 convolution_convert_fusion.2
  4.3 3.8 %collective-permute-start = (bf16[128,1024]{1,0:T(8,128)(2,1)S(1)}, bf16[128,1024]{1,0:T(8,128)(2,1)}, u32[]{:S(2)}, u32[]{:S(2)}) collective-permute-start(bf16[128,1024]{1,0:T(8,128)(2,1)S(1)} %dynamic-slice_bitcast_fusion), channel_id=1, source_target_pairs={{0,2},{2,0},{1,3},{3,1},{4,6},{6,4},{5,7},{7,5},{8,10},{10,8},{9,1... | collective-permute-start | bytes 786440 | tf_op jit(solution)/shard_map/ppermute | solution.py:384
  8.2 1.0 collective-permute-start.2
  9.2 0.1 copy.14
  9.4 8.1 %fusion.2.emb_ref = bf16[1024,1024]{1,0:T(8,128)(2,1)} fusion(bf16[2048,1024]{1,0:T(8,128)(2,1)} %param.10, s32[1024]{0:T(1024)S(1)} %eq.45), kind=kOutput, calls=%fused_computation.5 | convolution fusion | flops 4298113024 | bytes 6295552 | tf_op jit(solution)/shard_map/dot_general | solution.py:28
  17.5 1.0 fusion.7
  18.9 1.3 collective-permute-done.3
  20.4 1.2 copy-done.5
  21.6 32.8 %shard_map.110 = (bf16[1024,1024]{1,0:T(8,128)(2,1)}, bf16[128,1024]{1,0:T(8,128)(2,1)S(1)}, bf16[512,1024]{1,0:T(8,128)(2,1)}, bf16[512,1024]{1,0:T(8,128)(2,1)...) custom-call(s32[13]{0:T(128)S(1)} %stack.55.at_ref, bf16[1024,1024]{1,0:T(8,128)(2,1)} %fusion.2.emb_ref, ...), custom_call_target="tpu_custom_call" | custom-call | flops 11811160064 | bytes 20971520 | tf_op jit(solution)/shard_map/pallas_call | solution.py:278
  54.4 1.0 copy-done.3
  55.4 0.1 collective-permute-start.8
  55.6 2.5 %collective-permute-start.4 = (bf16[512,1024]{1,0:T(8,128)(2,1)}, bf16[512,1024]{1,0:T(8,128)(2,1)}, u32[]{:S(2)}, u32[]{:S(2)}) collective-permute-start(bf16[512,1024]{1,0:T(8,128)(2,1)} %get-tuple-element.30), channel_id=1, source_target_pairs={{0,4},{1,13},{4,0},{5,9},{8,12},{9,5},{12,8},{13,1},{2,6},{3,15},{... | collective-permute-start | bytes 3145736 | tf_op jit(solution)/shard_map/ppermute | solution.py:132
  58.0 3.8 %collective-permute-start.5 = (bf16[512,1024]{1,0:T(8,128)(2,1)}, bf16[512,1024]{1,0:T(8,128)(2,1)}, u32[]{:S(2)}, u32[]{:S(2)}) collective-permute-start(bf16[512,1024]{1,0:T(8,128)(2,1)} %get-tuple-element.31), channel_id=1, source_target_pairs={{0,32},{1,97},{32,0},{33,65},{64,96},{65,33},{96,64},{97,1},{2,34}... | collective-permute-start | bytes 3145736 | tf_op jit(solution)/shard_map/ppermute | solution.py:132
  61.8 1.5 collective-permute-done.6
  63.4 0.9 collective-permute-start.7
  64.3 8.5 %collective-permute-done.7 = bf16[128,1024]{1,0:T(8,128)(2,1)} collective-permute-done((bf16[128,1024]{1,0:T(8,128)(2,1)S(1)}, bf16[128,1024]{1,0:T(8,128)(2,1)}, u32[]{:S(2)}, u32[]{:S(2)}) %collective-permute-start.7) | collective-permute-done | bytes 262176 | tf_op jit(solution)/shard_map/ppermute | solution.py:402
  72.9 1.4 collective-permute-done.5
  74.3 3.3 %convolution_convert_fusion = bf16[1024,1024]{0,1:T(8,128)(2,1)} fusion(bf16[256,1024]{1,0:T(8,128)(2,1)} %param.7, bf16[128,1024]{1,0:T(8,128)(2,1)} %collective-permute-done.7, bf16[128,1024]{1,0:T(8,128)(2,1)S(1)} %add_convert_fusion.2, pred[]{:T(512)S(6)} %eq.43), kind=kOutput, calls=%fused_computation.6 | convolution fusion | flops 540278784 | bytes 3145729 | tf_op jit(solution)/shard_map/dot_general | solution.py:28
  77.6 4.8 %all-to-all-start = ((bf16[32,32,1024]{2,1,0:T(8,128)(2,1)}), bf16[32,32,1024]{2,1,0:T(8,128)(2,1)}, u32[]{:S(2)}, u32[]{:S(2)}) async-start(bf16[32,32,1024]{2,1,0:T(8,128)(2,1)} %bitcast.61), calls=%async_computation | async-start | bytes 4194304 | tf_op jit(solution)/shard_map/all_to_all | solution.py:415
  82.4 1.5 convert_element_type.174
  83.9 0.2 convert_element_type.169
  84.2 2.3 %convert_element_type.175 = f32[512,1024]{1,0:T(8,128)S(1)} convert(bf16[512,1024]{1,0:T(8,128)(2,1)} %collective-permute-done.5) | non-fusion elementwise | flops 524288 | bytes 3145728 | tf_op jit(solution)/shard_map/convert_element_type | solution.py:141
  86.4 1.0 fusion.4
  87.5 1.2 collective-permute-start.10
  88.6 1.5 convert_element_type.170
  90.2 0.9 fusion.5
  91.1 0.5 copy-done.10
  91.6 1.2 collective-permute-start.9
  92.9 1.6 copy-done.2
  94.5 7.0 %shard_map.111 = bf16[1024,1024]{1,0:T(8,128)(2,1)S(1)} custom-call(s32[13]{0:T(128)S(1)} %stack.55.at_ref, s32[1,1024]{1,0:T(1,128)S(1)} %reshape_reshape.3.ids_ref, bf16[512,1024]{1,0:T(8,128)(2,1)S(1)} %bitcast.58, bf16[512,1024]{1,0:T(8,128)(2,1)} %collective-permute-done.2.oth_ref, bf16[1024,1024]{1,0:T(8,128)(2,1)S(1)} %copy-done.2, ...), custom_call_target="tpu_custom_call" | custom-call | flops 2147483648 | bytes 9437184 | tf_op jit(solution)/shard_map/pallas_call | solution.py:349
  101.5 1.4 copy-done.1
  102.8 10.4 %collective-permute-done.10 = bf16[256,1024]{1,0:T(8,128)(2,1)} collective-permute-done((bf16[256,1024]{1,0:T(8,128)(2,1)}, bf16[256,1024]{1,0:T(8,128)(2,1)}, u32[]{:S(2)}, u32[]{:S(2)}) %collective-permute-start.10) | collective-permute-done | bytes 524320 | tf_op jit(solution)/shard_map/ppermute | solution.py:132
  113.3 8.7 %all-to-all-start.1 = ((bf16[64,16,1024]{2,1,0:T(8,128)(2,1)}), bf16[64,16,1024]{2,1,0:T(8,128)(2,1)}, u32[]{:S(2)}, u32[]{:S(2)}) async-start(bf16[64,16,1024]{2,1,0:T(8,128)(2,1)} %bitcast.55), calls=%async_computation.1 | async-start | bytes 4194304 | tf_op jit(solution)/shard_map/all_to_all | solution.py:422
  122.0 3.1 %add_convert_fusion = (bf16[256,1024]{1,0:T(8,128)(2,1)S(1)}, bf16[256,1024]{1,0:T(8,128)(2,1)S(1)}) fusion(bf16[256,1024]{1,0:T(8,128)(2,1)} %collective-permute-done.10, f32[512,1024]{1,0:T(8,128)} %copy-done.9, f32[512,1024]{1,0:T(8,128)} %copy-done.7, bf16[256,1024]{1,0:T(8,128)(2,1)} %collective-permute-done.9, f32[512,1024]{1,0:T(8,128)} %copy-done.10, ...), kind=kLoop, calls=%fused_computation.17 | loop fusion | flops 3145728 | bytes 6291456 | tf_op jit(solution)/shard_map/convert_element_type | solution.py:153
  125.2 0.7 pad_maximum_fusion.1
  125.9 2.1 %collective-permute-start.12 = (bf16[128,1024]{1,0:T(8,128)(2,1)}, bf16[128,1024]{1,0:T(8,128)(2,1)}, u32[]{:S(2)}, u32[]{:S(2)}) collective-permute-start(bf16[128,1024]{1,0:T(8,128)(2,1)} %pad_maximum_fusion.1), channel_id=1, source_target_pairs={{0,4},{1,13},{4,0},{5,9},{8,12},{9,5},{12,8},{13,1},{2,6},{3,15},{... | collective-permute-start | bytes 786440 | tf_op jit(solution)/shard_map/ppermute | solution.py:132
  128.1 0.7 pad_maximum_fusion
  128.8 2.6 %collective-permute-start.11 = (bf16[128,1024]{1,0:T(8,128)(2,1)}, bf16[128,1024]{1,0:T(8,128)(2,1)}, u32[]{:S(2)}, u32[]{:S(2)}) collective-permute-start(bf16[128,1024]{1,0:T(8,128)(2,1)} %pad_maximum_fusion), channel_id=1, source_target_pairs={{0,32},{1,97},{32,0},{33,65},{64,96},{65,33},{96,64},{97,1},{2,34}... | collective-permute-start | bytes 786440 | tf_op jit(solution)/shard_map/ppermute | solution.py:132
  131.5 2.0 reduce_sum.21
  133.5 16.9 %collective-permute-done.12 = bf16[128,1024]{1,0:T(8,128)(2,1)} collective-permute-done((bf16[128,1024]{1,0:T(8,128)(2,1)}, bf16[128,1024]{1,0:T(8,128)(2,1)}, u32[]{:S(2)}, u32[]{:S(2)}) %collective-permute-start.12) | collective-permute-done | bytes 262176 | tf_op jit(solution)/shard_map/ppermute | solution.py:132
  150.4 1.8 collective-permute-done.11
  152.2 1.6 broadcast_in_dim.2
  153.8 1.0 convert_element_type.189
  154.9 0.8 copy-done.12
  155.6 1.0 convert_element_type.196
  156.6 0.8 copy-done.11
  157.4 0.4 collective-permute-start.14
  157.9 6.3 %all-to-all-start.2 = ((bf16[32,32,1024]{2,1,0:T(8,128)(2,1)}), bf16[32,32,1024]{2,1,0:T(8,128)(2,1)}, u32[]{:S(2)}, u32[]{:S(2)}) async-start(bf16[32,32,1024]{2,1,0:T(8,128)(2,1)} %broadcast_in_dim.2), calls=%async_computation.2 | async-start | bytes 4194304 | tf_op jit(solution)/shard_map/all_to_all | solution.py:430
  164.2 1.1 add_convert_fusion.5
  165.3 1.0 add_convert_fusion.4
  166.4 2.0 collective-permute-start.15
  168.4 0.6 collective-permute-start.16
  168.9 2.1 %collective-permute-start.17 = (bf16[16,2048]{1,0:T(8,128)(2,1)S(1)}, bf16[16,2048]{1,0:T(8,128)(2,1)S(1)}, u32[]{:S(2)}, u32[]{:S(2)}) collective-permute-start(bf16[16,2048]{1,0:T(8,128)(2,1)S(1)} %get-tuple-element.58), channel_id=1, source_target_pairs={{0,18},{16,0},{2,16},{18,2},{1,19},{17,1},{3,17},{19,3},{4,22},{20... | collective-permute-start | bytes 196616 | tf_op jit(solution)/shard_map/ppermute | solution.py:136
  171.1 2.6 %convolution_convert_fusion.1 = bf16[256,1024]{1,0:T(8,128)(2,1)} fusion(bf16[1024,1024]{1,0:T(8,128)(2,1)S(1)} %copy-done, bf16[128,1024]{1,0:T(8,128)(2,1)} %collective-permute-done.7, bf16[128,1024]{1,0:T(8,128)(2,1)S(1)} %copy-done.16, pred[]{:T(512)S(6)} %eq.43), kind=kOutput, calls=%fused_computation.7 | convolution fusion | flops 539492352 | bytes 3145729 | tf_op jit(solution)/shard_map/dot_general | solution.py:28
  173.6 10.8 %collective-permute-done.15 = bf16[16,2048]{1,0:T(8,128)(2,1)S(1)} collective-permute-done((bf16[16,2048]{1,0:T(8,128)(2,1)S(1)}, bf16[16,2048]{1,0:T(8,128)(2,1)S(1)}, u32[]{:S(2)}, u32[]{:S(2)}) %collective-permute-start.15) | collective-permute-done | bytes 65568 | tf_op jit(solution)/shard_map/ppermute | solution.py:136
  184.4 2.5 %collective-permute-done.16 = bf16[16,2048]{1,0:T(8,128)(2,1)S(1)} collective-permute-done((bf16[16,2048]{1,0:T(8,128)(2,1)S(1)}, bf16[16,2048]{1,0:T(8,128)(2,1)S(1)}, u32[]{:S(2)}, u32[]{:S(2)}) %collective-permute-start.16) | collective-permute-done | bytes 65568 | tf_op jit(solution)/shard_map/ppermute | solution.py:136
  186.9 2.5 %collective-permute-done.17 = bf16[16,2048]{1,0:T(8,128)(2,1)S(1)} collective-permute-done((bf16[16,2048]{1,0:T(8,128)(2,1)S(1)}, bf16[16,2048]{1,0:T(8,128)(2,1)S(1)}, u32[]{:S(2)}, u32[]{:S(2)}) %collective-permute-start.17) | collective-permute-done | bytes 65568 | tf_op jit(solution)/shard_map/ppermute | solution.py:136
  189.4 7.5 %collective-permute-start.19 = (f32[8,1024]{1,0:T(8,128)S(1)}, f32[8,1024]{1,0:T(8,128)S(1)}, u32[]{:S(2)}, u32[]{:S(2)}) collective-permute-start(f32[8,1024]{1,0:T(8,128)S(1)} %pad_maximum_fusion.3), channel_id=1, source_target_pairs={{0,0},{1,64},{32,32},{33,96},{64,1},{65,65},{96,33},{97,97},{2,2},... | collective-permute-start | bytes 98312 | tf_op jit(solution)/shard_map/ppermute | solution.py:444
  197.1 2.6 %convert_reduce_fusion = f32[16,1024]{1,0:T(8,128)} fusion(bf16[64,16,1024]{2,1,0:T(8,128)(2,1)} %all-to-all-done.1), kind=kLoop, calls=%fused_computation.2 | loop fusion | flops 2080768 | bytes 2162688 | tf_op jit(solution)/shard_map/reduce_sum | solution.py:431
  199.7 0.6 copy.16
  200.4 4.1 %bitcast_convert_fusion = f32[1024,1024]{1,0:T(8,128)} fusion(bf16[32,32,1024]{2,1,0:T(8,128)(2,1)} %all-to-all-done.2), kind=kLoop, calls=%fused_computation.4 | loop fusion | flops 1048576 | bytes 6291456 | tf_op jit(solution)/shard_map/convert_element_type | solution.py:430
  204.4 0.6 copy.18
  (68 shorter events, 1.3 us)
Async XLA Ops:
  0.6 1.9 copy-start
  0.6 8.5 %copy-start.17 = (s32[64,8]{0,1:T(8,128)S(1)}, s32[64,8]{0,1:T(8,128)}, u32[]{:S(2)}) copy-start(s32[64,8]{0,1:T(8,128)} %param.9) | copy-start | bytes 6148
  0.7 7.5 %copy-start.4 = (bf16[64,8,1024]{2,1,0:T(8,128)(2,1)S(1)}, bf16[64,8,1024]{2,1,0:T(8,128)(2,1)}, u32[]{:S(2)}) copy-start(bf16[64,8,1024]{2,1,0:T(8,128)(2,1)} %param.13) | copy-start | bytes 3145732
  0.7 8.5 %collective-permute-start.1 = (s32[64,8]{0,1:T(8,128)}, s32[64,8]{0,1:T(8,128)S(1)}, u32[]{:S(2)}, u32[]{:S(2)}) collective-permute-start(s32[64,8]{0,1:T(8,128)} %param.9), channel_id=1, source_target_pairs={{0,1},{1,0},{2,3},{3,2},{4,5},{5,4},{6,7},{7,6},{8,9},{9,8},{10,11... | collective-permute-start | bytes 6152 | tf_op jit(solution)/shard_map/ppermute | solution.py:387
  4.3 3.9 %copy-start.13 = (bf16[256,1024]{1,0:T(8,128)(2,1)}, bf16[256,1024]{1,0:T(8,128)(2,1)S(1)}, u32[]{:S(2)}) copy-start(bf16[256,1024]{1,0:T(8,128)(2,1)S(1)} %convolution_convert_fusion.2) | copy-start | bytes 1572868
  4.3 13.2 %collective-permute-start = (bf16[128,1024]{1,0:T(8,128)(2,1)S(1)}, bf16[128,1024]{1,0:T(8,128)(2,1)}, u32[]{:S(2)}, u32[]{:S(2)}) collective-permute-start(bf16[128,1024]{1,0:T(8,128)(2,1)S(1)} %dynamic-slice_bitcast_fusion), channel_id=1, source_target_pairs={{0,2},{2,0},{1,3},{3,1},{4,6},{6,4},{5,7},{7,5},{8,10},{10,8},{9,1... | collective-permute-start | bytes 786440 | tf_op jit(solution)/shard_map/ppermute | solution.py:384
  8.2 9.4 %collective-permute-start.2 = (bf16[512,1024]{1,0:T(8,128)(2,1)S(1)}, bf16[512,1024]{1,0:T(8,128)(2,1)}, u32[]{:S(2)}, u32[]{:S(2)}) collective-permute-start(bf16[512,1024]{1,0:T(8,128)(2,1)S(1)} %bitcast.56), channel_id=1, source_target_pairs={{0,1},{1,0},{2,3},{3,2},{4,5},{5,4},{6,7},{7,6},{8,9},{9,8},{10,11... | collective-permute-start | bytes 3145736 | tf_op jit(solution)/shard_map/ppermute | solution.py:389
  9.4 8.1 %copy-start.14 = (bf16[256,1024]{1,0:T(8,128)(2,1)S(1)}, bf16[256,1024]{1,0:T(8,128)(2,1)}, u32[]{:S(2)}) copy-start(bf16[256,1024]{1,0:T(8,128)(2,1)} %copy-done.13) | copy-start | bytes 1572868
  18.6 1.6 collective-permute-start.3
  20.4 1.2 copy-start.5
  54.4 1.0 copy-start.3
  55.4 18.9 %collective-permute-start.8 = (bf16[1024,1024]{1,0:T(8,128)(2,1)}, bf16[1024,1024]{1,0:T(8,128)(2,1)}, u32[]{:S(2)}, u32[]{:S(2)}) collective-permute-start(bf16[1024,1024]{1,0:T(8,128)(2,1)} %get-tuple-element.33.mine_ref), channel_id=1, source_target_pairs={{0,1},{1,0},{2,3},{3,2},{4,5},{5,4},{6,7},{7,6},{8,9},{9,8},{10,11... | collective-permute-start | bytes 6291464 | tf_op jit(solution)/shard_map/ppermute | solution.py:406
  55.6 17.3 %collective-permute-start.4 = (bf16[512,1024]{1,0:T(8,128)(2,1)}, bf16[512,1024]{1,0:T(8,128)(2,1)}, u32[]{:S(2)}, u32[]{:S(2)}) collective-permute-start(bf16[512,1024]{1,0:T(8,128)(2,1)} %get-tuple-element.30), channel_id=1, source_target_pairs={{0,4},{1,13},{4,0},{5,9},{8,12},{9,5},{12,8},{13,1},{2,6},{3,15},{... | collective-permute-start | bytes 3145736 | tf_op jit(solution)/shard_map/ppermute | solution.py:132
  58.0 16.3 %collective-permute-start.5 = (bf16[512,1024]{1,0:T(8,128)(2,1)}, bf16[512,1024]{1,0:T(8,128)(2,1)}, u32[]{:S(2)}, u32[]{:S(2)}) collective-permute-start(bf16[512,1024]{1,0:T(8,128)(2,1)} %get-tuple-element.31), channel_id=1, source_target_pairs={{0,32},{1,97},{32,0},{33,65},{64,96},{65,33},{96,64},{97,1},{2,34}... | collective-permute-start | bytes 3145736 | tf_op jit(solution)/shard_map/ppermute | solution.py:132
  61.8 1.5 collective-permute-start.6
  63.4 14.2 %copy-start.15 = (bf16[128,1024]{1,0:T(8,128)(2,1)}, bf16[128,1024]{1,0:T(8,128)(2,1)S(1)}, u32[]{:S(2)}) copy-start(bf16[128,1024]{1,0:T(8,128)(2,1)S(1)} %add_convert_fusion.2) | copy-start | bytes 786436
  63.4 9.5 %collective-permute-start.7 = (bf16[128,1024]{1,0:T(8,128)(2,1)S(1)}, bf16[128,1024]{1,0:T(8,128)(2,1)}, u32[]{:S(2)}, u32[]{:S(2)}) collective-permute-start(bf16[128,1024]{1,0:T(8,128)(2,1)S(1)} %add_convert_fusion.2), channel_id=1, source_target_pairs={{0,2},{2,0},{1,3},{3,1},{4,6},{6,4},{5,7},{7,5},{8,10},{10,8},{9,1... | collective-permute-start | bytes 786440 | tf_op jit(solution)/shard_map/ppermute | solution.py:402
  77.6 35.7 %all-to-all-start = ((bf16[32,32,1024]{2,1,0:T(8,128)(2,1)}), bf16[32,32,1024]{2,1,0:T(8,128)(2,1)}, u32[]{:S(2)}, u32[]{:S(2)}) async-start(bf16[32,32,1024]{2,1,0:T(8,128)(2,1)} %bitcast.61), calls=%async_computation | async-start | bytes 4194304 | tf_op jit(solution)/shard_map/all_to_all | solution.py:415
  83.9 2.5 %copy-start.7 = (f32[512,1024]{1,0:T(8,128)}, f32[512,1024]{1,0:T(8,128)S(1)}, u32[]{:S(2)}) copy-start(f32[512,1024]{1,0:T(8,128)S(1)} %convert_element_type.174) | copy-start | bytes 6291460
  84.2 6.0 %copy-start.8 = (f32[512,1024]{1,0:T(8,128)}, f32[512,1024]{1,0:T(8,128)S(1)}, u32[]{:S(2)}) copy-start(f32[512,1024]{1,0:T(8,128)S(1)} %convert_element_type.169) | copy-start | bytes 6291460
  86.4 3.7 %copy-start.9 = (f32[512,1024]{1,0:T(8,128)}, f32[512,1024]{1,0:T(8,128)S(1)}, u32[]{:S(2)}) copy-start(f32[512,1024]{1,0:T(8,128)S(1)} %convert_element_type.175) | copy-start | bytes 6291460
  87.5 25.8 %collective-permute-start.10 = (bf16[256,1024]{1,0:T(8,128)(2,1)}, bf16[256,1024]{1,0:T(8,128)(2,1)}, u32[]{:S(2)}, u32[]{:S(2)}) collective-permute-start(bf16[256,1024]{1,0:T(8,128)(2,1)} %fusion.4), channel_id=1, source_target_pairs={{0,96},{1,33},{32,64},{33,1},{64,32},{65,97},{96,0},{97,65},{2,98}... | collective-permute-start | bytes 1572872 | tf_op jit(solution)/shard_map/ppermute | solution.py:132
  90.1 1.5 copy-start.10
  90.1 2.7 %copy-start.6 = (bf16[64,8,1024]{2,1,0:T(8,128)(2,1)S(1)}, bf16[64,8,1024]{2,1,0:T(8,128)(2,1)}, u32[]{:S(2)}) copy-start(bf16[64,8,1024]{2,1,0:T(8,128)(2,1)} %param.13) | copy-start | bytes 3145732
  91.6 21.7 %collective-permute-start.9 = (bf16[256,1024]{1,0:T(8,128)(2,1)}, bf16[256,1024]{1,0:T(8,128)(2,1)}, u32[]{:S(2)}, u32[]{:S(2)}) collective-permute-start(bf16[256,1024]{1,0:T(8,128)(2,1)} %fusion.5), channel_id=1, source_target_pairs={{0,12},{1,5},{4,8},{5,1},{8,4},{9,13},{12,0},{13,9},{2,14},{3,7},{... | collective-permute-start | bytes 1572872 | tf_op jit(solution)/shard_map/ppermute | solution.py:132
  92.9 1.6 copy-start.2
  101.4 1.4 copy-start.1
  113.3 39.0 %all-to-all-start.1 = ((bf16[64,16,1024]{2,1,0:T(8,128)(2,1)}), bf16[64,16,1024]{2,1,0:T(8,128)(2,1)}, u32[]{:S(2)}, u32[]{:S(2)}) async-start(bf16[64,16,1024]{2,1,0:T(8,128)(2,1)} %bitcast.55), calls=%async_computation.1 | async-start | bytes 4194304 | tf_op jit(solution)/shard_map/all_to_all | solution.py:422
  125.9 24.5 %collective-permute-start.12 = (bf16[128,1024]{1,0:T(8,128)(2,1)}, bf16[128,1024]{1,0:T(8,128)(2,1)}, u32[]{:S(2)}, u32[]{:S(2)}) collective-permute-start(bf16[128,1024]{1,0:T(8,128)(2,1)} %pad_maximum_fusion.1), channel_id=1, source_target_pairs={{0,4},{1,13},{4,0},{5,9},{8,12},{9,5},{12,8},{13,1},{2,6},{3,15},{... | collective-permute-start | bytes 786440 | tf_op jit(solution)/shard_map/ppermute | solution.py:132
  128.8 23.4 %collective-permute-start.11 = (bf16[128,1024]{1,0:T(8,128)(2,1)}, bf16[128,1024]{1,0:T(8,128)(2,1)}, u32[]{:S(2)}, u32[]{:S(2)}) collective-permute-start(bf16[128,1024]{1,0:T(8,128)(2,1)} %pad_maximum_fusion), channel_id=1, source_target_pairs={{0,32},{1,97},{32,0},{33,65},{64,96},{65,33},{96,64},{97,1},{2,34}... | collective-permute-start | bytes 786440 | tf_op jit(solution)/shard_map/ppermute | solution.py:132
  154.8 0.8 copy-start.12
  155.6 8.6 %collective-permute-start.13 = (bf16[64,1024]{1,0:T(8,128)(2,1)S(1)}, bf16[64,1024]{1,0:T(8,128)(2,1)}, u32[]{:S(2)}, u32[]{:S(2)}) collective-permute-start(bf16[64,1024]{1,0:T(8,128)(2,1)S(1)} %fusion.10), channel_id=1, source_target_pairs={{0,96},{1,33},{32,64},{33,1},{64,32},{65,97},{96,0},{97,65},{2,98}... | collective-permute-start | bytes 393224 | tf_op jit(solution)/shard_map/ppermute | solution.py:132
  156.6 0.8 copy-start.11
  157.4 7.9 %collective-permute-start.14 = (bf16[64,1024]{1,0:T(8,128)(2,1)S(1)}, bf16[64,1024]{1,0:T(8,128)(2,1)S(1)}, u32[]{:S(2)}, u32[]{:S(2)}) collective-permute-start(bf16[64,1024]{1,0:T(8,128)(2,1)S(1)} %fusion.8), channel_id=1, source_target_pairs={{0,12},{1,5},{4,8},{5,1},{8,4},{9,13},{12,0},{13,9},{2,14},{3,7},{... | collective-permute-start | bytes 393224 | tf_op jit(solution)/shard_map/ppermute | solution.py:132
  157.9 42.5 %all-to-all-start.2 = ((bf16[32,32,1024]{2,1,0:T(8,128)(2,1)}), bf16[32,32,1024]{2,1,0:T(8,128)(2,1)}, u32[]{:S(2)}, u32[]{:S(2)}) async-start(bf16[32,32,1024]{2,1,0:T(8,128)(2,1)} %broadcast_in_dim.2), calls=%async_computation.2 | async-start | bytes 4194304 | tf_op jit(solution)/shard_map/all_to_all | solution.py:430
  164.2 6.9 %copy-start.16 = (bf16[128,1024]{1,0:T(8,128)(2,1)S(1)}, bf16[128,1024]{1,0:T(8,128)(2,1)}, u32[]{:S(2)}) copy-start(bf16[128,1024]{1,0:T(8,128)(2,1)} %copy-done.15) | copy-start | bytes 786436
  166.4 18.1 %collective-permute-start.15 = (bf16[16,2048]{1,0:T(8,128)(2,1)S(1)}, bf16[16,2048]{1,0:T(8,128)(2,1)S(1)}, u32[]{:S(2)}, u32[]{:S(2)}) collective-permute-start(bf16[16,2048]{1,0:T(8,128)(2,1)S(1)} %get-tuple-element.57), channel_id=1, source_target_pairs={{0,2},{16,18},{2,0},{18,16},{1,3},{17,19},{3,1},{19,17},{4,6},{20,... | collective-permute-start | bytes 196616 | tf_op jit(solution)/shard_map/ppermute | solution.py:136
  168.4 18.5 %collective-permute-start.16 = (bf16[16,2048]{1,0:T(8,128)(2,1)S(1)}, bf16[16,2048]{1,0:T(8,128)(2,1)S(1)}, u32[]{:S(2)}, u32[]{:S(2)}) collective-permute-start(bf16[16,2048]{1,0:T(8,128)(2,1)S(1)} %get-tuple-element.59), channel_id=1, source_target_pairs={{0,16},{16,2},{2,18},{18,0},{1,17},{17,3},{3,19},{19,1},{4,20},{20... | collective-permute-start | bytes 196616 | tf_op jit(solution)/shard_map/ppermute | solution.py:136
  168.9 20.4 %collective-permute-start.17 = (bf16[16,2048]{1,0:T(8,128)(2,1)S(1)}, bf16[16,2048]{1,0:T(8,128)(2,1)S(1)}, u32[]{:S(2)}, u32[]{:S(2)}) collective-permute-start(bf16[16,2048]{1,0:T(8,128)(2,1)S(1)} %get-tuple-element.58), channel_id=1, source_target_pairs={{0,18},{16,0},{2,16},{18,2},{1,19},{17,1},{3,17},{19,3},{4,22},{20... | collective-permute-start | bytes 196616 | tf_op jit(solution)/shard_map/ppermute | solution.py:136
  189.4 10.3 %collective-permute-start.19 = (f32[8,1024]{1,0:T(8,128)S(1)}, f32[8,1024]{1,0:T(8,128)S(1)}, u32[]{:S(2)}, u32[]{:S(2)}) collective-permute-start(f32[8,1024]{1,0:T(8,128)S(1)} %pad_maximum_fusion.3), channel_id=1, source_target_pairs={{0,0},{1,64},{32,32},{33,96},{64,1},{65,65},{96,33},{97,97},{2,2},... | collective-permute-start | bytes 98312 | tf_op jit(solution)/shard_map/ppermute | solution.py:444
  197.0 2.7 %collective-permute-start.18 = (f32[8,1536]{1,0:T(8,128)S(1)}, f32[8,1536]{1,0:T(8,128)S(1)}, u32[]{:S(2)}, u32[]{:S(2)}) collective-permute-start(f32[8,1536]{1,0:T(8,128)S(1)} %get-tuple-element.65), channel_id=1, source_target_pairs={{0,1},{1,0},{2,3},{3,2},{4,5},{5,4},{6,7},{7,6},{8,9},{9,8},{10,11... | collective-permute-start | bytes 147464 | tf_op jit(solution)/shard_map/ppermute | solution.py:449

commit v4 on v3

--- a/solution.py
+++ b/solution.py
@@ -28,11 +28,11 @@
     return lax.dot_general(a, b, (((ca,), (cb,)), ((), ())), preferred_element_type=F32)
 
 
-def attend(query, keys, values, d_mixed):
-    row = lax.broadcasted_iota(jnp.int32, (2 * BLOCK, BLOCK), 0) % BLOCK
-    col = lax.broadcasted_iota(jnp.int32, (2 * BLOCK, BLOCK), 1)
-    visible = (row // BOOKS == col // BOOKS) & (col <= row)
+def attend(proj, d_mixed, mixed, d_proj, at):
+    half = d_mixed.shape[1]
     low = lax.broadcasted_iota(jnp.int32, (BLOCK, LANES), 1) < SIZE
+    group = lax.broadcasted_iota(jnp.int32, (BOOKS, 2 * BLOCK), 1) % BLOCK // BOOKS
+    frames = BLOCK // BOOKS
 
     def stack(a):
         zero = jnp.zeros_like(a)
@@ -41,19 +41,40 @@
     def pick(a):
         return jnp.where(low, a[:BLOCK], a[BLOCK:]).astype(BF16)
 
-    query, d_mixed = stack(query), stack(d_mixed)
-    scores = dot(query, keys, 1, 1) * F32(0.125)
-    weights = jnp.where(visible, jnp.exp(scores), F32(0.0))
-    exact = weights * (F32(1.0) / jnp.sum(weights, axis=1, keepdims=True))
-    probs = exact.astype(BF16)
-    mixed = pick(dot(probs, values, 1, 0))
-    d_probs = dot(d_mixed, values, 1, 1).astype(BF16).astype(F32)
-    inner = jnp.sum(d_probs * exact, axis=1, keepdims=True)
-    d_scores = (exact * (d_probs - inner) * F32(0.125)).astype(BF16)
-    d_query = pick(dot(d_scores, keys, 1, 0))
-    d_keys = dot(d_scores, query, 0, 0).astype(BF16)
-    d_values = dot(probs, d_mixed, 0, 0).astype(BF16)
-    return mixed, d_query, d_keys, d_values
+    def gather(a):
+        out = a[:BOOKS]
+        for f in range(1, frames):
+            out = jnp.where(group == f, a[f * BOOKS : (f + 1) * BOOKS], out)
+        return out
+
+    def spread(a):
+        zero = jnp.zeros_like(a)
+        return jnp.concatenate(
+            [jnp.where(group == f, a, zero) for f in range(frames)], axis=0
+        ).astype(BF16)
+
+    pairs = half // LANES
+    cols = [slice(p * LANES, (p + 1) * LANES) for p in range(pairs)]
+    kcols = [slice(half + c.start, half + c.stop) for c in cols]
+    vcols = [slice(2 * half + c.start, 2 * half + c.stop) for c in cols]
+    scores = [gather(dot(proj[at, k], stack(proj[at, q]), 1, 1)) for q, k in zip(cols, kcols)]
+    d_probs = [gather(dot(proj[at, v], stack(d_mixed[at, q]), 1, 1)) for q, v in zip(cols, vcols)]
+    scores = jnp.concatenate(scores, axis=1) * F32(0.125)
+    d_probs = jnp.concatenate(d_probs, axis=1).astype(BF16).astype(F32)
+    key = lax.broadcasted_iota(jnp.int32, scores.shape, 0)
+    query = lax.broadcasted_iota(jnp.int32, scores.shape, 1) % BOOKS
+    weights = jnp.where(key <= query, jnp.exp(scores), F32(0.0))
+    exact = weights / jnp.sum(weights, axis=0, keepdims=True)
+    inner = jnp.sum(d_probs * exact, axis=0, keepdims=True)
+    d_scores = exact * (d_probs - inner) * F32(0.125)
+    for p in range(pairs):
+        here = slice(p * 2 * BLOCK, (p + 1) * 2 * BLOCK)
+        probs = spread(exact[:, here])
+        mixed[at, cols[p]] = pick(dot(probs, proj[at, vcols[p]], 0, 0))
+        d_proj[at, vcols[p]] = dot(probs, stack(d_mixed[at, cols[p]]), 1, 0).astype(BF16)
+        ds = spread(d_scores[:, here])
+        d_proj[at, cols[p]] = pick(dot(ds, proj[at, kcols[p]], 0, 0))
+        d_proj[at, kcols[p]] = dot(ds, stack(proj[at, cols[p]]), 1, 0).astype(BF16)
 
 
 def ring_place(axis):
@@ -138,14 +159,14 @@
             ]
 
     def add(self):
-        got, keep = [g.astype(F32) for g in self.got], self.keep.astype(F32)
+        got, keep = self.got, self.keep
         if self.order[0].islower() and self.step == 0:
             half = keep.shape[0] // 2
-            self.keep = (keep[:half] + got[0][:half]).astype(BF16)
-            self.give = (keep[half:] + got[0][half:]).astype(BF16)
+            self.keep = (keep[:half].astype(F32) + got[0][:half].astype(F32)).astype(BF16)
+            self.give = (keep[half:].astype(F32) + got[0][half:].astype(F32)).astype(BF16)
             self.step = 1
             return
-        total = sum(got, keep)
+        total = sum([g.astype(F32) for g in got], keep.astype(F32))
         self.step, self.order = 0, self.order[1:]
         if not self.order:
             self.total = total
@@ -191,6 +212,11 @@
     for s, got in zip(streams, out[0]):
         s.got = got
     return out[1]
+
+
+def after(streams, value):
+    for s in streams:
+        s.got, _ = lax.optimization_barrier((s.got, value))
 
 
 def block_kernel(
@@ -210,14 +236,7 @@
         proj[:, part * half : (part + 1) * half] = dot(stream, w_ref[...], 1, 0).astype(BF16)
     d_mixed[...] = dot(cot, wo_ref[...], 1, 1).astype(BF16)
     for block in range(rows // BLOCK):
-        at = slice(block * BLOCK, (block + 1) * BLOCK)
-        for pair in range(half // LANES):
-            q = slice(pair * LANES, (pair + 1) * LANES)
-            k = slice(half + pair * LANES, half + (pair + 1) * LANES)
-            v = slice(2 * half + pair * LANES, 2 * half + (pair + 1) * LANES)
-            mixed[at, q], d_proj[at, q], d_proj[at, k], d_proj[at, v] = attend(
-                proj[at, q], proj[at, k], proj[at, v], d_mixed[at, q]
-            )
+        attend(proj, d_mixed, mixed, d_proj, slice(block * BLOCK, (block + 1) * BLOCK))
     d_flat = dot(d_proj[:, :half], wq_ref[...], 1, 1)
     d_flat += dot(d_proj[:, half : 2 * half], wk_ref[...], 1, 1)
     d_flat += dot(d_proj[:, 2 * half :], wv_ref[...], 1, 1)
@@ -255,7 +274,7 @@
 
 
 def halves(rows, width):
-    last = 1
+    last = STEPS // 2 - 1
     return [
         pl.BlockSpec((rows, width), lambda i, *_: (jnp.minimum(i, last), 0)),
         pl.BlockSpec((rows, width), lambda i, *_: (jnp.maximum(i - last - 1, 0), 0)),
@@ -319,7 +338,7 @@
     )(at, embedded, context, own, oth, qkv_weight, qkv_weight, qkv_weight, out_weight)
 
 
-def table_kernel(at_ref, ids_ref, own_ref, oth_ref, mine_ref, other_ref, d_table_ref, acc):
+def table_kernel(at_ref, ids_ref, own_ref, oth_ref, mine_ref, other_ref, give_ref, keep_ref, acc):
     step = pl.program_id(0)
     cot = jnp.where(step < pl.num_programs(0) // 2, own_ref[...], oth_ref[...])
     d_flat = (mine_ref[...].astype(F32) + other_ref[...].astype(F32)).astype(BF16)
@@ -339,13 +358,16 @@
 
     @pl.when(step == pl.num_programs(0) - 1)
     def _():
-        d_table_ref[...] = acc[...].astype(BF16)
+        def read(chip):
+            return acc[pl.ds(pl.multiple_of(chip * 16, 16), 16), :]
+
+        write_parts(at_ref, "y", give_ref, keep_ref, read)
 
 
 def table_grad(at, ids, own, oth, mine, other, vocab):
     tokens, width = mine.shape
     rows = tokens // STEPS
-    out = (vocab // 2, width)
+    out = (vocab // 4, width)
     return pl.pallas_call(
         table_kernel,
         grid_spec=pltpu.PrefetchScalarGridSpec(
@@ -357,11 +379,11 @@
                 pl.BlockSpec((rows, width), lambda i, a: (i, 0)),
                 pl.BlockSpec((rows, width), lambda i, a: ((i + STEPS // 2) % STEPS, 0)),
             ],
-            out_specs=pl.BlockSpec(out, lambda i, a: (0, 0)),
-            scratch_shapes=[pltpu.VMEM(out, F32)],
+            out_specs=[pl.BlockSpec(out, lambda i, a: (0, 0))] * 2,
+            scratch_shapes=[pltpu.VMEM((vocab // 2, width), F32)],
         ),
-        out_shape=jax.ShapeDtypeStruct(out, BF16),
-        compiler_params=pltpu.CompilerParams(vmem_limit_bytes=32 * 1024 * 1024),
+        out_shape=[jax.ShapeDtypeStruct(out, BF16)] * 2,
+        compiler_params=pltpu.CompilerParams(vmem_limit_bytes=56 * 1024 * 1024),
         cost_estimate=pl.CostEstimate(
             flops=tokens * width * vocab, bytes_accessed=9 * tokens * width, transcendentals=0
         ),
@@ -399,44 +421,48 @@
         at, embedded, context, own, oth, qkv_weight, out_weight
     )
     d_ctx = (d_ctx.astype(F32) + swap(d_ctx).astype(F32)).astype(BF16)
+    qk, vo = Stream(give_x, keep_x, "xzY"), Stream(give_z, keep_z, "zxY")
+    qk.give, vo.give, d_flat, d_ctx = lax.optimization_barrier((qk.give, vo.give, d_flat, d_ctx))
     d_ctx_far = lax.ppermute(d_ctx, "yh", SWAP)
-    qk, vo = Stream(give_x, keep_x, "xzY"), Stream(give_z, keep_z, "zxY")
     for s in (qk, vo):
         s.send()
     other = swap(d_flat)
-    d_ctx, d_ctx_far, other = together([qk, vo], d_ctx, d_ctx_far, other)
-
+    parts = table_grad(at, ids.reshape(1, tokens), own, oth, d_flat, other, vocab)
+    parts, d_ctx, d_ctx_far = together([qk, vo], parts, d_ctx, d_ctx_far)
+    rows = Stream(*parts, "yXZ")
+    streams = [qk, vo, rows]
+    rows.send()
+    for s in (qk, vo):
+        s.add()
+        s.send()
     d_ctx = jnp.where(
         yh == 0,
         jnp.concatenate([d_ctx, d_ctx_far], axis=0),
         jnp.concatenate([d_ctx_far, d_ctx], axis=0),
     )
-    ctx_part = dot(hidden, d_ctx, 0, 0).astype(BF16)
-    arrived = lax.all_to_all(ctx_part.reshape(32, 32, width), SEQ, 0, 0, tiled=False)
-    for s in (qk, vo):
+    ctx_part = dot(hidden, d_ctx, 0, 0).astype(BF16).reshape(32, 32, width)
+    (ctx_part,) = together(streams, ctx_part)
+    arrived = lax.all_to_all(ctx_part, SEQ, 0, 0, tiled=False)
+    for s in streams:
         s.add()
         s.send()
-    d_table = table_grad(at, ids.reshape(1, tokens), own, oth, d_flat, other, vocab)
-    arrived, d_table = together([qk, vo], arrived, d_table)
-
-    got_table = lax.all_to_all(d_table.reshape(64, 16, width), ALL[:4], 0, 0, tiled=False)
     ctx_sum = jnp.sum(arrived.astype(F32), axis=0).astype(BF16)
     spread = jnp.broadcast_to(ctx_sum[None], (32, 32, width))
-    for s in (qk, vo):
+    (spread,) = together(streams, spread)
+    grad_ctx = lax.all_to_all(spread, SEQ, 0, 0, tiled=False).reshape(32 * 32, width).astype(F32)
+    for s in streams:
         s.add()
         s.send()
-    got_table, spread = together([qk, vo], got_table, spread)
-
-    grad_ctx = lax.all_to_all(spread, SEQ, 0, 0, tiled=False).reshape(32 * 32, width).astype(F32)
-    grad_table = jnp.sum(got_table.astype(F32), axis=0)
-    for s in (qk, vo):
-        s.add()
-        s.send()
+    after(streams, grad_ctx[:8, :128])
     for s in (qk, vo):
         s.add()
     both = join(qk, vo)
     both.send()
+    rows.add()
+    rows.send()
     both.add()
+    rows.add()
+    grad_table = rows.total
     d_hidden = dot(d_ctx, ctx_weight, 1, 1).astype(BF16)
 
     sum_qkv, sum_out = both.total[:, : 3 * half], both.total[:, 3 * half :]

time: 208 us -> 183 us (0.88); the launches traced: 205 us -> 182 us
  waiting for transfers between devices: 57.7 us -> 46.8 us
  Pallas kernels: 39.8 us -> 33.3 us
  local copies, waits for them, and re-layouts: 11.1 us -> 7.42 us
  other arithmetic: 26.1 us -> 22.9 us
    ppermute x8 -> x10, waiting for transfers between devices: 30.6 us -> 12.2 us  [send(): lax.ppermute(self.give, RINGS[axis] + ('c',), ring_pairs(axis, self.step))]
    ppermute x3 -> x9, waiting for transfers between devices: 15.7 us -> 0.02 us  [send(): lax.ppermute(give, RINGS[axis], ring_shift(axis, shift))]
    all_to_all x1, waiting for transfers between devices: 0.01 us -> 14 us  [on_device(): lax.all_to_all(spread, SEQ, 0, 0, tiled=False).reshape(32 * 32, width)]
    all_to_all x2 -> x1, waiting for transfers between devices: 0.01 us -> 14 us  [on_device(): arrived = lax.all_to_all(ctx_part, SEQ, 0, 0, tiled=False)]
    ppermute x3 -> x9, starting transfers between devices: 4.69 us -> 15.3 us  [send(): lax.ppermute(give, RINGS[axis], ring_shift(axis, shift))]
    all_to_all x2 -> x1, starting transfers between devices: 13.5 us -> 4.78 us  [on_device(): arrived = lax.all_to_all(ctx_part, SEQ, 0, 0, tiled=False)]
    ppermute x1, waiting for transfers between devices: 8.55 us -> 0.01 us  [on_device(): d_ctx_far = lax.ppermute(d_ctx, 'yh', SWAP)]
    pallas_call x1, Pallas kernels: 32.8 us -> 24.3 us  [block(): pl.pallas_call(block_kernel, grid_spec=pltpu.PrefetchScalarGridSpec(num_s...]
  transfers between devices with their start and end apart: 23 -> 30, of which waited for: 10 -> 12; matrix products, arithmetic and copies ran while one was open for 16% -> 22% of each run, Pallas kernels for 3% -> 5%
where the time goes in v4:
time: 183 us; the launch traced here: 182 us
  starting transfers between devices  54.7 us (30%)
  waiting for transfers between devices  46.8 us (26%)
  Pallas kernels  33.3 us (18%)
  other arithmetic  22.9 us (13%)
  matrix products  15.8 us (9%)
  local copies, waits for them, and re-layouts  7.42 us (4%)
    pallas_call x1, Pallas kernels, block(): pl.pallas_call(block_kernel, grid_spec=pltpu.PrefetchScalarGridSpec(num_s...  24.3 us
    dot_general x4, matrix products, dot(): lax.dot_general(a, b, (((ca,), (cb,)), ((), ())), preferred_element_type=...  15.8 us
    ppermute x10, starting transfers between devices, send(): lax.ppermute(self.give, RINGS[axis] + ('c',), ring_pairs(axis, self.step))  15.4 us
    ppermute x9, starting transfers between devices, send(): lax.ppermute(give, RINGS[axis], ring_shift(axis, shift))  15.3 us
    all_to_all x1, waiting for transfers between devices, on_device(): lax.all_to_all(spread, SEQ, 0, 0, tiled=False).reshape(32 * 32, width)  14 us
    all_to_all x1, waiting for transfers between devices, on_device(): arrived = lax.all_to_all(ctx_part, SEQ, 0, 0, tiled=False)  14 us
    ppermute x10, waiting for transfers between devices, send(): lax.ppermute(self.give, RINGS[axis] + ('c',), ring_pairs(axis, self.step))  12.2 us
    all_to_all x1, starting transfers between devices, on_device(): lax.all_to_all(spread, SEQ, 0, 0, tiled=False).reshape(32 * 32, width)  9.64 us
  transfers between devices with their start and end apart: 30, of which 12 were waited for; matrix products, arithmetic and copies ran while one was open for 22% of the time, Pallas kernels for 5%

profile of v4, /device:TPU:1, one launch (start us, length us, event | category | flops | bytes accessed | tf_op | source)
XLA Modules:
  0.0 182.2 jit_solution(16301267406857530711)
XLA Ops:
  0.7 1.5 collective-permute-start.1
  2.2 0.4 copy-done
  2.5 1.7 convolution_convert_fusion.2
  4.3 3.8 %collective-permute-start = (bf16[128,1024]{1,0:T(8,128)(2,1)S(1)}, bf16[128,1024]{1,0:T(8,128)(2,1)}, u32[]{:S(2)}, u32[]{:S(2)}) collective-permute-start(bf16[128,1024]{1,0:T(8,128)(2,1)S(1)} %dynamic-slice_bitcast_fusion), channel_id=1, source_target_pairs={{0,2},{2,0},{1,3},{3,1},{4,6},{6,4},{5,7},{7,5},{8,10},{10,8},{9,1... | collective-permute-start | bytes 786440 | tf_op jit(solution)/shard_map/ppermute | solution.py:406
  8.2 1.0 collective-permute-start.2
  9.4 8.1 %fusion.2.emb_ref = bf16[1024,1024]{1,0:T(8,128)(2,1)} fusion(bf16[2048,1024]{1,0:T(8,128)(2,1)} %param.10, s32[1024]{0:T(1024)S(1)} %eq.49), kind=kOutput, calls=%fused_computation.4 | convolution fusion | flops 4298113024 | bytes 6295552 | tf_op jit(solution)/shard_map/dot_general | solution.py:28
  17.5 1.0 fusion.3
  18.9 1.2 collective-permute-done.3
  20.4 1.2 copy-done.5
  21.6 24.3 %shard_map.110 = (bf16[1024,1024]{1,0:T(8,128)(2,1)}, bf16[128,1024]{1,0:T(8,128)(2,1)S(1)}, bf16[512,1024]{1,0:T(8,128)(2,1)}, bf16[512,1024]{1,0:T(8,128)(2,1)...) custom-call(s32[13]{0:T(128)S(1)} %stack.55.at_ref, bf16[1024,1024]{1,0:T(8,128)(2,1)} %fusion.2.emb_ref, ...), custom_call_target="tpu_custom_call" | custom-call | flops 11811160064 | bytes 20971520 | tf_op jit(solution)/shard_map/pallas_call | solution.py:297
  45.9 1.0 copy-done.1
  46.8 0.2 collective-permute-start.4
  47.0 1.4 collective-permute-done.4
  48.4 0.2 collective-permute-start.7
  48.7 2.5 %collective-permute-start.5 = (bf16[512,1024]{1,0:T(8,128)(2,1)}, bf16[512,1024]{1,0:T(8,128)(2,1)}, u32[]{:S(2)}, u32[]{:S(2)}) collective-permute-start(bf16[512,1024]{1,0:T(8,128)(2,1)} %get-tuple-element.46), channel_id=1, source_target_pairs={{0,4},{1,13},{4,0},{5,9},{8,12},{9,5},{12,8},{13,1},{2,6},{3,15},{... | collective-permute-start | bytes 3145736 | tf_op jit(solution)/shard_map/ppermute | solution.py:153
  51.2 3.8 %collective-permute-start.6 = (bf16[512,1024]{1,0:T(8,128)(2,1)}, bf16[512,1024]{1,0:T(8,128)(2,1)}, u32[]{:S(2)}, u32[]{:S(2)}) collective-permute-start(bf16[512,1024]{1,0:T(8,128)(2,1)} %get-tuple-element.47), channel_id=1, source_target_pairs={{0,32},{1,97},{32,0},{33,65},{64,96},{65,33},{96,64},{97,1},{2,34}... | collective-permute-start | bytes 3145736 | tf_op jit(solution)/shard_map/ppermute | solution.py:153
  54.9 0.8 collective-permute-start.8
  55.7 0.7 reshape_reshape.3.ids_ref
  56.4 9.0 %shard_map.111 = (bf16[512,1024]{1,0:T(8,128)(2,1)}, bf16[512,1024]{1,0:T(8,128)(2,1)}) custom-call(s32[13]{0:T(128)} %copy-done.3, s32[1,1024]{1,0:T(1,128)} %reshape_reshape.3.ids_ref, bf16[512,1024]{1,0:T(8,128)(2,1)} %bitcast.79, bf16[512,1024]{1,0:T(8,128)(2,1)} %collective-permute-done.2.oth_ref, bf16[1024,1024]{1,0:T(8,128)(2,1)} %get-tuple-element.48.mine_ref, ...), custom_call_target="tpu_custom_call" | custom-call | flops 2147483648 | bytes 9437184 | tf_op jit(solution)/shard_map/pallas_call | solution.py:371
  65.4 2.0 %collective-permute-done.6 = bf16[512,1024]{1,0:T(8,128)(2,1)} collective-permute-done((bf16[512,1024]{1,0:T(8,128)(2,1)}, bf16[512,1024]{1,0:T(8,128)(2,1)}, u32[]{:S(2)}, u32[]{:S(2)}) %collective-permute-start.6) | collective-permute-done | bytes 1048608 | tf_op jit(solution)/shard_map/ppermute | solution.py:153
  67.4 0.8 collective-permute-start.11
  68.2 2.0 %add_convert_fusion.6 = bf16[256,1024]{1,0:T(8,128)(2,1)} fusion(bf16[512,1024]{1,0:T(8,128)(2,1)} %collective-permute-done.6, bf16[512,1024]{1,0:T(8,128)(2,1)S(1)} %copy-done.2), kind=kLoop, calls=%fused_computation.14 | loop fusion | flops 1048576 | bytes 1572864 | tf_op jit(solution)/shard_map/convert_element_type | solution.py:166
  70.2 2.0 %add_convert_fusion.7 = bf16[256,1024]{1,0:T(8,128)(2,1)} fusion(bf16[512,1024]{1,0:T(8,128)(2,1)} %collective-permute-done.5, bf16[512,1024]{1,0:T(8,128)(2,1)S(1)} %get-tuple-element.54), kind=kLoop, calls=%fused_computation.15 | loop fusion | flops 1048576 | bytes 1572864 | tf_op jit(solution)/shard_map/convert_element_type | solution.py:166
  72.3 3.3 %convolution_convert_fusion = bf16[1024,1024]{0,1:T(8,128)(2,1)} fusion(bf16[256,1024]{1,0:T(8,128)(2,1)} %param.7, bf16[128,1024]{1,0:T(8,128)(2,1)} %collective-permute-done.8, bf16[128,1024]{1,0:T(8,128)(2,1)S(1)} %add_convert_fusion.9, pred[]{:T(512)S(6)} %eq.47), kind=kOutput, calls=%fused_computation.5 | convolution fusion | flops 540278784 | bytes 3145729 | tf_op jit(solution)/shard_map/dot_general | solution.py:28
  75.6 3.3 %collective-permute-done.10 = bf16[256,1024]{1,0:T(8,128)(2,1)} collective-permute-done((bf16[256,1024]{1,0:T(8,128)(2,1)}, bf16[256,1024]{1,0:T(8,128)(2,1)}, u32[]{:S(2)}, u32[]{:S(2)}) %collective-permute-start.10) | collective-permute-done | bytes 524320 | tf_op jit(solution)/shard_map/ppermute | solution.py:153
  78.9 2.0 %collective-permute-done.9 = bf16[256,1024]{1,0:T(8,128)(2,1)} collective-permute-done((bf16[256,1024]{1,0:T(8,128)(2,1)}, bf16[256,1024]{1,0:T(8,128)(2,1)}, u32[]{:S(2)}, u32[]{:S(2)}) %collective-permute-start.9) | collective-permute-done | bytes 524320 | tf_op jit(solution)/shard_map/ppermute | solution.py:153
  80.9 2.0 %collective-permute-done.11 = bf16[512,1024]{1,0:T(8,128)(2,1)} collective-permute-done((bf16[512,1024]{1,0:T(8,128)(2,1)}, bf16[512,1024]{1,0:T(8,128)(2,1)}, u32[]{:S(2)}, u32[]{:S(2)}) %collective-permute-start.11) | collective-permute-done | bytes 1048608 | tf_op jit(solution)/shard_map/ppermute | solution.py:153
  82.9 4.8 %all-to-all-start = ((bf16[32,32,1024]{2,1,0:T(8,128)(2,1)}), bf16[32,32,1024]{2,1,0:T(8,128)(2,1)}, u32[]{:S(2)}, u32[]{:S(2)}) async-start(bf16[32,32,1024]{2,1,0:T(8,128)(2,1)} %bitcast.82), calls=%async_computation | async-start | bytes 4194304 | tf_op jit(solution)/shard_map/all_to_all | solution.py:445
  87.7 2.2 %add_convert_fusion.2 = bf16[256,1024]{1,0:T(8,128)(2,1)} fusion(bf16[512,1024]{1,0:T(8,128)(2,1)} %collective-permute-done.11, bf16[512,1024]{1,0:T(8,128)(2,1)} %get-tuple-element.61), kind=kLoop, calls=%fused_computation.10 | loop fusion | flops 1048576 | bytes 1572864 | tf_op jit(solution)/shard_map/convert_element_type | solution.py:166
  89.9 1.1 collective-permute-start.14
  91.0 2.3 %add_convert_fusion.3 = (bf16[256,1024]{1,0:T(8,128)(2,1)S(1)}, bf16[256,1024]{1,0:T(8,128)(2,1)S(1)}) fusion(bf16[256,1024]{1,0:T(8,128)(2,1)} %collective-permute-done.10, bf16[512,1024]{1,0:T(8,128)(2,1)} %collective-permute-done.6, bf16[512,1024]{1,0:T(8,128)(2,1)} %copy-done.1, bf16[256,1024]{1,0:T(8,128)(2,1)} %collective-permute-done.9, ...), kind=kLoop, calls=%fused_computation.11 | loop fusion | flops 4194304 | bytes 4194304 | tf_op jit(solution)/shard_map/convert_element_type | solution.py:174
  93.3 0.7 pad_maximum_fusion.1
  94.0 2.4 %collective-permute-start.13 = (bf16[128,1024]{1,0:T(8,128)(2,1)}, bf16[128,1024]{1,0:T(8,128)(2,1)S(1)}, u32[]{:S(2)}, u32[]{:S(2)}) collective-permute-start(bf16[128,1024]{1,0:T(8,128)(2,1)} %pad_maximum_fusion.1), channel_id=1, source_target_pairs={{0,4},{1,13},{4,0},{5,9},{8,12},{9,5},{12,8},{13,1},{2,6},{3,15},{... | collective-permute-start | bytes 786440 | tf_op jit(solution)/shard_map/ppermute | solution.py:153
  96.5 0.7 pad_maximum_fusion
  97.2 2.6 %collective-permute-start.12 = (bf16[128,1024]{1,0:T(8,128)(2,1)}, bf16[128,1024]{1,0:T(8,128)(2,1)S(1)}, u32[]{:S(2)}, u32[]{:S(2)}) collective-permute-start(bf16[128,1024]{1,0:T(8,128)(2,1)} %pad_maximum_fusion), channel_id=1, source_target_pairs={{0,32},{1,97},{32,0},{33,65},{64,96},{65,33},{96,64},{97,1},{2,34}... | collective-permute-start | bytes 786440 | tf_op jit(solution)/shard_map/ppermute | solution.py:153
  99.8 14.0 %all-to-all-done = bf16[32,32,1024]{2,1,0:T(8,128)(2,1)} async-done(((bf16[32,32,1024]{2,1,0:T(8,128)(2,1)}), bf16[32,32,1024]{2,1,0:T(8,128)(2,1)}, u32[]{:S(2)}, u32[]{:S(2)}) %all-to-all-start) | async-done | bytes 2097184 | tf_op jit(solution)/shard_map/all_to_all | solution.py:445
  113.8 2.0 %reduce_sum.12 = bf16[32,1024]{1,0:T(8,128)(2,1)S(1)} reduce(bf16[32,32,1024]{2,1,0:T(8,128)(2,1)} %all-to-all-done, bf16[]{:T(256)} %constant.261.clone.1), dimensions={0}, to_apply=%region_0.1 | reduce | flops 1015808 | bytes 2162690 | tf_op jit(solution)/shard_map/reduce_sum | solution.py:449
  115.7 0.9 collective-permute-done.13
  116.7 1.9 %collective-permute-done.14 = bf16[256,1024]{1,0:T(8,128)(2,1)} collective-permute-done((bf16[256,1024]{1,0:T(8,128)(2,1)}, bf16[256,1024]{1,0:T(8,128)(2,1)}, u32[]{:S(2)}, u32[]{:S(2)}) %collective-permute-start.14) | collective-permute-done | bytes 524320 | tf_op jit(solution)/shard_map/ppermute | solution.py:153
  118.6 1.6 broadcast_in_dim.2
  120.2 9.6 %all-to-all-start.1 = ((bf16[32,32,1024]{2,1,0:T(8,128)(2,1)}), bf16[32,32,1024]{2,1,0:T(8,128)(2,1)}, u32[]{:S(2)}, u32[]{:S(2)}) async-start(bf16[32,32,1024]{2,1,0:T(8,128)(2,1)} %broadcast_in_dim.2), calls=%async_computation.1 | async-start | bytes 4194304 | tf_op jit(solution)/shard_map/all_to_all | solution.py:452
  130.0 2.7 %convolution_convert_fusion.1 = bf16[256,1024]{1,0:T(8,128)(2,1)} fusion(bf16[1024,1024]{1,0:T(8,128)(2,1)S(1)} %copy-done, bf16[128,1024]{1,0:T(8,128)(2,1)} %collective-permute-done.8, bf16[128,1024]{1,0:T(8,128)(2,1)S(1)} %add_convert_fusion.9, pred[]{:T(512)S(6)} %eq.47), kind=kOutput, calls=%fused_computation.6 | convolution fusion | flops 539492352 | bytes 3145729 | tf_op jit(solution)/shard_map/dot_general | solution.py:28
  132.7 0.7 fusion.6
  133.4 1.2 collective-permute-start.21
  134.5 0.7 fusion.4
  135.2 1.2 collective-permute-start.22
  136.4 1.5 add_convert_fusion
  137.9 0.8 constant_dynamic-slice_fusion.9
  138.7 2.4 %collective-permute-start.15 = (bf16[64,1024]{1,0:T(8,128)(2,1)}, bf16[64,1024]{1,0:T(8,128)(2,1)S(1)}, u32[]{:S(2)}, u32[]{:S(2)}) collective-permute-start(bf16[64,1024]{1,0:T(8,128)(2,1)} %bitcast.28), channel_id=1, source_target_pairs={{0,8},{4,12},{8,0},{12,4},{1,9},{5,13},{9,1},{13,5},{2,10},{6,14},... | collective-permute-start | bytes 393224 | tf_op jit(solution)/shard_map/ppermute | solution.py:157
  141.1 2.7 %collective-permute-start.17 = (bf16[64,1024]{1,0:T(8,128)(2,1)}, bf16[64,1024]{1,0:T(8,128)(2,1)S(1)}, u32[]{:S(2)}, u32[]{:S(2)}) collective-permute-start(bf16[64,1024]{1,0:T(8,128)(2,1)} %bitcast.30), channel_id=1, source_target_pairs={{0,12},{4,0},{8,4},{12,8},{1,13},{5,1},{9,5},{13,9},{2,14},{6,2},{... | collective-permute-start | bytes 393224 | tf_op jit(solution)/shard_map/ppermute | solution.py:157
  143.7 14.0 %all-to-all-done.1 = bf16[32,32,1024]{2,1,0:T(8,128)(2,1)} async-done(((bf16[32,32,1024]{2,1,0:T(8,128)(2,1)}), bf16[32,32,1024]{2,1,0:T(8,128)(2,1)}, u32[]{:S(2)}, u32[]{:S(2)}) %all-to-all-start.1) | async-done | bytes 2097184 | tf_op jit(solution)/shard_map/all_to_all | solution.py:452
  157.7 4.1 %bitcast_convert_fusion = f32[1024,1024]{1,0:T(8,128)} fusion(bf16[32,32,1024]{2,1,0:T(8,128)(2,1)} %all-to-all-done.1), kind=kLoop, calls=%fused_computation.3 | loop fusion | flops 1048576 | bytes 6291456 | tf_op jit(solution)/shard_map/convert_element_type | solution.py:452
  161.8 1.0 add_convert_fusion.12
  162.8 1.0 add_convert_fusion.11
  163.8 2.6 %collective-permute-start.23 = (bf16[16,2048]{1,0:T(8,128)(2,1)S(1)}, bf16[16,2048]{1,0:T(8,128)(2,1)S(1)}, u32[]{:S(2)}, u32[]{:S(2)}) collective-permute-start(bf16[16,2048]{1,0:T(8,128)(2,1)S(1)} %get-tuple-element.85), channel_id=1, source_target_pairs={{0,2},{16,18},{2,0},{18,16},{1,3},{17,19},{3,1},{19,17},{4,6},{20,... | collective-permute-start | bytes 196616 | tf_op jit(solution)/shard_map/ppermute | solution.py:157
  166.4 0.4 collective-permute-start.24
  166.8 2.3 %collective-permute-start.25 = (bf16[16,2048]{1,0:T(8,128)(2,1)S(1)}, bf16[16,2048]{1,0:T(8,128)(2,1)S(1)}, u32[]{:S(2)}, u32[]{:S(2)}) collective-permute-start(bf16[16,2048]{1,0:T(8,128)(2,1)S(1)} %get-tuple-element.86), channel_id=1, source_target_pairs={{0,18},{16,0},{2,16},{18,2},{1,19},{17,1},{3,17},{19,3},{4,22},{20... | collective-permute-start | bytes 196616 | tf_op jit(solution)/shard_map/ppermute | solution.py:157
  169.2 2.2 %collective-permute-start.18 = (bf16[16,1024]{1,0:T(8,128)(2,1)S(1)}, bf16[16,1024]{1,0:T(8,128)(2,1)S(1)}, u32[]{:S(2)}, u32[]{:S(2)}) collective-permute-start(bf16[16,1024]{1,0:T(8,128)(2,1)S(1)} %get-tuple-element.92), channel_id=1, source_target_pairs={{0,64},{32,96},{64,0},{96,32},{1,65},{33,97},{65,1},{97,33},{2,66}... | collective-permute-start | bytes 98312 | tf_op jit(solution)/shard_map/ppermute | solution.py:157
  171.4 2.7 %collective-permute-start.20 = (bf16[16,1024]{1,0:T(8,128)(2,1)S(1)}, bf16[16,1024]{1,0:T(8,128)(2,1)S(1)}, u32[]{:S(2)}, u32[]{:S(2)}) collective-permute-start(bf16[16,1024]{1,0:T(8,128)(2,1)S(1)} %get-tuple-element.93), channel_id=1, source_target_pairs={{0,96},{32,0},{64,32},{96,64},{1,97},{33,1},{65,33},{97,65},{2,98}... | collective-permute-start | bytes 98312 | tf_op jit(solution)/shard_map/ppermute | solution.py:157
  174.2 1.9 %collective-permute-start.27 = (f32[8,1024]{1,0:T(8,128)S(1)}, f32[8,1024]{1,0:T(8,128)S(1)}, u32[]{:S(2)}, u32[]{:S(2)}) collective-permute-start(f32[8,1024]{1,0:T(8,128)S(1)} %pad_maximum_fusion.3), channel_id=1, source_target_pairs={{0,0},{1,64},{32,32},{33,96},{64,1},{65,65},{96,33},{97,97},{2,2},... | collective-permute-start | bytes 98312 | tf_op jit(solution)/shard_map/ppermute | solution.py:470
  176.3 0.7 fusion.14
  176.9 4.0 %collective-permute-done.27 = f32[8,1024]{1,0:T(8,128)S(1)} collective-permute-done((f32[8,1024]{1,0:T(8,128)S(1)}, f32[8,1024]{1,0:T(8,128)S(1)}, u32[]{:S(2)}, u32[]{:S(2)}) %collective-permute-start.27) | collective-permute-done | bytes 32800 | tf_op jit(solution)/shard_map/ppermute | solution.py:470
  181.0 0.6 copy.16
  181.6 0.6 copy.18
  (63 shorter events, 1.3 us)
Async XLA Ops:
  0.6 1.9 %copy-start = (bf16[1024,1024]{1,0:T(8,128)(2,1)S(1)}, bf16[1024,1024]{1,0:T(8,128)(2,1)}, u32[]{:S(2)}) copy-start(bf16[1024,1024]{1,0:T(8,128)(2,1)} %param.8) | copy-start | bytes 6291460
  0.6 8.5 %copy-start.9 = (s32[64,8]{0,1:T(8,128)S(1)}, s32[64,8]{0,1:T(8,128)}, u32[]{:S(2)}) copy-start(s32[64,8]{0,1:T(8,128)} %param.9) | copy-start | bytes 6148
  0.7 7.5 %copy-start.4 = (bf16[64,8,1024]{2,1,0:T(8,128)(2,1)S(1)}, bf16[64,8,1024]{2,1,0:T(8,128)(2,1)}, u32[]{:S(2)}) copy-start(bf16[64,8,1024]{2,1,0:T(8,128)(2,1)} %param.13) | copy-start | bytes 3145732
  0.7 8.5 %collective-permute-start.1 = (s32[64,8]{0,1:T(8,128)}, s32[64,8]{0,1:T(8,128)S(1)}, u32[]{:S(2)}, u32[]{:S(2)}) collective-permute-start(s32[64,8]{0,1:T(8,128)} %param.9), channel_id=1, source_target_pairs={{0,1},{1,0},{2,3},{3,2},{4,5},{5,4},{6,7},{7,6},{8,9},{9,8},{10,11... | collective-permute-start | bytes 6152 | tf_op jit(solution)/shard_map/ppermute | solution.py:409
  4.3 3.9 %copy-start.7 = (bf16[256,1024]{1,0:T(8,128)(2,1)}, bf16[256,1024]{1,0:T(8,128)(2,1)S(1)}, u32[]{:S(2)}) copy-start(bf16[256,1024]{1,0:T(8,128)(2,1)S(1)} %convolution_convert_fusion.2) | copy-start | bytes 1572868
  4.3 13.2 %collective-permute-start = (bf16[128,1024]{1,0:T(8,128)(2,1)S(1)}, bf16[128,1024]{1,0:T(8,128)(2,1)}, u32[]{:S(2)}, u32[]{:S(2)}) collective-permute-start(bf16[128,1024]{1,0:T(8,128)(2,1)S(1)} %dynamic-slice_bitcast_fusion), channel_id=1, source_target_pairs={{0,2},{2,0},{1,3},{3,1},{4,6},{6,4},{5,7},{7,5},{8,10},{10,8},{9,1... | collective-permute-start | bytes 786440 | tf_op jit(solution)/shard_map/ppermute | solution.py:406
  8.2 9.4 %collective-permute-start.2 = (bf16[512,1024]{1,0:T(8,128)(2,1)S(1)}, bf16[512,1024]{1,0:T(8,128)(2,1)}, u32[]{:S(2)}, u32[]{:S(2)}) collective-permute-start(bf16[512,1024]{1,0:T(8,128)(2,1)S(1)} %bitcast.80), channel_id=1, source_target_pairs={{0,1},{1,0},{2,3},{3,2},{4,5},{5,4},{6,7},{7,6},{8,9},{9,8},{10,11... | collective-permute-start | bytes 3145736 | tf_op jit(solution)/shard_map/ppermute | solution.py:411
  9.4 8.1 %copy-start.8 = (bf16[256,1024]{1,0:T(8,128)(2,1)S(1)}, bf16[256,1024]{1,0:T(8,128)(2,1)}, u32[]{:S(2)}) copy-start(bf16[256,1024]{1,0:T(8,128)(2,1)} %copy-done.7) | copy-start | bytes 1572868
  18.6 1.6 collective-permute-start.3
  18.9 26.9 %copy-start.3 = (s32[13]{0:T(128)}, s32[13]{0:T(128)S(1)}, u32[]{:S(2)}) copy-start(s32[13]{0:T(128)S(1)} %stack.55.at_ref) | copy-start | bytes 160
  20.4 1.2 copy-start.5
  45.9 1.0 copy-start.1
  46.8 1.5 collective-permute-start.4
  48.4 8.0 %collective-permute-start.7 = (bf16[1024,1024]{1,0:T(8,128)(2,1)}, bf16[1024,1024]{1,0:T(8,128)(2,1)}, u32[]{:S(2)}, u32[]{:S(2)}) collective-permute-start(bf16[1024,1024]{1,0:T(8,128)(2,1)} %get-tuple-element.48.mine_ref), channel_id=1, source_target_pairs={{0,1},{1,0},{2,3},{3,2},{4,5},{5,4},{6,7},{7,6},{8,9},{9,8},{10,11... | collective-permute-start | bytes 6291464 | tf_op jit(solution)/shard_map/ppermute | solution.py:429
  48.7 16.8 %collective-permute-start.5 = (bf16[512,1024]{1,0:T(8,128)(2,1)}, bf16[512,1024]{1,0:T(8,128)(2,1)}, u32[]{:S(2)}, u32[]{:S(2)}) collective-permute-start(bf16[512,1024]{1,0:T(8,128)(2,1)} %get-tuple-element.46), channel_id=1, source_target_pairs={{0,4},{1,13},{4,0},{5,9},{8,12},{9,5},{12,8},{13,1},{2,6},{3,15},{... | collective-permute-start | bytes 3145736 | tf_op jit(solution)/shard_map/ppermute | solution.py:153
  51.2 16.3 %collective-permute-start.6 = (bf16[512,1024]{1,0:T(8,128)(2,1)}, bf16[512,1024]{1,0:T(8,128)(2,1)}, u32[]{:S(2)}, u32[]{:S(2)}) collective-permute-start(bf16[512,1024]{1,0:T(8,128)(2,1)} %get-tuple-element.47), channel_id=1, source_target_pairs={{0,32},{1,97},{32,0},{33,65},{64,96},{65,33},{96,64},{97,1},{2,34}... | collective-permute-start | bytes 3145736 | tf_op jit(solution)/shard_map/ppermute | solution.py:153
  54.9 10.5 %collective-permute-start.8 = (bf16[128,1024]{1,0:T(8,128)(2,1)S(1)}, bf16[128,1024]{1,0:T(8,128)(2,1)}, u32[]{:S(2)}, u32[]{:S(2)}) collective-permute-start(bf16[128,1024]{1,0:T(8,128)(2,1)S(1)} %add_convert_fusion.9), channel_id=1, source_target_pairs={{0,2},{2,0},{1,3},{3,1},{4,6},{6,4},{5,7},{7,5},{8,10},{10,8},{9,1... | collective-permute-start | bytes 786440 | tf_op jit(solution)/shard_map/ppermute | solution.py:426
  56.4 11.8 %copy-start.2 = (bf16[512,1024]{1,0:T(8,128)(2,1)S(1)}, bf16[512,1024]{1,0:T(8,128)(2,1)}, u32[]{:S(2)}) copy-start(bf16[512,1024]{1,0:T(8,128)(2,1)} %copy-done.1) | copy-start | bytes 3145732
  67.4 15.5 %collective-permute-start.11 = (bf16[512,1024]{1,0:T(8,128)(2,1)}, bf16[512,1024]{1,0:T(8,128)(2,1)}, u32[]{:S(2)}, u32[]{:S(2)}) collective-permute-start(bf16[512,1024]{1,0:T(8,128)(2,1)} %get-tuple-element.58), channel_id=1, source_target_pairs={{0,16},{1,19},{16,0},{17,3},{2,18},{3,17},{18,2},{19,1},{4,20},{5,... | collective-permute-start | bytes 3145736 | tf_op jit(solution)/shard_map/ppermute | solution.py:153
  70.2 8.6 %collective-permute-start.10 = (bf16[256,1024]{1,0:T(8,128)(2,1)}, bf16[256,1024]{1,0:T(8,128)(2,1)}, u32[]{:S(2)}, u32[]{:S(2)}) collective-permute-start(bf16[256,1024]{1,0:T(8,128)(2,1)} %add_convert_fusion.6), channel_id=1, source_target_pairs={{0,96},{1,33},{32,64},{33,1},{64,32},{65,97},{96,0},{97,65},{2,98}... | collective-permute-start | bytes 1572872 | tf_op jit(solution)/shard_map/ppermute | solution.py:153
  72.3 8.6 %collective-permute-start.9 = (bf16[256,1024]{1,0:T(8,128)(2,1)}, bf16[256,1024]{1,0:T(8,128)(2,1)}, u32[]{:S(2)}, u32[]{:S(2)}) collective-permute-start(bf16[256,1024]{1,0:T(8,128)(2,1)} %add_convert_fusion.7), channel_id=1, source_target_pairs={{0,12},{1,5},{4,8},{5,1},{8,4},{9,13},{12,0},{13,9},{2,14},{3,7},{... | collective-permute-start | bytes 1572872 | tf_op jit(solution)/shard_map/ppermute | solution.py:153
  82.9 30.9 %all-to-all-start = ((bf16[32,32,1024]{2,1,0:T(8,128)(2,1)}), bf16[32,32,1024]{2,1,0:T(8,128)(2,1)}, u32[]{:S(2)}, u32[]{:S(2)}) async-start(bf16[32,32,1024]{2,1,0:T(8,128)(2,1)} %bitcast.82), calls=%async_computation | async-start | bytes 4194304 | tf_op jit(solution)/shard_map/all_to_all | solution.py:445
  89.9 28.7 %collective-permute-start.14 = (bf16[256,1024]{1,0:T(8,128)(2,1)}, bf16[256,1024]{1,0:T(8,128)(2,1)}, u32[]{:S(2)}, u32[]{:S(2)}) collective-permute-start(bf16[256,1024]{1,0:T(8,128)(2,1)} %add_convert_fusion.2), channel_id=1, source_target_pairs={{0,18},{1,17},{16,2},{17,1},{2,16},{3,19},{18,0},{19,3},{4,22},{5,... | collective-permute-start | bytes 1572872 | tf_op jit(solution)/shard_map/ppermute | solution.py:153
  94.0 22.6 %collective-permute-start.13 = (bf16[128,1024]{1,0:T(8,128)(2,1)}, bf16[128,1024]{1,0:T(8,128)(2,1)S(1)}, u32[]{:S(2)}, u32[]{:S(2)}) collective-permute-start(bf16[128,1024]{1,0:T(8,128)(2,1)} %pad_maximum_fusion.1), channel_id=1, source_target_pairs={{0,4},{1,13},{4,0},{5,9},{8,12},{9,5},{12,8},{13,1},{2,6},{3,15},{... | collective-permute-start | bytes 786440 | tf_op jit(solution)/shard_map/ppermute | solution.py:153
  97.2 19.5 %collective-permute-start.12 = (bf16[128,1024]{1,0:T(8,128)(2,1)}, bf16[128,1024]{1,0:T(8,128)(2,1)S(1)}, u32[]{:S(2)}, u32[]{:S(2)}) collective-permute-start(bf16[128,1024]{1,0:T(8,128)(2,1)} %pad_maximum_fusion), channel_id=1, source_target_pairs={{0,32},{1,97},{32,0},{33,65},{64,96},{65,33},{96,64},{97,1},{2,34}... | collective-permute-start | bytes 786440 | tf_op jit(solution)/shard_map/ppermute | solution.py:153
  120.2 37.6 %all-to-all-start.1 = ((bf16[32,32,1024]{2,1,0:T(8,128)(2,1)}), bf16[32,32,1024]{2,1,0:T(8,128)(2,1)}, u32[]{:S(2)}, u32[]{:S(2)}) async-start(bf16[32,32,1024]{2,1,0:T(8,128)(2,1)} %broadcast_in_dim.2), calls=%async_computation.1 | async-start | bytes 4194304 | tf_op jit(solution)/shard_map/all_to_all | solution.py:452
  130.0 6.4 %copy-start.6 = (bf16[512,1024]{1,0:T(8,128)(2,1)S(1)}, bf16[512,1024]{1,0:T(8,128)(2,1)}, u32[]{:S(2)}) copy-start(bf16[512,1024]{1,0:T(8,128)(2,1)} %get-tuple-element.61) | copy-start | bytes 3145732
  133.4 28.4 %collective-permute-start.21 = (bf16[64,1024]{1,0:T(8,128)(2,1)}, bf16[64,1024]{1,0:T(8,128)(2,1)}, u32[]{:S(2)}, u32[]{:S(2)}) collective-permute-start(bf16[64,1024]{1,0:T(8,128)(2,1)} %fusion.6), channel_id=1, source_target_pairs={{0,96},{1,33},{32,64},{33,1},{64,32},{65,97},{96,0},{97,65},{2,98}... | collective-permute-start | bytes 393224 | tf_op jit(solution)/shard_map/ppermute | solution.py:153
  135.2 26.6 %collective-permute-start.22 = (bf16[64,1024]{1,0:T(8,128)(2,1)}, bf16[64,1024]{1,0:T(8,128)(2,1)}, u32[]{:S(2)}, u32[]{:S(2)}) collective-permute-start(bf16[64,1024]{1,0:T(8,128)(2,1)} %fusion.4), channel_id=1, source_target_pairs={{0,12},{1,5},{4,8},{5,1},{8,4},{9,13},{12,0},{13,9},{2,14},{3,7},{... | collective-permute-start | bytes 393224 | tf_op jit(solution)/shard_map/ppermute | solution.py:153
  138.7 28.1 %collective-permute-start.15 = (bf16[64,1024]{1,0:T(8,128)(2,1)}, bf16[64,1024]{1,0:T(8,128)(2,1)S(1)}, u32[]{:S(2)}, u32[]{:S(2)}) collective-permute-start(bf16[64,1024]{1,0:T(8,128)(2,1)} %bitcast.28), channel_id=1, source_target_pairs={{0,8},{4,12},{8,0},{12,4},{1,9},{5,13},{9,1},{13,5},{2,10},{6,14},... | collective-permute-start | bytes 393224 | tf_op jit(solution)/shard_map/ppermute | solution.py:157
  141.1 28.0 %collective-permute-start.16 = (bf16[64,1024]{1,0:T(8,128)(2,1)}, bf16[64,1024]{1,0:T(8,128)(2,1)S(1)}, u32[]{:S(2)}, u32[]{:S(2)}) collective-permute-start(bf16[64,1024]{1,0:T(8,128)(2,1)} %bitcast.29), channel_id=1, source_target_pairs={{0,4},{4,8},{8,12},{12,0},{1,5},{5,9},{9,13},{13,1},{2,6},{6,10},{... | collective-permute-start | bytes 393224 | tf_op jit(solution)/shard_map/ppermute | solution.py:157
  141.1 28.0 %collective-permute-start.17 = (bf16[64,1024]{1,0:T(8,128)(2,1)}, bf16[64,1024]{1,0:T(8,128)(2,1)S(1)}, u32[]{:S(2)}, u32[]{:S(2)}) collective-permute-start(bf16[64,1024]{1,0:T(8,128)(2,1)} %bitcast.30), channel_id=1, source_target_pairs={{0,12},{4,0},{8,4},{12,8},{1,13},{5,1},{9,5},{13,9},{2,14},{6,2},{... | collective-permute-start | bytes 393224 | tf_op jit(solution)/shard_map/ppermute | solution.py:157
  163.8 7.6 %collective-permute-start.23 = (bf16[16,2048]{1,0:T(8,128)(2,1)S(1)}, bf16[16,2048]{1,0:T(8,128)(2,1)S(1)}, u32[]{:S(2)}, u32[]{:S(2)}) collective-permute-start(bf16[16,2048]{1,0:T(8,128)(2,1)S(1)} %get-tuple-element.85), channel_id=1, source_target_pairs={{0,2},{16,18},{2,0},{18,16},{1,3},{17,19},{3,1},{19,17},{4,6},{20,... | collective-permute-start | bytes 196616 | tf_op jit(solution)/shard_map/ppermute | solution.py:157
  166.4 7.7 %collective-permute-start.24 = (bf16[16,2048]{1,0:T(8,128)(2,1)S(1)}, bf16[16,2048]{1,0:T(8,128)(2,1)S(1)}, u32[]{:S(2)}, u32[]{:S(2)}) collective-permute-start(bf16[16,2048]{1,0:T(8,128)(2,1)S(1)} %get-tuple-element.87), channel_id=1, source_target_pairs={{0,16},{16,2},{2,18},{18,0},{1,17},{17,3},{3,19},{19,1},{4,20},{20... | collective-permute-start | bytes 196616 | tf_op jit(solution)/shard_map/ppermute | solution.py:157
  166.8 7.3 %collective-permute-start.25 = (bf16[16,2048]{1,0:T(8,128)(2,1)S(1)}, bf16[16,2048]{1,0:T(8,128)(2,1)S(1)}, u32[]{:S(2)}, u32[]{:S(2)}) collective-permute-start(bf16[16,2048]{1,0:T(8,128)(2,1)S(1)} %get-tuple-element.86), channel_id=1, source_target_pairs={{0,18},{16,0},{2,16},{18,2},{1,19},{17,1},{3,17},{19,3},{4,22},{20... | collective-permute-start | bytes 196616 | tf_op jit(solution)/shard_map/ppermute | solution.py:157
  169.2 7.0 %collective-permute-start.18 = (bf16[16,1024]{1,0:T(8,128)(2,1)S(1)}, bf16[16,1024]{1,0:T(8,128)(2,1)S(1)}, u32[]{:S(2)}, u32[]{:S(2)}) collective-permute-start(bf16[16,1024]{1,0:T(8,128)(2,1)S(1)} %get-tuple-element.92), channel_id=1, source_target_pairs={{0,64},{32,96},{64,0},{96,32},{1,65},{33,97},{65,1},{97,33},{2,66}... | collective-permute-start | bytes 98312 | tf_op jit(solution)/shard_map/ppermute | solution.py:157
  171.4 4.8 %collective-permute-start.19 = (bf16[16,1024]{1,0:T(8,128)(2,1)S(1)}, bf16[16,1024]{1,0:T(8,128)(2,1)S(1)}, u32[]{:S(2)}, u32[]{:S(2)}) collective-permute-start(bf16[16,1024]{1,0:T(8,128)(2,1)S(1)} %get-tuple-element.94), channel_id=1, source_target_pairs={{0,32},{32,64},{64,96},{96,0},{1,33},{33,65},{65,97},{97,1},{2,34}... | collective-permute-start | bytes 98312 | tf_op jit(solution)/shard_map/ppermute | solution.py:157
  171.4 4.8 %collective-permute-start.20 = (bf16[16,1024]{1,0:T(8,128)(2,1)S(1)}, bf16[16,1024]{1,0:T(8,128)(2,1)S(1)}, u32[]{:S(2)}, u32[]{:S(2)}) collective-permute-start(bf16[16,1024]{1,0:T(8,128)(2,1)S(1)} %get-tuple-element.93), channel_id=1, source_target_pairs={{0,96},{32,0},{64,32},{96,64},{1,97},{33,1},{65,33},{97,65},{2,98}... | collective-permute-start | bytes 98312 | tf_op jit(solution)/shard_map/ppermute | solution.py:157
  174.2 6.7 %collective-permute-start.27 = (f32[8,1024]{1,0:T(8,128)S(1)}, f32[8,1024]{1,0:T(8,128)S(1)}, u32[]{:S(2)}, u32[]{:S(2)}) collective-permute-start(f32[8,1024]{1,0:T(8,128)S(1)} %pad_maximum_fusion.3), channel_id=1, source_target_pairs={{0,0},{1,64},{32,32},{33,96},{64,1},{65,65},{96,33},{97,97},{2,2},... | collective-permute-start | bytes 98312 | tf_op jit(solution)/shard_map/ppermute | solution.py:470
  176.2 4.8 %collective-permute-start.26 = (f32[8,1536]{1,0:T(8,128)S(1)}, f32[8,1536]{1,0:T(8,128)S(1)}, u32[]{:S(2)}, u32[]{:S(2)}) collective-permute-start(f32[8,1536]{1,0:T(8,128)S(1)} %get-tuple-element.96), channel_id=1, source_target_pairs={{0,1},{1,0},{2,3},{3,2},{4,5},{5,4},{6,7},{7,6},{8,9},{9,8},{10,11... | collective-permute-start | bytes 147464 | tf_op jit(solution)/shard_map/ppermute | solution.py:475
